TPU v7x, 32 devices: a whole 2x2x4 slice. The times are simulated.
32 devices in a mesh: page: 8 (over z, y), seq: 4 (over x, core).
Axes of the slice: x: 2, y: 2, z: 4, core: 2. Of those that a mesh axis runs over, the one named last changes fastest.
Arguments:
- tokens: bfloat16 [24, 512, 768], P('page', 'seq'), may hold values from -6 to 6
- patches: bfloat16 [24, 64, 768], P('page', 'seq'), may hold values from -6 to 6
- page_length: int32 [24], P('page'), may hold values from 64 to 512, as said below
- box_position: int32 [2, 24, 512], P(None, 'page'), may hold values from 0 to 1023
- query_weight: bfloat16 [768, 768], replicated, may hold values from -0.21875 to 0.21875
- key_weight: bfloat16 [768, 768], replicated, may hold values from -0.21875 to 0.21875
- value_weight: bfloat16 [768, 768], replicated, may hold values from -0.21875 to 0.21875
- out_weight: bfloat16 [768, 768], replicated, may hold values from -0.625 to 0.625
- up_weight: bfloat16 [768, 3072], replicated, may hold values from -0.21875 to 0.21875
- down_weight: bfloat16 [3072, 768], replicated, may hold values from -0.109375 to 0.109375
- conv_weight: bfloat16 [768, 9], replicated, may hold values from -1.796875 to 1.796875
- patch_conv_weight: bfloat16 [768, 9], replicated, may hold values from -1.796875 to 1.796875
- query_bias: bfloat16 [768], replicated, may hold values from -3 to 3
- value_bias: bfloat16 [768], replicated, may hold values from -3 to 3
- out_bias: bfloat16 [768], replicated, may hold values from -3 to 3
- up_bias: bfloat16 [3072], replicated, may hold values from -3 to 3
- down_bias: bfloat16 [768], replicated, may hold values from -3 to 3
- attention_gain: bfloat16 [768], replicated, may hold values from 0.5 to 1.5
- attention_shift: bfloat16 [768], replicated, may hold values from -1.796875 to 1.796875
- feedforward_gain: bfloat16 [768], replicated, may hold values from 0.5 to 1.5
- feedforward_shift: bfloat16 [768], replicated, may hold values from -1.796875 to 1.796875
- reading_bias_table: bfloat16 [12, 32], replicated, may hold values from -4 to 4
- horizontal_bias_table: bfloat16 [12, 64], replicated, may hold values from -4 to 4
- vertical_bias_table: bfloat16 [12, 64], replicated, may hold values from -4 to 4
- cotangent: bfloat16 [24, 512, 768], P('page', 'seq'), may hold values from -6 to 6
- patch_cotangent: bfloat16 [24, 64, 768], P('page', 'seq'), may hold values from -6 to 6
Outputs:
- output: float32 [24, 512, 768], P('page', 'seq')
- patch_output: float32 [24, 64, 768], P('page', 'seq')
- tokens_gradient: float32 [24, 512, 768], P('page', 'seq')
- patches_gradient: float32 [24, 64, 768], P('page', 'seq')
- query_weight_gradient: float32 [768, 768], P('page', 'seq')
- key_weight_gradient: float32 [768, 768], P('page', 'seq')
- value_weight_gradient: float32 [768, 768], P('page', 'seq')
- out_weight_gradient: float32 [768, 768], P('page', 'seq')
- up_weight_gradient: float32 [768, 3072], P('page', 'seq')
- down_weight_gradient: float32 [3072, 768], P('page', 'seq')
- conv_weight_gradient: float32 [768, 9], replicated
- patch_conv_weight_gradient: float32 [768, 9], replicated
- query_bias_gradient: float32 [768], replicated
- value_bias_gradient: float32 [768], replicated
- out_bias_gradient: float32 [768], replicated
- up_bias_gradient: float32 [3072], replicated
- down_bias_gradient: float32 [768], replicated
- attention_gain_gradient: float32 [768], replicated
- attention_shift_gradient: float32 [768], replicated
- feedforward_gain_gradient: float32 [768], replicated
- feedforward_shift_gradient: float32 [768], replicated
- line_table_gradient: float32 [12, 32], replicated
- across_table_gradient: float32 [12, 64], replicated
- upward_table_gradient: float32 [12, 64], replicated
Inputs may be any that keep to these rules, and one draw needn't show every extreme that they name: `page_length`: in every aligned block of 3 pages (the pages of one index of page) at least one page has 512 tokens.
All inputs are finite; a program needn't handle non-finite values.
Results may differ from a plain program's by a relative error of at most 0.019.
The roundings to bfloat16 on the way count: a program that leaves them out, or rounds other values in their place, can miss the bound.
Values may be sent and summed in bfloat16 or wider, within the bound.
A program may use at most 256 MiB of HBM per device.

v0:
```python
import functools

import jax
import jax.numpy as jnp
from jax import lax
from jax.experimental import pallas as pl
from jax.experimental.pallas import tpu as pltpu
from jax.sharding import PartitionSpec as P

GRID_SIDE = 8


epsilon = 1e-05
coordinate_step = 16
masked_score = -1000000000.0
patch_pitch = 146
patch_centre = 73


def with_halo(cells, sides, width):
    for axis, dim in sides:
        count = lax.axis_size(axis)
        ends = count - 1
        head = lax.slice_in_dim(cells, 0, width, axis=dim)
        tail = lax.slice_in_dim(cells, cells.shape[dim] - width, cells.shape[dim], axis=dim)
        cells = jnp.concatenate(
            [
                lax.ppermute(tail, axis, [(i, (i + 1) % count) for i in range(ends)]),
                cells,
                lax.ppermute(head, axis, [((i + 1) % count, i) for i in range(ends)]),
            ],
            axis=dim,
        )
    return cells


def layer_norm(values, gain_vector, shift_vector):
    row_mean = jnp.mean(values, axis=-1, keepdims=True)
    centred = values - row_mean
    variance = jnp.mean(centred * centred, axis=-1, keepdims=True)
    return centred * lax.rsqrt(variance + epsilon) * gain_vector + shift_vector


def gelu_exact(values):
    return jax.nn.gelu(values, approximate=False)


def flat_dot(operand, matrix):
    front = operand.shape[:-1]
    result = jnp.dot(
        operand.reshape(-1, operand.shape[-1]), matrix, preferred_element_type=jnp.float32
    )
    return result.reshape(front + (matrix.shape[-1],))


def back_dot(operand, matrix):
    front = operand.shape[:-1]
    result = lax.dot_general(
        operand.reshape(-1, operand.shape[-1]),
        matrix,
        (((1,), (1,)), ((), ())),
        preferred_element_type=jnp.float32,
    )
    return result.reshape(front + (matrix.shape[0],))


def outer_dot(operand, gradient):
    return lax.dot_general(
        operand.reshape(-1, operand.shape[-1]),
        gradient.reshape(-1, gradient.shape[-1]),
        (((0,), (0,)), ((), ())),
        preferred_element_type=jnp.float32,
    )


def row_sum(gradient):
    return jnp.sum(gradient.astype(jnp.float32).reshape(-1, gradient.shape[-1]), axis=0)


def swap(value, axis, bit):
    count = lax.axis_size(axis)
    return lax.ppermute(value, axis, [(i, i ^ bit) for i in range(count)])


def total_sum(vectors):
    flat = jnp.concatenate([vector.reshape(-1) for vector in vectors])
    flat = jnp.pad(flat, (0, -flat.size % 1024)).reshape(-1, 128)
    for bit in (1, 2):
        flat = flat + swap(flat, "seq", bit)
    bit = 1
    while bit < lax.axis_size("page"):
        flat = flat + swap(flat, "page", bit)
        bit *= 2
    flat = flat.reshape(-1)
    result, start = [], 0
    for vector in vectors:
        result.append(flat[start : start + vector.size].reshape(vector.shape))
        start += vector.size
    return result


def query_places(seq_index, shape, span, patch_span, text_slots):
    row = lax.broadcasted_iota(jnp.int32, shape, 0)
    return jnp.where(
        row < span, seq_index * span + row, text_slots + seq_index * patch_span + row - span
    )


FIXED = 2048.0


def lookup(table_row, lanes):
    return jnp.take_along_axis(jnp.broadcast_to(table_row, lanes.shape), lanes, axis=1)


def pair_masked(pair):
    lane = lax.broadcasted_iota(jnp.int32, pair.shape, 1)
    half = pair.shape[1] // 2
    zero = jnp.zeros_like(pair)
    return jnp.concatenate(
        [jnp.where(lane < half, pair, zero), jnp.where(lane < half, zero, pair)], axis=0
    )


def pair_merged(both):
    rows, width = both.shape[0] // 2, both.shape[1]
    lane = lax.broadcasted_iota(jnp.int32, (rows, width), 1)
    return jnp.where(lane < width // 2, both[:rows], both[rows:])


def dot_nt(left, right):
    return lax.dot_general(left, right, (((1,), (1,)), ((), ())), preferred_element_type=jnp.float32)


def dot_nn(left, right):
    return lax.dot_general(left, right, (((1,), (0,)), ((), ())), preferred_element_type=jnp.float32)


def dot_tn(left, right):
    return lax.dot_general(left, right, (((0,), (0,)), ((), ())), preferred_element_type=jnp.float32)


CHUNK = 16


MESH = pl.DeviceIdType.MESH


def places_of(pages):
    page = lax.axis_index("page")
    seq = lax.axis_index("seq")
    bits = []
    rest = page
    for _ in range(pages.bit_length() - 1):
        bits.append(rest % 2)
        rest = rest // 2
    return page, bits, seq, seq // 2, seq % 2


def sibling_of(seq):
    return seq + 1 - 2 * (seq % 2)


def across_of(seq):
    return seq + 2 - 4 * (seq // 2)


def remote(source, target, send, receive, page, seq):
    return pltpu.make_async_remote_copy(
        src_ref=source, dst_ref=target, send_sem=send, recv_sem=receive, device_id=(page, seq), device_id_type=MESH
    )


def column_of(row):
    square = jnp.broadcast_to(row.astype(jnp.float32), (128, 128)).T
    return square[:, 0:1].astype(jnp.int32)


def forward_kernel(
    pages,
    length_ref, tokens_ref, patches_ref, box_ref, taps_ref, query_weight_ref, key_weight_ref, value_weight_ref,
    vector_ref, table_ref,
    hidden_ref, hidden_low_ref, query_ref, key_ref, value_ref, mixture_ref, weights_ref, columns_ref, rows_ref,
    query_rows_ref,
    arrived, text, grid, low, scores, across_ref, upward_ref, live_ref, line_ref, packed_ref,
    send_sem, recv_sem,
):
    page_at, _, seq, _, _ = places_of(pages)
    count, span, width = tokens_ref.shape
    patch_span = patches_ref.shape[1]
    row_count = span + patch_span
    key_pad = key_ref.shape[1]
    text_slots = 4 * span
    rim = 8
    pairs = weights_ref.shape[1]
    peers = (sibling_of(seq), across_of(seq))
    barrier = pltpu.get_barrier_semaphore()
    for peer in peers:
        pl.semaphore_signal(barrier, inc=1, device_id=(page_at, peer), device_id_type=MESH)
    pl.semaphore_wait(barrier, 2)

    def first_copies(page, side):
        return (
            remote(
                tokens_ref.at[page], arrived.at[side, page, 0:span], send_sem.at[2 * side, page],
                recv_sem.at[2 * side, page], page_at, peers[side],
            ),
            remote(
                patches_ref.at[page], arrived.at[side, page, span:row_count], send_sem.at[2 * side + 1, page],
                recv_sem.at[2 * side + 1, page], page_at, peers[side],
            ),
        )

    def onward_copy(page):
        return remote(
            arrived.at[1, page], arrived.at[2, page], send_sem.at[4, page], recv_sem.at[4, page], page_at, peers[0]
        )

    for page in range(count):
        for side in range(2):
            for copy in first_copies(page, side):
                copy.start()

    steps = jnp.floor(table_ref[...].astype(jnp.float32) * FIXED + 0.5).astype(jnp.int32)
    for pair in range(pairs):
        words = (steps[2 * pair : 2 * pair + 1] + 8192) + steps[2 * pair + 1 : 2 * pair + 2] * 65536
        packed_ref[0, pair : pair + 1, :] = words[:, 0:128]
        packed_ref[1, pair : pair + 1, :] = words[:, 128:256]
    key = lax.broadcasted_iota(jnp.int32, (row_count, key_pad), 1)
    place = query_places(seq, (row_count, key_pad), span, patch_span, text_slots)
    across_ref[...] = jnp.clip(key - place, -16, 15) + 16

    def fill(pair, carry):
        row = packed_ref[1, pl.ds(pair, 1), :]
        for at in range(0, key_pad, 128):
            line_ref[pair, :, at : at + 128] = lookup(row, across_ref[:, at : at + 128])
        return carry

    lax.fori_loop(0, pairs, fill, 0)
    text[0:rim, :] = jnp.zeros((rim, width), jnp.float32)
    text[rim + text_slots :, :] = jnp.zeros((rim, width), jnp.float32)
    grid[0:patch_span, :] = jnp.zeros((patch_span, width), jnp.float32)
    grid[patch_span * 5 :, :] = jnp.zeros((patch_span, width), jnp.float32)
    low[row_count * 4 :, :] = jnp.zeros((key_pad - row_count * 4, width), jnp.bfloat16)
    lanes = 256
    pair_width = 128
    power = 1.4426950408889634 / FIXED
    for copy in first_copies(0, 1):
        copy.wait_recv()
    onward_copy(0).start()

    def page_step(page, carry):
        length = length_ref[page]
        base = page * row_count
        cell = lax.broadcasted_iota(jnp.int32, (1, 128), 1)
        query_cell = seq * patch_span + cell
        row_cell = seq * patch_span + lax.broadcasted_iota(jnp.int32, (patch_span, 1), 0)
        for plane in range(2):
            boxes = box_ref[plane]
            of_page = lax.broadcasted_iota(jnp.int32, boxes.shape, 0) == page
            box = jnp.sum(jnp.where(of_page, boxes, 0), axis=0, keepdims=True)
            patch = 146 * ((cell % GRID_SIDE) if plane == 0 else (cell // GRID_SIDE)) + 73
            own_patch = 146 * ((query_cell % GRID_SIDE) if plane == 0 else (query_cell // GRID_SIDE)) + 73
            column_patch = 146 * ((row_cell % GRID_SIDE) if plane == 0 else (row_cell // GRID_SIDE)) + 73
            rows_ref[page, plane : plane + 1, 0:text_slots] = box
            rows_ref[page, plane : plane + 1, text_slots:key_pad] = patch
            own = rows_ref[page, plane : plane + 1, pl.ds(pl.multiple_of(seq * span, 128), span)]
            query_rows_ref[page, plane : plane + 1, 0:span] = own
            query_rows_ref[page, plane : plane + 1, span:256] = own_patch
            columns_ref[page, 0:span, plane * 128 : (plane + 1) * 128] = jnp.broadcast_to(column_of(own), (span, 128))
            columns_ref[page, span:row_count, plane * 128 : (plane + 1) * 128] = jnp.broadcast_to(
                column_patch, (patch_span, 128)
            )
        for plane, lanes_ref in enumerate((across_ref, upward_ref)):
            difference = rows_ref[page, plane : plane + 1, :] - columns_ref[page, :, plane * 128 : plane * 128 + 1]
            lanes_ref[...] = jnp.clip(difference >> 4, -32, 31) + (32 + 64 * plane)
        key_at = lax.broadcasted_iota(jnp.int32, live_ref.shape, 1)
        key_cell = key_at - text_slots
        live = (key_at < length) | (
            (key_cell >= 0) & ((key_cell >> 3) < GRID_SIDE - 1) & ((key_cell & 7) < GRID_SIDE - 1)
        )
        live_ref[...] = jnp.where(live, 0.0, masked_score * FIXED)
        for copy in first_copies(page, 0):
            copy.wait_recv()
        onward_copy(page).wait_recv()

        def block_of(step, start, stop, at):
            if step:
                return arrived[step - 1, page, start:stop, at].astype(jnp.float32)
            if start:
                return patches_ref[page, :, at].astype(jnp.float32)
            return tokens_ref[page, :, at].astype(jnp.float32)

        def slot_of(step):
            return (seq, peers[0], peers[1], sibling_of(peers[1]))[step]

        everything = slice(0, width)
        for step in range(4):
            where = slot_of(step)
            at_place = where * span + lax.broadcasted_iota(jnp.int32, (span, 1), 0)
            text[pl.ds(pl.multiple_of(rim + where * span, 8), span), :] = jnp.where(
                at_place < length, block_of(step, 0, span, everything), 0.0
            )
            at_cell = where * patch_span + lax.broadcasted_iota(jnp.int32, (patch_span, 1), 0)
            cell_live = ((at_cell >> 3) < GRID_SIDE - 1) & ((at_cell & 7) < GRID_SIDE - 1)
            grid[pl.ds(pl.multiple_of(patch_span + where * patch_span, 8), patch_span), :] = jnp.where(
                cell_live, block_of(step, span, row_count, everything), 0.0
            )
        for step in range(4):
            where = slot_of(step)

            def convolve(tile, carry):
                at = pl.ds(pl.multiple_of(tile * lanes, lanes), lanes)
                window = text[pl.ds(pl.multiple_of(where * span, 8), span + 2 * rim), at]
                centre = taps_ref[1:2, at] + taps_ref[4:5, at] + taps_ref[7:8, at]
                total = block_of(step, 0, span, at) + window[rim : rim + span] * centre
                for dilation in (1, 2, 3):
                    for offset in (-1, 1):
                        tap = 3 * (dilation - 1) + offset + 1
                        anchor = rim + offset * dilation
                        total = total + window[anchor : anchor + span] * taps_ref[tap : tap + 1, at]
                low[pl.ds(pl.multiple_of(where * span, 16), span), at] = total.astype(jnp.bfloat16)
                window = grid[pl.ds(pl.multiple_of(where * patch_span, 8), 3 * patch_span), at]
                patch_total = block_of(step, span, row_count, at)
                for vertical in (-1, 0, 1):
                    for horizontal in (-1, 0, 1):
                        tap = 9 + 3 * (vertical + 1) + horizontal + 1
                        anchor = patch_span + vertical * GRID_SIDE + horizontal
                        patch_total = patch_total + window[anchor : anchor + patch_span] * taps_ref[tap : tap + 1, at]
                low[pl.ds(pl.multiple_of(text_slots + where * patch_span, 16), patch_span), at] = (
                    patch_total.astype(jnp.bfloat16)
                )
                if step == 0:
                    for first, rows_here, value in ((0, span, total), (span, patch_span, patch_total)):
                        here = pl.ds(pl.multiple_of(base + first, 16), rows_here)
                        hidden_ref[here, at] = value
                        hidden_low_ref[here, at] = value.astype(jnp.bfloat16)
                return carry

            lax.fori_loop(0, width // lanes, convolve, 0)
        own_rows = pl.ds(pl.multiple_of(base, 16), row_count)

        def project(tile, carry):
            at = pl.ds(pl.multiple_of(tile * lanes, lanes), lanes)
            key_ref[page, :, at] = dot_nn(low[...], key_weight_ref[:, at]).astype(jnp.bfloat16)
            value_ref[page, :, at] = (dot_nn(low[...], value_weight_ref[:, at]) + vector_ref[1:2, at]).astype(
                jnp.bfloat16
            )
            query_ref[own_rows, at] = (
                (dot_nn(hidden_low_ref[own_rows, :], query_weight_ref[:, at]) + vector_ref[0:1, at])
                .astype(jnp.bfloat16)
                * jnp.bfloat16(0.125)
            )
            return carry

        lax.fori_loop(0, width // lanes, project, 0)

        @pl.when(page < count - 1)
        def _():
            for copy in first_copies(page + 1, 1):
                copy.wait_recv()
            onward_copy(page + 1).start()

        def attend(pair, carry):
            at = pl.ds(pl.multiple_of(pair * pair_width, pair_width), pair_width)
            scores[...] = dot_nt(pair_masked(query_ref[own_rows, at] * jnp.bfloat16(FIXED)), key_ref[page, :, at])
            plane_row = packed_ref[0, pl.ds(pair, 1), :]
            for start in range(0, row_count, CHUNK):
                here = slice(start, start + CHUNK)
                packed = []
                for block_at in range(0, key_pad, 128):
                    lane = slice(block_at, block_at + 128)
                    packed.append(
                        line_ref[pair, here, lane]
                        + lookup(plane_row, across_ref[here, lane])
                        + lookup(plane_row, upward_ref[here, lane])
                    )
                for side in range(2):
                    there = slice(side * row_count + start, side * row_count + start + CHUNK)
                    parts, top = [], None
                    for index, word in enumerate(packed):
                        lane = slice(128 * index, 128 * (index + 1))
                        field = (word >> 16) if side else (word & 0xFFFF)
                        part = (scores[there, lane] + field.astype(jnp.float32)) + live_ref[0:1, lane]
                        top = part if top is None else jnp.maximum(top, part)
                        parts.append(part)
                    top = jnp.max(top, axis=1, keepdims=True)
                    parts = [jnp.exp2((part - top) * power) for part in parts]
                    total = parts[0]
                    for part in parts[1:]:
                        total = total + part
                    inverse = 1.0 / jnp.sum(total, axis=1, keepdims=True)
                    for index, part in enumerate(parts):
                        weights_ref[page, pair, there, 128 * index : 128 * (index + 1)] = (part * inverse).astype(
                            jnp.bfloat16
                        )
            mixture_ref[own_rows, at] = pair_merged(
                dot_nn(weights_ref[page, pair], value_ref[page, :, at])
            ).astype(jnp.bfloat16)
            return carry

        lax.fori_loop(0, pairs, attend, 0)
        return carry

    lax.fori_loop(0, count, page_step, 0)
    for page in range(count):
        for side in range(2):
            for copy in first_copies(page, side):
                copy.wait_send()
        onward_copy(page).wait_send()


VMEM = pltpu.VMEM
KERNEL_VMEM = 48 * 1024 * 1024


def in_vmem(count):
    return [pl.BlockSpec(memory_space=VMEM)] * count


def forward(pages, lengths, tokens, patches, box, taps, matrices, vectors, table):
    count, span, width = tokens.shape
    patch_span = patches.shape[1]
    row_count = span + patch_span
    total_rows = count * row_count
    key_pad = -(-4 * row_count // 128) * 128
    pairs = table.shape[0] // 2
    bf16, f32, i32 = jnp.bfloat16, jnp.float32, jnp.int32
    own = jax.ShapeDtypeStruct((total_rows, width), bf16)
    every = jax.ShapeDtypeStruct((count, key_pad, width), bf16)
    return pl.pallas_call(
        functools.partial(forward_kernel, pages),
        out_shape=(
            jax.ShapeDtypeStruct((total_rows, width), f32), own, own, every, every, own,
            jax.ShapeDtypeStruct((count, pairs, 2 * row_count, key_pad), bf16),
            jax.ShapeDtypeStruct((count, row_count, 256), i32),
            jax.ShapeDtypeStruct((count, 8, key_pad), i32),
            jax.ShapeDtypeStruct((count, 8, 256), i32),
        ),
        in_specs=[pl.BlockSpec(memory_space=pltpu.SMEM)] + in_vmem(9),
        out_specs=tuple(in_vmem(10)),
        scratch_shapes=[
            VMEM((3, count, row_count, width), bf16),
            VMEM((4 * span + 16, width), f32),
            VMEM((6 * patch_span, width), f32),
            VMEM((key_pad, width), bf16),
            VMEM((2 * row_count, key_pad), f32),
            VMEM((row_count, key_pad), i32),
            VMEM((row_count, key_pad), i32),
            VMEM((8, key_pad), f32),
            VMEM((pairs, row_count, key_pad), i32),
            VMEM((2, 8, 128), i32),
            pltpu.SemaphoreType.DMA((5, count)),
            pltpu.SemaphoreType.DMA((5, count)),
        ],
        compiler_params=pltpu.CompilerParams(
            collective_id=0, has_side_effects=True, vmem_limit_bytes=KERNEL_VMEM
        ),
        cost_estimate=pl.CostEstimate(flops=8_000_000_000, bytes_accessed=25_000_000, transcendentals=3_000_000),
        name="forward",
    )(lengths, tokens, patches, box, taps, *matrices, vectors, table)


def backward_kernel(
    scalar_ref, columns_ref, rows_ref, query_rows_ref, query_ref, key_ref, value_ref, mixture_back_ref, weights_ref,
    query_back_ref, block_back_ref, plane_back_ref, line_back_ref,
    back, steps, mask_ref, hot_ref, query_hot_ref, band_ref,
):
    seq_index = scalar_ref[0]
    row_count, width = query_ref.shape
    key_pad = key_ref.shape[0]
    count = 4
    patch_span = GRID_SIDE * GRID_SIDE // count
    span = row_count - patch_span
    text_slots = span * count
    columns, rows = columns_ref[...], rows_ref[...]
    mask_ref[:, 0:key_pad] = ((rows[0:1, :] & 15) < (columns[:, 0:1] & 15)).astype(jnp.float32).astype(jnp.bfloat16)
    mask_ref[:, key_pad:] = ((rows[1:2, :] & 15) < (columns[:, 1:2] & 15)).astype(jnp.float32).astype(jnp.bfloat16)
    bin_at = lax.broadcasted_iota(jnp.int32, (128, key_pad), 0) - 1
    key_block = lax.broadcasted_iota(jnp.int32, (128, key_pad), 1) >> 4
    for side in range(2):
        key_bin = rows[side : side + 1, :] >> 4
        plain = (key_bin == bin_at).astype(jnp.float32)
        lower = (key_bin - 1 == bin_at).astype(jnp.float32)
        plain, lower = jnp.where(bin_at < 64, plain, 0.0), jnp.where(bin_at < 64, lower, 0.0)
        mine = slice(128 * side, 128 * (side + 1))
        other = slice(128 * (1 - side), 128 * (2 - side))
        change = lower - plain
        if side == 0:
            plain = jnp.where(bin_at - 71 == key_block, 1.0, plain)
        hot_ref[mine, 0:key_pad] = plain.astype(jnp.bfloat16)
        hot_ref[mine, (1 + side) * key_pad : (2 + side) * key_pad] = change.astype(jnp.bfloat16)
        hot_ref[other, (1 + side) * key_pad : (2 + side) * key_pad] = jnp.zeros((128, key_pad), jnp.bfloat16)
    half_bin = lax.broadcasted_iota(jnp.int32, (72, row_count), 0)
    for side in range(2):
        query_hot_ref[72 * side : 72 * (side + 1), :] = (
            (71 - (query_rows_ref[side : side + 1, :] >> 4) == half_bin).astype(jnp.float32).astype(jnp.bfloat16)
        )
    lane128 = lax.broadcasted_iota(jnp.int32, (row_count, 128), 1)
    place = query_places(seq_index, (row_count, 128), span, patch_span, text_slots)
    aim = place + lane128 - 32
    near = (lane128 < 64) & (aim >= 0) & (aim < text_slots + patch_span * count)
    apart = (aim >> 4) - (place >> 4)
    near = near & (apart >= -1) & (apart <= 1)
    band_ref[...] = jnp.where(near, aim, -1)
    pair_width = 128
    line_back_ref[...] = jnp.zeros_like(line_back_ref)
    plane_back_ref[...] = jnp.zeros_like(plane_back_ref)

    def attend(pair, carry):
        at = pl.ds(pl.multiple_of(pair * pair_width, pair_width), pair_width)
        both_query = pair_masked(query_ref[:, at])
        both_back = pair_masked(mixture_back_ref[:, at])
        back[...] = dot_nt(both_back, value_ref[:, at])
        for start in range(0, 2 * row_count, CHUNK):
            there = slice(start, start + CHUNK)
            here = slice(start % row_count, start % row_count + CHUNK)
            parts, total = [], None
            for block_at in range(0, key_pad, 128):
                lane = slice(block_at, block_at + 128)
                part = weights_ref[pair, there, lane].astype(jnp.float32)
                product = part * back[there, lane]
                total = product if total is None else total + product
                parts.append(part)
            mean = jnp.sum(total, axis=1, keepdims=True)
            for index, part in enumerate(parts):
                lane = slice(128 * index, 128 * (index + 1))
                step = (part * (back[there, lane] - mean)).astype(jnp.bfloat16)
                steps[there, lane] = step
                steps[there, key_pad + 128 * index : key_pad + 128 * (index + 1)] = step * mask_ref[here, lane]
                steps[there, 2 * key_pad + 128 * index : 2 * key_pad + 128 * (index + 1)] = (
                    step * mask_ref[here, key_pad + 128 * index : key_pad + 128 * (index + 1)]
                )
        query_back_ref[:, at] = (pair_merged(dot_nn(steps[:, 0:key_pad], key_ref[:, at])) * 0.125).astype(
            jnp.bfloat16
        )
        for kind, value in enumerate(
            (dot_tn(steps[:, 0:key_pad], both_query), dot_tn(weights_ref[pair], both_back))
        ):
            value = value.astype(jnp.bfloat16)
            for where in range(count):
                step_at = seq_index ^ where
                slot = (step_at & 1) * 2 + (step_at >> 1)
                block_back_ref[slot, kind, 0:span, at] = value[where * span : (where + 1) * span]
                block_back_ref[slot, kind, span:row_count, at] = value[
                    text_slots + where * patch_span : text_slots + (where + 1) * patch_span
                ]
        bins = dot_nt(steps[...], hot_ref[...])
        low_bins = bins.astype(jnp.bfloat16)
        lane_one = lax.broadcasted_iota(jnp.int32, (1, 128), 1)
        far = lane128 - 72 - (place >> 4)
        in_line = (lane128 >= 72) & (lane128 < 72 + key_pad // 16)
        for side in range(2):
            head = pl.ds(2 * pair + side, 1)
            own = slice(side * row_count, (side + 1) * row_count)
            both = dot_nn(query_hot_ref[...], low_bins[own])
            for plane in range(2):
                table = both[72 * plane : 72 * (plane + 1), 128 * plane : 128 * (plane + 1)]
                wide_lane = lax.broadcasted_iota(jnp.int32, table.shape, 1)
                table = jnp.where(wide_lane < 72, table, 0.0)
                table = jnp.concatenate([table, jnp.zeros_like(table)], axis=1)
                sheared = pltpu.roll(table, 0, 1, stride=1, stride_axis=0)
                plane_back_ref[plane, head, :] = jnp.sum(sheared, axis=0, keepdims=True)
            line_bins = bins[own, 0:128]
            low_tail = jnp.sum(jnp.where(in_line & (far <= -2), line_bins, 0.0), axis=(0, 1), keepdims=True)
            high_tail = jnp.sum(jnp.where(in_line & (far >= 2), line_bins, 0.0), axis=(0, 1), keepdims=True)
            band = jnp.zeros((1, 128), jnp.float32)
            base = side * row_count
            for first, rows_here, block in (
                (0, span, seq_index),
                (0, 32, jnp.maximum(seq_index - 1, 0)),
                (span - 32, 32, seq_index + 1),
                (span, patch_span, count - 1),
                (span, patch_span, count),
            ):
                aims = band_ref[first : first + rows_here, :]
                source = steps[
                    base + first : base + first + rows_here, pl.ds(pl.multiple_of(block * 128, 128), 128)
                ].astype(jnp.float32)
                taken = jnp.take_along_axis(source, aims & 127, axis=1)
                right = (aims >> 7) == block
                if first == 0 and rows_here == 32:
                    right = right & (seq_index > 0)
                band = band + jnp.sum(jnp.where(right, taken, 0.0), axis=0, keepdims=True)
            line_back_ref[head, :] = (
                band + jnp.where(lane_one == 0, low_tail, 0.0) + jnp.where(lane_one == 63, high_tail, 0.0)
            )
        return carry

    lax.fori_loop(0, width // pair_width, attend, 0)


def backward_page(scalars, columns, rows, query_rows, queries, keys, values, mixture_back, weights):
    row_count, width = queries.shape
    key_pad = keys.shape[0]
    heads = 2 * weights.shape[0]
    return pl.pallas_call(
        backward_kernel,
        out_shape=(
            jax.ShapeDtypeStruct((row_count, width), jnp.bfloat16),
            jax.ShapeDtypeStruct((4, 2, row_count, width), jnp.bfloat16),
            jax.ShapeDtypeStruct((2, heads, 256), jnp.float32),
            jax.ShapeDtypeStruct((heads, 128), jnp.float32),
        ),
        in_specs=[pl.BlockSpec(memory_space=pltpu.SMEM)] + in_vmem(8),
        out_specs=tuple(in_vmem(4)),
        scratch_shapes=[
            pltpu.VMEM((2 * row_count, key_pad), jnp.float32),
            pltpu.VMEM((2 * row_count, 3 * key_pad), jnp.bfloat16),
            pltpu.VMEM((row_count, 2 * key_pad), jnp.bfloat16),
            pltpu.VMEM((256, 3 * key_pad), jnp.bfloat16),
            pltpu.VMEM((144, row_count), jnp.bfloat16),
            pltpu.VMEM((row_count, 128), jnp.int32),
        ],
        compiler_params=pltpu.CompilerParams(vmem_limit_bytes=KERNEL_VMEM),
        cost_estimate=pl.CostEstimate(flops=3_000_000_000, bytes_accessed=6_000_000, transcendentals=1_000_000),
        name="backward_page",
    )(scalars, columns, rows, query_rows, queries, keys, values, mixture_back, weights)


def block_slots(scalar_ref, page, column, levels):
    far = page ^ scalar_ref[2]
    side = column ^ scalar_ref[3]
    rest = 0
    for level in range(1, levels):
        rest = rest + (((far >> level) & 1) << (levels - 1 - level))
    near = far & 1
    return (side << levels) + (near << (levels - 1)) + rest, (near << levels) + (side << (levels - 1)) + rest


NORM_CHUNK = 48


def norm_rows(values):
    mean = jnp.mean(values, axis=-1, keepdims=True)
    centred = values - mean
    scale = lax.rsqrt(jnp.mean(centred * centred, axis=-1, keepdims=True) + epsilon)
    return centred * scale, scale


def norm_back(delta, unit, scale):
    return scale * (
        delta
        - jnp.mean(delta, axis=-1, keepdims=True)
        - unit * jnp.mean(delta * unit, axis=-1, keepdims=True)
    )


def column_sum(values):
    return jnp.sum(values, axis=0, keepdims=True)


OUT_BIAS, DOWN_BIAS, FIRST_GAIN, FIRST_SHIFT, SECOND_GAIN, SECOND_SHIFT = range(6)
UP_BIAS = 6


def middle_kernel(
    pages, direct,
    scalar_ref, hidden_ref, mixture_ref, cotangent_ref, patch_cotangent_ref, out_weight_ref, up_weight_ref,
    down_weight_ref, vector_ref,
    output_ref, patch_output_ref, first_back_ref, mixture_back_ref, sums_ref, *rest,
):
    if direct:
        bundle_ref, *rest = rest
    else:
        normed_out_ref, up_out_ref, activated_out_ref, down_out_ref, attention_out_ref, *rest = rest
    state, unit, scale_ref, normed, activated, slope, up_back, down_back, attention_back, flipped = rest
    count, span, width = output_ref.shape
    patch_span = patch_output_ref.shape[1]
    row_count = span + patch_span
    total_rows = count * row_count
    wide = up_weight_ref.shape[1]
    lanes = 256
    sums_ref[...] = jnp.zeros_like(sums_ref)

    def tile_at(tile):
        return pl.ds(pl.multiple_of(tile * lanes, lanes), lanes)

    def attention_tile(tile, carry):
        at = tile_at(tile)
        state[:, at] = hidden_ref[:, at] + (dot_nn(mixture_ref[...], out_weight_ref[:, at]) + vector_ref[2:3, at])
        return carry

    lax.fori_loop(0, width // lanes, attention_tile, 0)

    def first_norm(chunk, carry):
        here = pl.ds(pl.multiple_of(chunk * NORM_CHUNK, 16), NORM_CHUNK)
        rows, scale = norm_rows(state[here, :])
        unit[here, :] = rows
        scale_ref[here, :] = jnp.broadcast_to(scale, (NORM_CHUNK, 128))
        rows = rows * vector_ref[4:5, :] + vector_ref[5:6, :]
        state[here, :] = rows
        normed[here, :] = rows.astype(jnp.bfloat16)
        return carry

    lax.fori_loop(0, total_rows // NORM_CHUNK, first_norm, 0)

    def up_tile(tile, carry):
        at = tile_at(tile)
        branch = dot_nn(normed[...], up_weight_ref[:, at]) + vector_ref[pl.ds(8 + tile // 3, 1), tile_at(tile % 3)]
        chance = 0.5 * (1.0 + lax.erf(branch * 0.7071067811865476))
        activated[:, at] = (branch * chance).astype(jnp.bfloat16)
        slope[:, at] = chance + branch * (jnp.exp(branch * branch * -0.5) * 0.3989422804014327)
        return carry

    lax.fori_loop(0, wide // lanes, up_tile, 0)

    def down_tile(tile, carry):
        at = tile_at(tile)
        state[:, at] = state[:, at] + (dot_nn(activated[...], down_weight_ref[:, at]) + vector_ref[3:4, at])
        return carry

    lax.fori_loop(0, width // lanes, down_tile, 0)

    def second_norm(start, rows_here, page, out_ref, delta_ref):
        here = pl.ds(pl.multiple_of(page * row_count + start, 16), rows_here)
        there = pl.ds(0 if start == span else start, rows_here)
        rows, scale = norm_rows(state[here, :])
        out_ref[page, there, :] = rows * vector_ref[6:7, :] + vector_ref[7:8, :]
        delta = delta_ref[page, there, :].astype(jnp.float32)
        back = norm_back(delta * vector_ref[6:7, :], rows, scale)
        state[here, :] = back
        low = back.astype(jnp.bfloat16)
        down_back[here, :] = low
        for index, value in (
            (SECOND_GAIN, delta * rows), (SECOND_SHIFT, delta), (DOWN_BIAS, low.astype(jnp.float32))
        ):
            sums_ref[index : index + 1, :] += column_sum(value)

    def second_page(page, carry):
        for start in range(0, span, 32):
            second_norm(start, 32, page, output_ref, cotangent_ref)
        second_norm(span, patch_span, page, patch_output_ref, patch_cotangent_ref)
        return carry

    lax.fori_loop(0, count, second_page, 0)

    def up_back_tile(tile, carry):
        at = tile_at(tile)
        low = (dot_nt(down_back[...], down_weight_ref[at, :]) * slope[:, at]).astype(jnp.bfloat16)
        up_back[:, at] = low
        sums_ref[pl.ds(UP_BIAS + tile // 3, 1), tile_at(tile % 3)] = column_sum(low.astype(jnp.float32))
        return carry

    lax.fori_loop(0, wide // lanes, up_back_tile, 0)

    def normed_back_tile(tile, carry):
        at = tile_at(tile)
        state[:, at] = state[:, at] + dot_nt(up_back[...], up_weight_ref[at, :])
        return carry

    lax.fori_loop(0, width // lanes, normed_back_tile, 0)

    def first_back(chunk, carry):
        here = pl.ds(pl.multiple_of(chunk * NORM_CHUNK, 16), NORM_CHUNK)
        delta, rows = state[here, :], unit[here, :]
        back = norm_back(delta * vector_ref[4:5, :], rows, scale_ref[here, 0:1])
        first_back_ref[here, :] = back
        low = back.astype(jnp.bfloat16)
        attention_back[here, :] = low
        for index, value in (
            (FIRST_GAIN, delta * rows), (FIRST_SHIFT, delta), (OUT_BIAS, low.astype(jnp.float32))
        ):
            sums_ref[index : index + 1, :] += column_sum(value)
        return carry

    lax.fori_loop(0, total_rows // NORM_CHUNK, first_back, 0)

    def mixture_tile(tile, carry):
        at = tile_at(tile)
        mixture_back_ref[:, at] = dot_nt(attention_back[...], out_weight_ref[at, :]).astype(jnp.bfloat16)
        return carry

    lax.fori_loop(0, width // lanes, mixture_tile, 0)
    if not direct:
        normed_out_ref[...] = normed[...]
        up_out_ref[...] = up_back[...]
        activated_out_ref[...] = activated[...]
        down_out_ref[...] = down_back[...]
        attention_out_ref[...] = attention_back[...]
        return
    levels = pages.bit_length() - 1
    core = scalar_ref[1]
    rows = width // pages
    tall = wide // pages
    block = 384
    groups = wide // (2 * block)
    flipped[...] = normed[...].T

    def up_weight_tile(tile, carry):
        column, group = tile // groups, tile % groups
        at = pl.ds(pl.multiple_of(tile * block, block), block)
        result = dot_nn(flipped[...], up_back[:, at]).astype(jnp.bfloat16)
        for page in range(pages):
            slot = block_slots(scalar_ref, page, column, levels)[0]
            bundle_ref[core, slot, pl.ds(pl.multiple_of(group * rows, 16), rows), :] = result[
                page * rows : (page + 1) * rows
            ]
        return carry

    lax.fori_loop(0, 2 * groups, up_weight_tile, 0)

    def down_weight_tile(page, carry):
        at = pl.ds(pl.multiple_of(page * tall, 128), tall)
        result = dot_tn(activated[:, at], down_back[...]).astype(jnp.bfloat16)
        for column in range(2):
            slot = block_slots(scalar_ref, page, column, levels)[1]
            bundle_ref[1 - core, slot, 0:tall, :] = result[:, column * block : (column + 1) * block]
        return carry

    lax.fori_loop(0, pages, down_weight_tile, 0)
    flipped[...] = mixture_ref[...].T
    half = rows // 2

    def out_weight_tile(column, carry):
        at = pl.ds(pl.multiple_of(column * block, block), block)
        result = dot_nn(flipped[...], attention_back[:, at]).astype(jnp.bfloat16)
        for page in range(pages):
            slots = block_slots(scalar_ref, page, column, levels)
            for order in range(2):
                first = page * rows + order * half
                bundle_ref[core if order == 0 else 1 - core, slots[order], tall : tall + half, :] = result[
                    first : first + half
                ]
        return carry

    lax.fori_loop(0, 2, out_weight_tile, 0)


def middle(places, hidden, mixture, cotangent, patch_cotangent, matrices, vectors, pages):
    count, span, width = cotangent.shape
    patch_span = patch_cotangent.shape[1]
    total_rows = hidden.shape[0]
    wide = matrices[1].shape[1]
    direct = (width // pages) % 32 == 0
    bf16, f32 = jnp.bfloat16, jnp.float32
    if direct:
        extra = (jax.ShapeDtypeStruct((2, 2 * pages, (wide + width // 2) // pages, 384), bf16),)
    else:
        extra = tuple(
            jax.ShapeDtypeStruct((total_rows, size), bf16) for size in (width, wide, wide, width, width)
        )
    result = pl.pallas_call(
        functools.partial(middle_kernel, pages, direct),
        out_shape=(
            jax.ShapeDtypeStruct(cotangent.shape, f32),
            jax.ShapeDtypeStruct(patch_cotangent.shape, f32),
            jax.ShapeDtypeStruct((total_rows, width), f32),
            jax.ShapeDtypeStruct((total_rows, width), bf16),
            jax.ShapeDtypeStruct((16, width), f32),
        )
        + extra,
        in_specs=[pl.BlockSpec(memory_space=pltpu.SMEM)] + in_vmem(8),
        out_specs=tuple(in_vmem(5 + len(extra))),
        scratch_shapes=[
            pltpu.VMEM((total_rows, width), f32),
            pltpu.VMEM((total_rows, width), f32),
            pltpu.VMEM((total_rows, 128), f32),
            pltpu.VMEM((total_rows, width), bf16),
            pltpu.VMEM((total_rows, wide), bf16),
            pltpu.VMEM((total_rows, wide), f32),
            pltpu.VMEM((total_rows, wide), bf16),
            pltpu.VMEM((total_rows, width), bf16),
            pltpu.VMEM((total_rows, width), bf16),
            pltpu.VMEM((width, total_rows), bf16),
        ],
        compiler_params=pltpu.CompilerParams(vmem_limit_bytes=56 * 1024 * 1024),
        cost_estimate=pl.CostEstimate(flops=14_000_000_000, bytes_accessed=30_000_000, transcendentals=2_600_000),
        name="middle",
    )(places, hidden, mixture, cotangent, patch_cotangent, *matrices, vectors)
    first, rest = result[:5], result[5:]
    if direct:
        return first + rest
    normed, up_back, activated, down_back, attention_back = rest
    return first + (
        indexed_bundle(
            (
                ((normed, up_back, None), (mixture, attention_back, 0)),
                ((activated, down_back, None), (mixture, attention_back, 1)),
            ),
            places,
            pages,
        ),
    )


def indexed_bundle(matrices, scalars, pages):
    levels = pages.bit_length() - 1
    place = jnp.arange(2 * pages, dtype=jnp.int32)
    bits = [(place >> (levels - k)) & 1 for k in range(levels + 1)]
    halves = []
    for order, group in enumerate(matrices):
        side, near = (bits[0], bits[1]) if order == 0 else (bits[1], bits[0])
        far = near
        for level in range(1, levels):
            far = far + (bits[level + 1] << level)
        index = (far ^ scalars[2]) * 2 + (side ^ scalars[3])
        blocks = []
        for operand, gradient, part in group:
            rows = in_blocks(outer_dot(operand, gradient).astype(jnp.bfloat16), pages)
            if part is not None:
                half = rows.shape[1] // 2
                rows = rows[:, part * half : (part + 1) * half]
            blocks.append(rows)
        halves.append(jnp.concatenate(blocks, axis=1)[index])
    first, second = halves
    mine = scalars[1] == 0
    return jnp.stack([jnp.where(mine, first, second), jnp.where(mine, second, first)])


def attention_weight_kernel(
    pages, scalar_ref, hidden_ref, query_back_ref, key_back_ref, value_back_ref, out_ref, flipped
):
    levels = pages.bit_length() - 1
    core = scalar_ref[1]
    rows = hidden_ref.shape[1] // pages
    half = rows // 2
    lanes = out_ref.shape[3]
    flipped[...] = hidden_ref[...].T

    def tile(column, carry):
        at = pl.ds(pl.multiple_of(column * lanes, lanes), lanes)
        for index, back_ref in enumerate((query_back_ref, key_back_ref, value_back_ref)):
            result = dot_nn(flipped[...], back_ref[:, at]).astype(jnp.bfloat16)
            for page in range(pages):
                slots = block_slots(scalar_ref, page, column, levels)
                first = page * rows
                if index < 2:
                    where = core if index == 0 else 1 - core
                    out_ref[where, slots[index], 0:rows, :] = result[first : first + rows]
                else:
                    out_ref[core, slots[0], rows : rows + half, :] = result[first : first + half]
                    out_ref[1 - core, slots[1], rows : rows + half, :] = result[first + half : first + rows]
        return carry

    lax.fori_loop(0, 2, tile, 0)


def in_blocks(matrix, pages):
    rows, columns = matrix.shape[0] // pages, matrix.shape[1] // 2
    lanes = min(columns, 384)
    blocks = matrix.reshape(pages, rows, 2, columns // lanes, lanes)
    return blocks.transpose(0, 2, 3, 1, 4).reshape(pages * 2, rows * columns // lanes, lanes)


def attention_bundle(places, operands, pages):
    hidden, query_back, key_back, value_back = operands
    width = hidden.shape[1]
    if (width // pages) % 32:
        return indexed_bundle(
            (
                ((hidden, query_back, None), (hidden, value_back, 0)),
                ((hidden, key_back, None), (hidden, value_back, 1)),
            ),
            places,
            pages,
        )
    return pl.pallas_call(
        functools.partial(attention_weight_kernel, pages),
        out_shape=jax.ShapeDtypeStruct((2, 2 * pages, 3 * width // (2 * pages), 384), jnp.bfloat16),
        in_specs=[pl.BlockSpec(memory_space=pltpu.SMEM)] + in_vmem(4),
        out_specs=in_vmem(1)[0],
        scratch_shapes=[pltpu.VMEM(hidden.shape[::-1], jnp.bfloat16)],
        compiler_params=pltpu.CompilerParams(vmem_limit_bytes=KERNEL_VMEM),
        cost_estimate=pl.CostEstimate(flops=1_600_000_000, bytes_accessed=10_000_000, transcendentals=0),
        name="attention_weights",
    )(places, *operands)


def exchange(value, pages, step):
    moves = []
    for page in range(pages):
        for seq in range(4):
            on_page, on_seq = page, seq
            if (seq % 2 == step) if step < 2 else False:
                on_seq = seq ^ 2
            else:
                on_page = page ^ (1 if step < 2 else 1 << (step - 1))
            moves.append((page * 4 + seq, on_page * 4 + on_seq))
    return lax.ppermute(value, ("page", "seq"), moves)


def added(kept, got):
    return (kept.astype(jnp.float32) + got.astype(jnp.float32)).astype(jnp.bfloat16)


def bundle_sum(state, pages):
    for step in range(pages.bit_length()):
        half = state.shape[0] // 2
        state = added(state[:half], exchange(state[half:], pages, step))
    return state[0]


def bundle_parts(state, wide_rows, core):
    lanes = state.shape[1] // 2
    first = core == 0
    tail = state[wide_rows:]
    if wide_rows > 2 * tail.shape[0]:
        group = state[:wide_rows].reshape(4, wide_rows // 4, 2 * lanes)
        low = group[:2].transpose(1, 0, 2).reshape(-1, lanes)
        high = group[2:].transpose(1, 0, 2).reshape(-1, lanes)
    else:
        low, high = state[:wide_rows, :lanes], state[:wide_rows, lanes:]
    left, right = state[:wide_rows, :lanes], state[:wide_rows, lanes:]
    sent = jnp.concatenate(
        [jnp.where(first, high, left), jnp.where(first, tail[:, lanes:], tail[:, :lanes])], axis=0
    )
    got = swap(sent, "seq", 1)
    kept_tail = jnp.where(first, tail[:, :lanes], tail[:, lanes:])
    one = jnp.where(first, low, got[:wide_rows])
    two = jnp.where(first, got[:wide_rows], right)
    three = jnp.concatenate(
        [jnp.where(first, kept_tail, got[wide_rows:]), jnp.where(first, got[wide_rows:], kept_tail)], axis=0
    )
    return [value.astype(jnp.float32) for value in (one, two, three)]


def grid_live(cells):
    return (cells // GRID_SIDE < GRID_SIDE - 1) & (cells % GRID_SIDE < GRID_SIDE - 1)


def grid_boxes(cells):
    return jnp.stack(
        [
            patch_pitch * (cells % GRID_SIDE) + patch_centre,
            patch_pitch * (cells // GRID_SIDE) + patch_centre,
        ]
    )


def shards(
    tokens,
    patches,
    page_length,
    box_position,
    query_weight,
    key_weight,
    value_weight,
    out_weight,
    up_weight,
    down_weight,
    conv_weight,
    patch_conv_weight,
    query_bias,
    value_bias,
    out_bias,
    up_bias,
    down_bias,
    attention_gain,
    attention_shift,
    feedforward_gain,
    feedforward_shift,
    reading_bias_table,
    horizontal_bias_table,
    vertical_bias_table,
    cotangent,
    patch_cotangent,
):
    conv_taps = conv_weight.astype(jnp.float32)
    patch_taps = patch_conv_weight.astype(jnp.float32)
    query_offset = query_bias.astype(jnp.float32)
    value_offset = value_bias.astype(jnp.float32)
    out_offset = out_bias.astype(jnp.float32)
    up_offset = up_bias.astype(jnp.float32)
    down_offset = down_bias.astype(jnp.float32)
    first_gain = attention_gain.astype(jnp.float32)
    first_shift = attention_shift.astype(jnp.float32)
    second_gain = feedforward_gain.astype(jnp.float32)
    second_shift = feedforward_shift.astype(jnp.float32)
    page_count, span_size, model_width = tokens.shape
    patch_span = patches.shape[1]
    seq_count = lax.axis_size("seq")
    slot_size = span_size * seq_count
    patch_slots = patch_span * seq_count
    row_count = span_size + patch_span
    key_count = row_count * seq_count
    head_count = reading_bias_table.shape[0]
    head_size = model_width // head_count
    line_bins = reading_bias_table.shape[1]
    plane_bins = horizontal_bias_table.shape[1]
    score_scale = head_size ** (-0.5)
    seq_index = lax.axis_index("seq")
    text_places = seq_index * span_size + jnp.arange(span_size, dtype=jnp.int32)
    local_cells = seq_index * patch_span + jnp.arange(patch_span, dtype=jnp.int32)
    text_live = text_places[None, :] < page_length[:, None]
    patch_live = grid_live(local_cells)
    text_factor = text_live[:, :, None]
    patch_factor = patch_live[None, :, None]
    masked = tokens * text_factor.astype(jnp.bfloat16)
    rimmed = with_halo(masked, (("seq", 1),), 3)
    reach = GRID_SIDE + 1
    patch_masked = patches * patch_factor.astype(jnp.bfloat16)
    patch_rimmed = with_halo(patch_masked, (("seq", 1),), reach)
    pages = lax.axis_size("page")
    table = jnp.concatenate(
        [
            horizontal_bias_table,
            vertical_bias_table,
            reading_bias_table,
            jnp.zeros((head_count, 256 - 2 * plane_bins - line_bins), jnp.bfloat16),
        ],
        axis=1,
    ).astype(jnp.float32)
    taps = jnp.pad(
        jnp.concatenate([conv_weight, patch_conv_weight], axis=1).astype(jnp.float32).T, ((0, 6), (0, 0))
    )
    vectors = jnp.concatenate(
        [
            jnp.stack(
                [
                    query_bias, value_bias, out_bias, down_bias,
                    attention_gain, attention_shift, feedforward_gain, feedforward_shift,
                ]
            ),
            up_bias.reshape(-1, model_width),
        ]
    ).astype(jnp.float32)
    (
        hidden, hidden_low, queries, keys, values, mixture_low, weights, columns, key_rows, query_rows,
    ) = forward(
        pages, page_length, tokens, patches, box_position, taps, (query_weight, key_weight, value_weight),
        vectors, table,
    )
    places = jnp.stack(
        [seq_index, seq_index % 2, lax.axis_index("page"), seq_index // 2]
    ).astype(jnp.int32)
    def flat(value):
        return value.reshape(-1, value.shape[-1])

    output, patch_output, delta_first, delta_mixture, middle_sums, feedforward_bundle = middle(
        places, hidden, mixture_low, cotangent, patch_cotangent,
        (out_weight, up_weight, down_weight), vectors, pages,
    )
    delta_first = delta_first.reshape(page_count, row_count, model_width)
    delta_mixture = delta_mixture.reshape(page_count, row_count, model_width)
    early_state = added(feedforward_bundle[0], swap(feedforward_bundle[1], "seq", 1))
    delta_mixture, early_state = lax.optimization_barrier((delta_mixture, early_state))
    delta_query_pages, delta_key_pages, delta_value_pages = [], [], []
    delta_plane, delta_line = 0.0, 0.0
    for page in range(page_count):
        delta_page_queries, delta_blocks, plane_part, line_part = backward_page(
            places,
            columns[page][:, ::128],
            key_rows[page],
            query_rows[page][:, :row_count],
            queries[page * row_count : (page + 1) * row_count],
            keys[page],
            values[page],
            delta_mixture[page],
            weights[page],
        )
        got = swap(delta_blocks[2:], "seq", 1)
        chip_sum = delta_blocks[:2].astype(jnp.float32) + got.astype(jnp.float32)
        got = swap(chip_sum[1].astype(jnp.bfloat16), "seq", 2)
        whole = (chip_sum[0] + got.astype(jnp.float32)).astype(jnp.bfloat16)
        delta_query_pages.append(delta_page_queries)
        delta_key_pages.append(whole[0])
        delta_value_pages.append(whole[1])
        delta_plane = delta_plane + plane_part
        delta_line = delta_line + line_part
    delta_queries = jnp.stack(delta_query_pages)
    delta_keys = jnp.stack(delta_key_pages)
    delta_values = jnp.stack(delta_value_pages)
    def clipped(sums, centre, bins):
        first, last = centre + 1 - bins // 2, centre - 1 + bins // 2
        return jnp.concatenate(
            [
                jnp.sum(sums[..., :first], axis=-1, keepdims=True),
                sums[..., first:last],
                jnp.sum(sums[..., last:], axis=-1, keepdims=True),
            ],
            axis=-1,
        )

    delta_plane = clipped(delta_plane, 72, plane_bins)
    delta_line = clipped(delta_line, 32, line_bins)
    delta_across, delta_upward = delta_plane[0], delta_plane[1]
    delta_query_offset = row_sum(delta_queries)
    delta_value_offset = row_sum(delta_values)
    delta_hidden = (
        delta_first
        + back_dot(delta_queries, query_weight)
        + back_dot(delta_keys, key_weight)
        + back_dot(delta_values, value_weight)
    )
    delta_position = delta_hidden[:, :span_size].astype(jnp.bfloat16)
    delta_rim = with_halo(delta_position, (("seq", 1),), 3)
    delta_masked = jnp.zeros((page_count, span_size, model_width), jnp.float32)
    tap_columns = []
    for dilation in (1, 2, 3):
        for offset in (-1, 0, 1):
            column = 3 * (dilation - 1) + offset + 1
            anchor = 3 + offset * dilation
            anchor_back = 3 - offset * dilation
            delta_masked = (
                delta_masked
                + delta_rim[:, anchor_back : anchor_back + span_size, :] * conv_taps[:, column]
            )
            tap_columns.append(
                jnp.einsum(
                    "ptd,ptd->d",
                    delta_position,
                    rimmed[:, anchor : anchor + span_size, :],
                    preferred_element_type=jnp.float32,
                )
            )
    delta_taps = jnp.stack(tap_columns, axis=1)
    tokens_gradient = delta_hidden[:, :span_size] + delta_masked * text_factor.astype(jnp.float32)
    delta_patch_position = delta_hidden[:, span_size:].astype(jnp.bfloat16)
    delta_patch_rim = with_halo(delta_patch_position, (("seq", 1),), reach)
    delta_patch_masked = jnp.zeros((page_count, patch_span, model_width), jnp.float32)
    patch_columns = []
    for vertical in (-1, 0, 1):
        for horizontal in (-1, 0, 1):
            column = 3 * (vertical + 1) + horizontal + 1
            anchor = reach + vertical * GRID_SIDE + horizontal
            anchor_back = reach - vertical * GRID_SIDE - horizontal
            delta_patch_masked = (
                delta_patch_masked
                + delta_patch_rim[:, anchor_back : anchor_back + patch_span, :]
                * patch_taps[:, column]
            )
            patch_columns.append(
                jnp.einsum(
                    "ptd,ptd->d",
                    delta_patch_position,
                    patch_rimmed[:, anchor : anchor + patch_span, :],
                    preferred_element_type=jnp.float32,
                )
            )
    delta_patch_taps = jnp.stack(patch_columns, axis=1)
    patches_gradient = delta_hidden[:, span_size:] + delta_patch_masked * patch_factor.astype(
        jnp.float32
    )
    tail_bundle = attention_bundle(
        places, [flat(value) for value in (hidden_low, delta_queries, delta_keys, delta_values)], pages
    )
    tail_state = added(tail_bundle[0], swap(tail_bundle[1], "seq", 1))
    query_part, key_part, value_part = bundle_parts(
        bundle_sum(tail_state, pages), model_width // pages, places[1]
    )
    up_part, down_part, out_part = bundle_parts(
        bundle_sum(early_state, pages), up_weight.shape[1] // pages, places[1]
    )
    up_part = up_part.reshape(model_width // pages, -1)
    matrix_parts = (query_part, key_part, value_part, out_part, up_part, down_part)
    vector_parts = total_sum(
        (
            delta_taps,
            delta_patch_taps,
            delta_query_offset,
            delta_value_offset,
            middle_sums[OUT_BIAS],
            middle_sums[UP_BIAS : UP_BIAS + 4].reshape(-1),
            middle_sums[DOWN_BIAS],
            middle_sums[FIRST_GAIN],
            middle_sums[FIRST_SHIFT],
            middle_sums[SECOND_GAIN],
            middle_sums[SECOND_SHIFT],
            delta_line,
            delta_across,
            delta_upward,
        )
    )
    return (
        output,
        patch_output,
        tokens_gradient,
        patches_gradient,
        matrix_parts[0],
        matrix_parts[1],
        matrix_parts[2],
        matrix_parts[3],
        matrix_parts[4],
        matrix_parts[5],
        vector_parts[0],
        vector_parts[1],
        vector_parts[2],
        vector_parts[3],
        vector_parts[4],
        vector_parts[5],
        vector_parts[6],
        vector_parts[7],
        vector_parts[8],
        vector_parts[9],
        vector_parts[10],
        vector_parts[11],
        vector_parts[12],
        vector_parts[13],
    )


def solution(mesh):
    in_specs = (
        P("page", "seq", None),
        P("page", "seq", None),
        P("page"),
        P(None, "page", None),
        P(),
        P(),
        P(),
        P(),
        P(),
        P(),
        P(),
        P(),
        P(),
        P(),
        P(),
        P(),
        P(),
        P(),
        P(),
        P(),
        P(),
        P(),
        P(),
        P(),
        P("page", "seq", None),
        P("page", "seq", None),
    )
    out_specs = (
        P("page", "seq", None),
        P("page", "seq", None),
        P("page", "seq", None),
        P("page", "seq", None),
        P("page", "seq"),
        P("page", "seq"),
        P("page", "seq"),
        P("page", "seq"),
        P("page", "seq"),
        P("page", "seq"),
        P(),
        P(),
        P(),
        P(),
        P(),
        P(),
        P(),
        P(),
        P(),
        P(),
        P(),
        P(),
        P(),
        P(),
    )
    return jax.shard_map(shards, mesh=mesh, in_specs=in_specs, out_specs=out_specs, check_vma=False)
```

profile of v0, /device:TPU:0, one launch (start us, length us, event | category | flops | bytes accessed | tf_op | source)
XLA Modules:
  0.0 350.5 jit_solution(12894261307974013793)
XLA Ops:
  15.1 50.9 %forward.1 = (f32[432,768]{1,0:T(8,128)}, bf16[432,768]{1,0:T(8,128)(2,1)S(1)}, bf16[432,768]{1,0:T(8,128)(2,1)S(1)}, bf16[3,640,768]{2,1,0:T(8,128)(2,1)}, bf16...) custom-call(s32[3]{0:T(128)S(1)} %copy-done.18, ...), custom_call_target="tpu_custom_call" | custom-call | flops 8000000000 | bytes 25000000 | tf_op jit(solution)/shard_map/forward/pallas_call | solution.py:431
  66.9 45.9 %middle.1 = (f32[3,128,768]{2,1,0:T(8,128)}, f32[3,16,768]{2,1,0:T(8,128)}, f32[432,768]{1,0:T(8,128)}, bf16[432,768]{1,0:T(8,128)(2,1)}, f32[16,768]{1,0:T(8,128)}, /*index=5*/bf16[2,16,432,384]{3,2,1,0:T(8,128)(2,1)}) custom-call(s32[4]{0:T(128)} %pad_add_fusion.scalar_ref, f32[432,768]{1,0:T(8,128)} %get-tuple-element.54.hidden_ref, ...), custom_call_target="tpu_custom_call" | custom-call | flops 14000000000 | bytes 30000000 | tf_op jit(solution)/shard_map/middle/pallas_call | solution.py:843
  112.8 5.5 %slice_bitcast_fusion = bf16[16,432,384]{2,1,0:T(8,128)(2,1)} fusion(bf16[2,16,432,384]{3,2,1,0:T(8,128)(2,1)} %get-tuple-element.66), kind=kLoop, calls=%fused_computation.3 | loop fusion | bytes 10616832 | tf_op jit(solution)/shard_map/squeeze | solution.py:1136
  120.5 2.5 collective-permute-start.24
  126.6 4.7 %collective-permute-start.22 = (bf16[3,3,768]{2,1,0:T(4,128)(2,1)}, bf16[3,3,768]{2,1,0:T(4,128)(2,1)}, u32[]{:S(2)}, u32[]{:S(2)}) collective-permute-start(bf16[3,3,768]{2,1,0:T(4,128)(2,1)} %get-tuple-element.202), channel_id=1, source_target_pairs={{0,1},{1,2},{2,3},{4,5},{5,6},{6,7},{8,9},{9,10},{10,11},{12,13},{... | collective-permute-start | bytes 41480 | tf_op jit(solution)/shard_map/ppermute | solution.py:28
  135.0 3.2 slice_bitcast_fusion.10
  139.6 2.9 slice_bitcast_fusion.3
  142.6 7.9 %fusion = bf16[16,432,384]{2,1,0:T(8,128)(2,1)} fusion(bf16[16,432,384]{2,1,0:T(8,128)(2,1)} %collective-permute-done, bf16[2,16,432,384]{3,2,1,0:T(8,128)(2,1)} %get-tuple-element.66), kind=kLoop, calls=%fused_computation.1 | loop fusion | flops 10616832 | bytes 15925248 | tf_op jit(solution)/shard_map/convert_element_type | solution.py:984
  151.1 11.9 %backward_page.3 = (bf16[144,768]{1,0:T(8,128)(2,1)S(1)}, bf16[4,2,144,768]{3,2,1,0:T(8,128)(2,1)S(1)}, f32[2,12,256]{2,1,0:T(8,128)S(1)}, f32[12,128]{1,0:T(8,128)S(1)}) custom-call(s32[4]{0:T(128)S(1)} %copy-done.17, s32[144,2]{1,0:T(8,128)S(1)} %slice.599.columns_ref, s32[8,640]{1,0:T(8,128)S(1)} %get-tuple-element.239.rows_ref, s32[8,144]{1,0:T(8,128)S(1)} %bitcast.248, ...), custom_call_target="tpu_custom_call" | custom-call | flops 3000000000 | bytes 6000000 | tf_op jit(solution)/shard_map/backward_page/pallas_call | solution.py:597
  163.0 11.9 %backward_page.4 = (bf16[144,768]{1,0:T(8,128)(2,1)S(1)}, bf16[4,2,144,768]{3,2,1,0:T(8,128)(2,1)S(1)}, f32[2,12,256]{2,1,0:T(8,128)S(1)}, f32[12,128]{1,0:T(8,128)S(1)}) custom-call(s32[4]{0:T(128)S(1)} %copy-done.17, s32[144,2]{1,0:T(8,128)S(1)} %copy-done.15, s32[8,640]{1,0:T(8,128)S(1)} %get-tuple-element.241.rows_ref, s32[8,144]{1,0:T(8,128)S(1)} %bitcast.247, ...), custom_call_target="tpu_custom_call" | custom-call | flops 3000000000 | bytes 6000000 | tf_op jit(solution)/shard_map/backward_page/pallas_call | solution.py:597
  176.2 11.9 %backward_page.5 = (bf16[144,768]{1,0:T(8,128)(2,1)S(1)}, bf16[4,2,144,768]{3,2,1,0:T(8,128)(2,1)S(1)}, f32[2,12,256]{2,1,0:T(8,128)S(1)}, f32[12,128]{1,0:T(8,128)S(1)}) custom-call(s32[4]{0:T(128)S(1)} %copy-done.17, s32[144,2]{1,0:T(8,128)S(1)} %copy-done.14, s32[8,640]{1,0:T(8,128)S(1)} %get-tuple-element.240.rows_ref, s32[8,144]{1,0:T(8,128)S(1)} %bitcast.246, ...), custom_call_target="tpu_custom_call" | custom-call | flops 3000000000 | bytes 6000000 | tf_op jit(solution)/shard_map/backward_page/pallas_call | solution.py:597
  195.0 2.2 slice.636
  197.2 2.1 slice.641
  200.0 3.6 %slice.705 = bf16[8,432,384]{2,1,0:T(8,128)(2,1)} slice(bf16[16,432,384]{2,1,0:T(8,128)(2,1)} %fusion), slice={[8:16], [0:432], [0:384]} | slice | bytes 5308416 | tf_op jit(solution)/shard_map/slice | solution.py:990
  209.8 2.0 collective-permute-start.4
  211.9 9.2 %collective-permute-done.2 = bf16[2,144,768]{2,1,0:T(8,128)(2,1)S(1)} collective-permute-done((bf16[2,144,768]{2,1,0:T(8,128)(2,1)S(1)}, bf16[2,144,768]{2,1,0:T(8,128)(2,1)S(1)}, u32[]{:S(2)}, u32[]{:S(2)}) %collective-permute-start.2) | collective-permute-done | bytes 442400 | tf_op jit(solution)/shard_map/ppermute | solution.py:82
  222.8 7.0 %collective-permute-done.4 = bf16[2,144,768]{2,1,0:T(8,128)(2,1)S(1)} collective-permute-done((bf16[2,144,768]{2,1,0:T(8,128)(2,1)S(1)}, bf16[2,144,768]{2,1,0:T(8,128)(2,1)S(1)}, u32[]{:S(2)}, u32[]{:S(2)}) %collective-permute-start.4) | collective-permute-done | bytes 442400 | tf_op jit(solution)/shard_map/ppermute | solution.py:82
  230.3 10.9 %collective-permute-done.6 = bf16[2,144,768]{2,1,0:T(8,128)(2,1)S(1)} collective-permute-done((bf16[2,144,768]{2,1,0:T(8,128)(2,1)S(1)}, bf16[2,144,768]{2,1,0:T(8,128)(2,1)S(1)}, u32[]{:S(2)}, u32[]{:S(2)}) %collective-permute-start.6) | collective-permute-done | bytes 442400 | tf_op jit(solution)/shard_map/ppermute | solution.py:82
  248.5 4.0 %fusion.18 = (f32[768]{0:T(1024)S(1)}, f32[768]{0:T(1024)S(1)}, f32[768]{0:T(1024)S(1)}, f32[768]{0:T(1024)S(1)}, f32[768]{0:T(1024)S(1)}, /*index=5*/f32[768]{0...) fusion(bf16[3,3,768]{2,1,0:T(4,128)(2,1)S(1)} %collective-permute-done.23, bf16[3,128,768]{2,1,0:T(8,128)(2,1)} %copy-done.23, ...), kind=kLoop, calls=%fused_computation.48 | loop fusion | flops 13560576 | bytes 1818624 | tf_op jit(solution)/shard_map/ptd,ptd->d/dot_general | solution.py:1200
  254.8 3.6 %attention_weights.1 = bf16[2,16,144,384]{3,2,1,0:T(8,128)(2,1)S(1)} custom-call(s32[4]{0:T(128)S(1)} %copy-done.17, bf16[432,768]{1,0:T(8,128)(2,1)S(1)} %get-tuple-element.75.hidden_ref, bf16[432,768]{1,0:T(8,128)(2,1)S(1)} %bitcast.240, bf16[432,768]{1,0:T(8,128)(2,1)S(1)} %bitcast.242, bf16[432,768]{1,0:T(8,128)(2,1)S(1)} %bitcast.241), custom_call_target="tpu_custom_call" | custom-call | flops 1600000000 | bytes 10000000 | tf_op jit(solution)/shard_map/attention_weights/pallas_call | solution.py:958
  259.7 2.9 collective-permute-done.26
  265.4 3.0 collective-permute-start.8
  268.4 7.1 %collective-permute-done.27 = f32[200,128]{1,0:T(8,128)S(1)} collective-permute-done((f32[200,128]{1,0:T(8,128)S(1)}, f32[200,128]{1,0:T(8,128)S(1)}, u32[]{:S(2)}, u32[]{:S(2)}) %collective-permute-start.27) | collective-permute-done | bytes 102432 | tf_op jit(solution)/shard_map/ppermute | solution.py:82
  277.2 2.4 add_convert_fusion
  286.6 2.7 fusion.11
  289.6 2.7 collective-permute-start.30
  293.2 2.0 collective-permute-done.30
  295.2 4.6 %collective-permute-done.12 = bf16[8,144,384]{2,1,0:T(8,128)(2,1)S(1)} collective-permute-done((bf16[8,144,384]{2,1,0:T(8,128)(2,1)S(1)}, bf16[8,144,384]{2,1,0:T(8,128)(2,1)S(1)}, u32[]{:S(2)}, u32[]{:S(2)}) %collective-permute-start.12) | collective-permute-done | bytes 884768 | tf_op jit(solution)/shard_map/ppermute | solution.py:980
  304.5 4.1 %collective-permute-done.13 = bf16[4,144,384]{2,1,0:T(8,128)(2,1)S(1)} collective-permute-done((bf16[4,144,384]{2,1,0:T(8,128)(2,1)S(1)}, bf16[4,144,384]{2,1,0:T(8,128)(2,1)S(1)}, u32[]{:S(2)}, u32[]{:S(2)}) %collective-permute-start.13) | collective-permute-done | bytes 442400 | tf_op jit(solution)/shard_map/ppermute | solution.py:980
  310.9 13.3 %collective-permute-done.14 = bf16[2,144,384]{2,1,0:T(8,128)(2,1)S(1)} collective-permute-done((bf16[2,144,384]{2,1,0:T(8,128)(2,1)S(1)}, bf16[2,144,384]{2,1,0:T(8,128)(2,1)S(1)}, u32[]{:S(2)}, u32[]{:S(2)}) %collective-permute-start.14) | collective-permute-done | bytes 221216 | tf_op jit(solution)/shard_map/ppermute | solution.py:980
  324.3 2.7 collective-permute-start.15
  327.6 11.9 %collective-permute-done.15 = bf16[1,144,384]{2,1,0:T(8,128)(2,1)S(1)} collective-permute-done((bf16[1,144,384]{2,1,0:T(8,128)(2,1)S(1)}, bf16[1,144,384]{2,1,0:T(8,128)(2,1)S(1)}, u32[]{:S(2)}, u32[]{:S(2)}) %collective-permute-start.15) | collective-permute-done | bytes 110624 | tf_op jit(solution)/shard_map/ppermute | solution.py:980
  (357 shorter events, 84.9 us)
Async XLA Ops:
  6.9 59.1 %copy-start.16 = (f32[12,768]{1,0:T(8,128)}, f32[12,768]{1,0:T(8,128)S(1)}, u32[]{:S(2)}) copy-start(f32[12,768]{1,0:T(8,128)S(1)} %convert_element_type.275.vector_ref) | copy-start | bytes 110596
  118.3 24.3 %collective-permute-start = (bf16[16,432,384]{2,1,0:T(8,128)(2,1)}, bf16[16,432,384]{2,1,0:T(8,128)(2,1)}, u32[]{:S(2)}, u32[]{:S(2)}) collective-permute-start(bf16[16,432,384]{2,1,0:T(8,128)(2,1)} %slice_bitcast_fusion), channel_id=1, source_target_pairs={{0,1},{1,0},{2,3},{3,2},{4,5},{5,4},{6,7},{7,6},{8,9},{9,8},{10,11... | collective-permute-start | bytes 15925256 | tf_op jit(solution)/shard_map/ppermute | solution.py:82
  120.5 124.7 %collective-permute-start.24 = (bf16[3,9,768]{2,1,0:T(8,128)(2,1)}, bf16[3,9,768]{2,1,0:T(8,128)(2,1)}, u32[]{:S(2)}, u32[]{:S(2)}) collective-permute-start(bf16[3,9,768]{2,1,0:T(8,128)(2,1)} %get-tuple-element.237), channel_id=1, source_target_pairs={{0,1},{1,2},{2,3},{4,5},{5,6},{6,7},{8,9},{9,10},{10,11},{12,13},{... | collective-permute-start | bytes 124424 | tf_op jit(solution)/shard_map/ppermute | solution.py:28
  123.0 122.2 %collective-permute-start.25 = (bf16[3,9,768]{2,1,0:T(8,128)(2,1)}, bf16[3,9,768]{2,1,0:T(8,128)(2,1)}, u32[]{:S(2)}, u32[]{:S(2)}) collective-permute-start(bf16[3,9,768]{2,1,0:T(8,128)(2,1)} %get-tuple-element.238), channel_id=1, source_target_pairs={{1,0},{2,1},{3,2},{5,4},{6,5},{7,6},{9,8},{10,9},{11,10},{13,12},{... | collective-permute-start | bytes 124424 | tf_op jit(solution)/shard_map/ppermute | solution.py:30
  126.6 121.8 %collective-permute-start.22 = (bf16[3,3,768]{2,1,0:T(4,128)(2,1)}, bf16[3,3,768]{2,1,0:T(4,128)(2,1)}, u32[]{:S(2)}, u32[]{:S(2)}) collective-permute-start(bf16[3,3,768]{2,1,0:T(4,128)(2,1)} %get-tuple-element.202), channel_id=1, source_target_pairs={{0,1},{1,2},{2,3},{4,5},{5,6},{6,7},{8,9},{9,10},{10,11},{12,13},{... | collective-permute-start | bytes 41480 | tf_op jit(solution)/shard_map/ppermute | solution.py:28
  191.5 14.2 %collective-permute-start.1 = (bf16[2,2,144,768]{3,2,1,0:T(8,128)(2,1)}, bf16[2,2,144,768]{3,2,1,0:T(8,128)(2,1)}, u32[]{:S(2)}, u32[]{:S(2)}) collective-permute-start(bf16[2,2,144,768]{3,2,1,0:T(8,128)(2,1)} %slice.631), channel_id=1, source_target_pairs={{0,1},{1,0},{2,3},{3,2},{4,5},{5,4},{6,7},{7,6},{8,9},{9,8},{10,11... | collective-permute-start | bytes 2654216 | tf_op jit(solution)/shard_map/ppermute | solution.py:82
  197.2 10.9 %collective-permute-start.3 = (bf16[2,2,144,768]{3,2,1,0:T(8,128)(2,1)}, bf16[2,2,144,768]{3,2,1,0:T(8,128)(2,1)}, u32[]{:S(2)}, u32[]{:S(2)}) collective-permute-start(bf16[2,2,144,768]{3,2,1,0:T(8,128)(2,1)} %slice.636), channel_id=1, source_target_pairs={{0,1},{1,0},{2,3},{3,2},{4,5},{5,4},{6,7},{7,6},{8,9},{9,8},{10,11... | collective-permute-start | bytes 2654216 | tf_op jit(solution)/shard_map/ppermute | solution.py:82
  206.1 3.6 %collective-permute-start.5 = (bf16[2,2,144,768]{3,2,1,0:T(8,128)(2,1)S(1)}, bf16[2,2,144,768]{3,2,1,0:T(8,128)(2,1)S(1)}, u32[]{:S(2)}, u32[]{:S(2)}) collective-permute-start(bf16[2,2,144,768]{3,2,1,0:T(8,128)(2,1)S(1)} %copy-done.29), channel_id=1, source_target_pairs={{0,1},{1,0},{2,3},{3,2},{4,5},{5,4},{6,7},{7,6},{8,9},{9,8},{10,11... | collective-permute-start | bytes 2654216 | tf_op jit(solution)/shard_map/ppermute | solution.py:82
  208.1 13.1 %collective-permute-start.2 = (bf16[2,144,768]{2,1,0:T(8,128)(2,1)S(1)}, bf16[2,144,768]{2,1,0:T(8,128)(2,1)S(1)}, u32[]{:S(2)}, u32[]{:S(2)}) collective-permute-start(bf16[2,144,768]{2,1,0:T(8,128)(2,1)S(1)} %fusion.42), channel_id=1, source_target_pairs={{0,2},{1,3},{2,0},{3,1},{4,6},{5,7},{6,4},{7,5},{8,10},{9,11},{10,... | collective-permute-start | bytes 1327112 | tf_op jit(solution)/shard_map/ppermute | solution.py:82
  209.8 20.0 %collective-permute-start.4 = (bf16[2,144,768]{2,1,0:T(8,128)(2,1)S(1)}, bf16[2,144,768]{2,1,0:T(8,128)(2,1)S(1)}, u32[]{:S(2)}, u32[]{:S(2)}) collective-permute-start(bf16[2,144,768]{2,1,0:T(8,128)(2,1)S(1)} %fusion.43), channel_id=1, source_target_pairs={{0,2},{1,3},{2,0},{3,1},{4,6},{5,7},{6,4},{7,5},{8,10},{9,11},{10,... | collective-permute-start | bytes 1327112 | tf_op jit(solution)/shard_map/ppermute | solution.py:82
  221.2 27.3 %collective-permute-start.23 = (bf16[3,3,768]{2,1,0:T(4,128)(2,1)S(1)}, bf16[3,3,768]{2,1,0:T(4,128)(2,1)S(1)}, u32[]{:S(2)}, u32[]{:S(2)}) collective-permute-start(bf16[3,3,768]{2,1,0:T(4,128)(2,1)S(1)} %copy-done.34), channel_id=1, source_target_pairs={{1,0},{2,1},{3,2},{5,4},{6,5},{7,6},{9,8},{10,9},{11,10},{13,12},{... | collective-permute-start | bytes 41480 | tf_op jit(solution)/shard_map/ppermute | solution.py:30
  229.8 11.3 %collective-permute-start.6 = (bf16[2,144,768]{2,1,0:T(8,128)(2,1)S(1)}, bf16[2,144,768]{2,1,0:T(8,128)(2,1)S(1)}, u32[]{:S(2)}, u32[]{:S(2)}) collective-permute-start(bf16[2,144,768]{2,1,0:T(8,128)(2,1)S(1)} %fusion.44), channel_id=1, source_target_pairs={{0,2},{1,3},{2,0},{3,1},{4,6},{5,7},{6,4},{7,5},{8,10},{9,11},{10,... | collective-permute-start | bytes 1327112 | tf_op jit(solution)/shard_map/ppermute | solution.py:82
  241.1 36.0 %collective-permute-start.17 = (bf16[8,432,384]{2,1,0:T(8,128)(2,1)}, bf16[8,432,384]{2,1,0:T(8,128)(2,1)}, u32[]{:S(2)}, u32[]{:S(2)}) collective-permute-start(bf16[8,432,384]{2,1,0:T(8,128)(2,1)} %slice.705), channel_id=1, source_target_pairs={{0,2},{1,5},{2,0},{3,7},{4,6},{5,1},{6,4},{7,3},{8,10},{9,13},{10,... | collective-permute-start | bytes 7962632 | tf_op jit(solution)/shard_map/ppermute | solution.py:980
  258.7 21.6 %collective-permute-start.11 = (bf16[16,144,384]{2,1,0:T(8,128)(2,1)S(1)}, bf16[16,144,384]{2,1,0:T(8,128)(2,1)S(1)}, u32[]{:S(2)}, u32[]{:S(2)}) collective-permute-start(bf16[16,144,384]{2,1,0:T(8,128)(2,1)S(1)} %slice_bitcast_fusion.4), channel_id=1, source_target_pairs={{0,1},{1,0},{2,3},{3,2},{4,5},{5,4},{6,7},{7,6},{8,9},{9,8},{10,11... | collective-permute-start | bytes 5308424 | tf_op jit(solution)/shard_map/ppermute | solution.py:82
  259.6 3.0 collective-permute-start.26
  262.6 12.9 %collective-permute-start.27 = (f32[200,128]{1,0:T(8,128)S(1)}, f32[200,128]{1,0:T(8,128)S(1)}, u32[]{:S(2)}, u32[]{:S(2)}) collective-permute-start(f32[200,128]{1,0:T(8,128)S(1)} %fusion.77), channel_id=1, source_target_pairs={{0,2},{1,3},{2,0},{3,1},{4,6},{5,7},{6,4},{7,5},{8,10},{9,11},{10,... | collective-permute-start | bytes 307208 | tf_op jit(solution)/shard_map/ppermute | solution.py:82
  264.1 19.1 %collective-permute-start.7 = (bf16[3,3,768]{2,1,0:T(4,128)(2,1)S(1)}, bf16[3,3,768]{2,1,0:T(4,128)(2,1)S(1)}, u32[]{:S(2)}, u32[]{:S(2)}) collective-permute-start(bf16[3,3,768]{2,1,0:T(4,128)(2,1)S(1)} %get-tuple-element.200), channel_id=1, source_target_pairs={{1,0},{2,1},{3,2},{5,4},{6,5},{7,6},{9,8},{10,9},{11,10},{13,12},{... | collective-permute-start | bytes 41480 | tf_op jit(solution)/shard_map/ppermute | solution.py:30
  265.4 19.4 %collective-permute-start.8 = (bf16[3,3,768]{2,1,0:T(4,128)(2,1)S(1)}, bf16[3,3,768]{2,1,0:T(4,128)(2,1)S(1)}, u32[]{:S(2)}, u32[]{:S(2)}) collective-permute-start(bf16[3,3,768]{2,1,0:T(4,128)(2,1)S(1)} %get-tuple-element.201), channel_id=1, source_target_pairs={{0,1},{1,2},{2,3},{4,5},{5,6},{6,7},{8,9},{9,10},{10,11},{12,13},{... | collective-permute-start | bytes 41480 | tf_op jit(solution)/shard_map/ppermute | solution.py:28
  275.6 6.4 %collective-permute-start.28 = (f32[200,128]{1,0:T(8,128)S(1)}, f32[200,128]{1,0:T(8,128)S(1)}, u32[]{:S(2)}, u32[]{:S(2)}) collective-permute-start(f32[200,128]{1,0:T(8,128)S(1)} %fusion.92), channel_id=1, source_target_pairs={{0,4},{4,0},{8,12},{12,8},{16,20},{20,16},{24,28},{28,24},{1,5},{5... | collective-permute-start | bytes 307208 | tf_op jit(solution)/shard_map/ppermute | solution.py:82
  279.7 22.7 %collective-permute-start.18 = (bf16[4,432,384]{2,1,0:T(8,128)(2,1)S(1)}, bf16[4,432,384]{2,1,0:T(8,128)(2,1)S(1)}, u32[]{:S(2)}, u32[]{:S(2)}) collective-permute-start(bf16[4,432,384]{2,1,0:T(8,128)(2,1)S(1)} %slice.857), channel_id=1, source_target_pairs={{0,4},{1,3},{2,6},{3,1},{4,0},{5,7},{6,2},{7,5},{8,12},{9,11},{10,... | collective-permute-start | bytes 3981320 | tf_op jit(solution)/shard_map/ppermute | solution.py:980
  281.0 18.9 %collective-permute-start.12 = (bf16[8,144,384]{2,1,0:T(8,128)(2,1)S(1)}, bf16[8,144,384]{2,1,0:T(8,128)(2,1)S(1)}, u32[]{:S(2)}, u32[]{:S(2)}) collective-permute-start(bf16[8,144,384]{2,1,0:T(8,128)(2,1)S(1)} %slice.842), channel_id=1, source_target_pairs={{0,2},{1,5},{2,0},{3,7},{4,6},{5,1},{6,4},{7,3},{8,10},{9,13},{10,... | collective-permute-start | bytes 2654216 | tf_op jit(solution)/shard_map/ppermute | solution.py:980
  281.9 10.3 %collective-permute-start.10 = (bf16[3,9,768]{2,1,0:T(8,128)(2,1)S(1)}, bf16[3,9,768]{2,1,0:T(8,128)(2,1)S(1)}, u32[]{:S(2)}, u32[]{:S(2)}) collective-permute-start(bf16[3,9,768]{2,1,0:T(8,128)(2,1)S(1)} %get-tuple-element.236), channel_id=1, source_target_pairs={{0,1},{1,2},{2,3},{4,5},{5,6},{6,7},{8,9},{9,10},{10,11},{12,13},{... | collective-permute-start | bytes 124424 | tf_op jit(solution)/shard_map/ppermute | solution.py:28
  283.3 9.0 %collective-permute-start.9 = (bf16[3,9,768]{2,1,0:T(8,128)(2,1)S(1)}, bf16[3,9,768]{2,1,0:T(8,128)(2,1)S(1)}, u32[]{:S(2)}, u32[]{:S(2)}) collective-permute-start(bf16[3,9,768]{2,1,0:T(8,128)(2,1)S(1)} %get-tuple-element.235), channel_id=1, source_target_pairs={{1,0},{2,1},{3,2},{5,4},{6,5},{7,6},{9,8},{10,9},{11,10},{13,12},{... | collective-permute-start | bytes 124424 | tf_op jit(solution)/shard_map/ppermute | solution.py:30
  284.8 4.7 %collective-permute-start.29 = (f32[200,128]{1,0:T(8,128)S(1)}, f32[200,128]{1,0:T(8,128)S(1)}, u32[]{:S(2)}, u32[]{:S(2)}) collective-permute-start(f32[200,128]{1,0:T(8,128)S(1)} %add.240), channel_id=1, source_target_pairs={{0,8},{4,12},{8,0},{12,4},{16,24},{20,28},{24,16},{28,20},{1,9},{5... | collective-permute-start | bytes 307208 | tf_op jit(solution)/shard_map/ppermute | solution.py:82
  289.6 5.6 %collective-permute-start.30 = (f32[200,128]{1,0:T(8,128)S(1)}, f32[200,128]{1,0:T(8,128)S(1)}, u32[]{:S(2)}, u32[]{:S(2)}) collective-permute-start(f32[200,128]{1,0:T(8,128)S(1)} %add.241), channel_id=1, source_target_pairs={{0,16},{4,20},{8,24},{12,28},{16,0},{20,4},{24,8},{28,12},{1,17},{... | collective-permute-start | bytes 307208 | tf_op jit(solution)/shard_map/ppermute | solution.py:82
  300.2 8.4 %collective-permute-start.13 = (bf16[4,144,384]{2,1,0:T(8,128)(2,1)S(1)}, bf16[4,144,384]{2,1,0:T(8,128)(2,1)S(1)}, u32[]{:S(2)}, u32[]{:S(2)}) collective-permute-start(bf16[4,144,384]{2,1,0:T(8,128)(2,1)S(1)} %slice.844), channel_id=1, source_target_pairs={{0,4},{1,3},{2,6},{3,1},{4,0},{5,7},{6,2},{7,5},{8,12},{9,11},{10,... | collective-permute-start | bytes 1327112 | tf_op jit(solution)/shard_map/ppermute | solution.py:980
  302.8 24.1 %collective-permute-start.19 = (bf16[2,432,384]{2,1,0:T(8,128)(2,1)S(1)}, bf16[2,432,384]{2,1,0:T(8,128)(2,1)S(1)}, u32[]{:S(2)}, u32[]{:S(2)}) collective-permute-start(bf16[2,432,384]{2,1,0:T(8,128)(2,1)S(1)} %slice.859), channel_id=1, source_target_pairs={{0,8},{1,9},{2,10},{3,11},{4,12},{5,13},{6,14},{7,15},{8,0},{9,1},... | collective-permute-start | bytes 1990664 | tf_op jit(solution)/shard_map/ppermute | solution.py:980
  308.7 15.5 %collective-permute-start.14 = (bf16[2,144,384]{2,1,0:T(8,128)(2,1)S(1)}, bf16[2,144,384]{2,1,0:T(8,128)(2,1)S(1)}, u32[]{:S(2)}, u32[]{:S(2)}) collective-permute-start(bf16[2,144,384]{2,1,0:T(8,128)(2,1)S(1)} %slice.846), channel_id=1, source_target_pairs={{0,8},{1,9},{2,10},{3,11},{4,12},{5,13},{6,14},{7,15},{8,0},{9,1},... | collective-permute-start | bytes 663560 | tf_op jit(solution)/shard_map/ppermute | solution.py:980
  324.3 15.2 %collective-permute-start.15 = (bf16[1,144,384]{2,1,0:T(8,128)(2,1)S(1)}, bf16[1,144,384]{2,1,0:T(8,128)(2,1)S(1)}, u32[]{:S(2)}, u32[]{:S(2)}) collective-permute-start(bf16[1,144,384]{2,1,0:T(8,128)(2,1)S(1)} %slice.848), channel_id=1, source_target_pairs={{0,16},{1,17},{2,18},{3,19},{4,20},{5,21},{6,22},{7,23},{8,24},{9,... | collective-permute-start | bytes 331784 | tf_op jit(solution)/shard_map/ppermute | solution.py:980
  327.2 18.5 %collective-permute-start.20 = (bf16[1,432,384]{2,1,0:T(8,128)(2,1)S(1)}, bf16[1,432,384]{2,1,0:T(8,128)(2,1)S(1)}, u32[]{:S(2)}, u32[]{:S(2)}) collective-permute-start(bf16[1,432,384]{2,1,0:T(8,128)(2,1)S(1)} %slice.861), channel_id=1, source_target_pairs={{0,16},{1,17},{2,18},{3,19},{4,20},{5,21},{6,22},{7,23},{8,24},{9,... | collective-permute-start | bytes 995336 | tf_op jit(solution)/shard_map/ppermute | solution.py:980
  339.8 4.9 %collective-permute-start.16 = (bf16[144,192]{1,0:T(8,128)(2,1)S(1)}, bf16[144,192]{1,0:T(8,128)(2,1)S(1)}, u32[]{:S(2)}, u32[]{:S(2)}) collective-permute-start(bf16[144,192]{1,0:T(8,128)(2,1)S(1)} %pad_maximum_fusion.12), channel_id=1, source_target_pairs={{0,1},{1,0},{2,3},{3,2},{4,5},{5,4},{6,7},{7,6},{8,9},{9,8},{10,11... | collective-permute-start | bytes 165896 | tf_op jit(solution)/shard_map/ppermute | solution.py:82
  346.3 1.5 collective-permute-start.21
  (67 other events, 319.2 us)
where the time goes:
time: 352 us; the launch traced here: 350 us
  Pallas kernels  136 us (39%)
  waiting for transfers between devices  74.5 us (21%)
  local copies, waits for them, and re-layouts  63.8 us (18%)
  starting transfers between devices  40 us (11%)
  other arithmetic  31.7 us (9%)
    pallas_call x1, Pallas kernels, forward(): pl.pallas_call(functools.partial(forward_kernel, pages), out_shape=(jax.S...  50.9 us
    pallas_call x1, Pallas kernels, middle(): pl.pallas_call(functools.partial(middle_kernel, pages, direct), out_shape...  45.9 us
    ppermute x15, waiting for transfers between devices, swap(): return lax.ppermute(value, axis, [(i, i ^ bit) for i in range(count)])  39.6 us
    pallas_call x3, Pallas kernels, backward_page(): pl.pallas_call(backward_kernel, out_shape=(jax.ShapeDtypeStruct((row_coun...  35.7 us
    ppermute x8, waiting for transfers between devices, exchange(): return lax.ppermute(value, ('page', 'seq'), moves)  34.9 us
    unnamed x153, local copies, waits for them, and re-layouts  20.2 us
    ppermute x15, starting transfers between devices, swap(): return lax.ppermute(value, axis, [(i, i ^ bit) for i in range(count)])  12.8 us
    convert_element_type x10, other arithmetic, added(): (kept.astype(jnp.float32) + got.astype(jnp.float32)).astype(jnp.bfloat16)  11.8 us
  transfers between devices with their start and end apart: 31, of which 14 were waited for; matrix products, arithmetic and copies ran while one was open for 18% of the time, Pallas kernels for 11%

commit v1 on v0

--- a/solution.py
+++ b/solution.py
@@ -461,7 +461,7 @@
     )(lengths, tokens, patches, box, taps, *matrices, vectors, table)
 
 
-def backward_kernel(
+def backward_page_kernel(
     scalar_ref, columns_ref, rows_ref, query_rows_ref, query_ref, key_ref, value_ref, mixture_back_ref, weights_ref,
     query_back_ref, block_back_ref, plane_back_ref, line_back_ref,
     back, steps, mask_ref, hot_ref, query_hot_ref, band_ref,
@@ -595,7 +595,7 @@
     key_pad = keys.shape[0]
     heads = 2 * weights.shape[0]
     return pl.pallas_call(
-        backward_kernel,
+        backward_page_kernel,
         out_shape=(
             jax.ShapeDtypeStruct((row_count, width), jnp.bfloat16),
             jax.ShapeDtypeStruct((4, 2, row_count, width), jnp.bfloat16),
@@ -618,14 +618,29 @@
     )(scalars, columns, rows, query_rows, queries, keys, values, mixture_back, weights)
 
 
-def block_slots(scalar_ref, page, column, levels):
-    far = page ^ scalar_ref[2]
-    side = column ^ scalar_ref[3]
-    rest = 0
-    for level in range(1, levels):
-        rest = rest + (((far >> level) & 1) << (levels - 1 - level))
-    near = far & 1
-    return (side << levels) + (near << (levels - 1)) + rest, (near << levels) + (side << (levels - 1)) + rest
+def early_orders(far, side):
+    return (far[1], far[0], side) + tuple(far[2:]), (far[0], far[1], side) + tuple(far[2:])
+
+
+def late_orders(far, side):
+    return (side,) + tuple(far), (far[0], side) + tuple(far[1:])
+
+
+def slot_of_bits(bits):
+    slot = 0
+    for bit in bits:
+        slot = slot * 2 + bit
+    return slot
+
+
+def apart(one, other):
+    return (one + other) % 2
+
+
+def early_slots(scalar_ref, page, column, levels):
+    far = [apart((page >> level) & 1, (scalar_ref[2] >> level) & 1) for level in range(levels)]
+    side = apart(column, scalar_ref[3])
+    return [slot_of_bits(order) for order in early_orders(far, side)]
 
 
 NORM_CHUNK = 48
@@ -792,7 +807,7 @@
         at = pl.ds(pl.multiple_of(tile * block, block), block)
         result = dot_nn(flipped[...], up_back[:, at]).astype(jnp.bfloat16)
         for page in range(pages):
-            slot = block_slots(scalar_ref, page, column, levels)[0]
+            slot = early_slots(scalar_ref, page, column, levels)[0]
             bundle_ref[core, slot, pl.ds(pl.multiple_of(group * rows, 16), rows), :] = result[
                 page * rows : (page + 1) * rows
             ]
@@ -804,7 +819,7 @@
         at = pl.ds(pl.multiple_of(page * tall, 128), tall)
         result = dot_tn(activated[:, at], down_back[...]).astype(jnp.bfloat16)
         for column in range(2):
-            slot = block_slots(scalar_ref, page, column, levels)[1]
+            slot = early_slots(scalar_ref, page, column, levels)[1]
             bundle_ref[1 - core, slot, 0:tall, :] = result[:, column * block : (column + 1) * block]
         return carry
 
@@ -816,7 +831,7 @@
         at = pl.ds(pl.multiple_of(column * block, block), block)
         result = dot_nn(flipped[...], attention_back[:, at]).astype(jnp.bfloat16)
         for page in range(pages):
-            slots = block_slots(scalar_ref, page, column, levels)
+            slots = early_slots(scalar_ref, page, column, levels)
             for order in range(2):
                 first = page * rows + order * half
                 bundle_ref[core if order == 0 else 1 - core, slots[order], tall : tall + half, :] = result[
@@ -827,12 +842,16 @@
     lax.fori_loop(0, 2, out_weight_tile, 0)
 
 
+def in_tiles(width, pages):
+    return (width // pages) % 32 == 0 and pages >= 4
+
+
 def middle(places, hidden, mixture, cotangent, patch_cotangent, matrices, vectors, pages):
     count, span, width = cotangent.shape
     patch_span = patch_cotangent.shape[1]
     total_rows = hidden.shape[0]
     wide = matrices[1].shape[1]
-    direct = (width // pages) % 32 == 0
+    direct = in_tiles(width, pages)
     bf16, f32 = jnp.bfloat16, jnp.float32
     if direct:
         extra = (jax.ShapeDtypeStruct((2, 2 * pages, (wide + width // 2) // pages, 384), bf16),)
@@ -908,34 +927,6 @@
     return jnp.stack([jnp.where(mine, first, second), jnp.where(mine, second, first)])
 
 
-def attention_weight_kernel(
-    pages, scalar_ref, hidden_ref, query_back_ref, key_back_ref, value_back_ref, out_ref, flipped
-):
-    levels = pages.bit_length() - 1
-    core = scalar_ref[1]
-    rows = hidden_ref.shape[1] // pages
-    half = rows // 2
-    lanes = out_ref.shape[3]
-    flipped[...] = hidden_ref[...].T
-
-    def tile(column, carry):
-        at = pl.ds(pl.multiple_of(column * lanes, lanes), lanes)
-        for index, back_ref in enumerate((query_back_ref, key_back_ref, value_back_ref)):
-            result = dot_nn(flipped[...], back_ref[:, at]).astype(jnp.bfloat16)
-            for page in range(pages):
-                slots = block_slots(scalar_ref, page, column, levels)
-                first = page * rows
-                if index < 2:
-                    where = core if index == 0 else 1 - core
-                    out_ref[where, slots[index], 0:rows, :] = result[first : first + rows]
-                else:
-                    out_ref[core, slots[0], rows : rows + half, :] = result[first : first + half]
-                    out_ref[1 - core, slots[1], rows : rows + half, :] = result[first + half : first + rows]
-        return carry
-
-    lax.fori_loop(0, 2, tile, 0)
-
-
 def in_blocks(matrix, pages):
     rows, columns = matrix.shape[0] // pages, matrix.shape[1] // 2
     lanes = min(columns, 384)
@@ -943,28 +934,582 @@
     return blocks.transpose(0, 2, 3, 1, 4).reshape(pages * 2, rows * columns // lanes, lanes)
 
 
-def attention_bundle(places, operands, pages):
-    hidden, query_back, key_back, value_back = operands
-    width = hidden.shape[1]
-    if (width // pages) % 32:
-        return indexed_bundle(
+class Halving:
+    def __init__(self, keep, source, landing, landings, partners, sibling, sems, chunks):
+        self.keep, self.landing, self.landings = keep, landing, landings
+        total = keep.shape[0]
+        unit = total // chunks
+        send_sem, recv_sem = sems
+        self.arrivals, self.sends, self.needs = {}, {}, {}
+        used = 0
+        for chunk in range(chunks):
+            lo = total - (chunk + 1) * unit
+            copy = remote(
+                source.at[lo : lo + unit], landing.at[lo : lo + unit], send_sem.at[used], recv_sem.at[used], *sibling
+            )
+            self.arrivals["core", chunk] = (copy, landing, lo, unit)
+            used += 1
+        for step, (into, partner) in enumerate(zip(landings, partners, strict=True)):
+            size = total >> (step + 1)
+            piece = min(unit, size)
+            for chunk in range(size // piece):
+                lo = size - (chunk + 1) * piece
+                copy = remote(
+                    keep.at[size + lo : size + lo + piece], into.at[lo : lo + piece], send_sem.at[used],
+                    recv_sem.at[used], *partner,
+                )
+                self.arrivals[step, chunk] = (copy, into, lo, piece)
+                self.sends[step, chunk] = copy
+                self.needs[step, chunk] = {
+                    (source_step, block)
+                    for block in range(size + lo, size + lo + piece)
+                    for source_step in ("core", *range(step))
+                }
+                used += 1
+        self.done = set()
+
+    def start(self):
+        for key, (copy, *_) in self.arrivals.items():
+            if key[0] == "core":
+                copy.start()
+
+    def take(self, *key):
+        copy, into, lo, count = self.arrivals[key]
+        copy.wait_recv()
+
+        def add(block, carry):
+            self.keep[block] = self.keep[block] + into[block]
+            return carry
+
+        lax.fori_loop(lo, lo + count, add, 0)
+        for block in range(lo, lo + count):
+            self.done.add((key[0], block))
+        for name in list(self.sends):
+            if self.needs[name] <= self.done:
+                self.sends.pop(name).start()
+
+    def finish(self):
+        for copy, *_ in self.arrivals.values():
+            copy.wait_send()
+
+
+def backward_kernel(
+    pages,
+    length_ref, query_ref, mixture_back_ref, columns_ref, rows_ref, query_rows_ref, tokens_ref, patches_ref, taps_ref,
+    middle_sums_ref, bundle_any, weights_any, key_any, value_any, hidden_any, first_back_any, query_weight_any,
+    key_weight_any, value_weight_any,
+    tokens_back_ref, patches_back_ref, early_ref, late_ref, sums_ref,
+    keep, landing, landings, late, late_landing, late_landings, weights_buf, key_buf, value_buf, outgoing, from_sib,
+    from_far, matrices, hidden, flipped, total_back, query_back, key_back, value_back, back, steps, mask_ref, hot_ref,
+    query_hot_ref, band_ref, table_acc, band_acc, table_out, text_rim, patch_rim, sums, sums_in,
+    load_sem, page_sem, early_send, early_recv, late_send, late_recv, sib_send, sib_recv, far_send, far_recv, rim_send,
+    rim_recv, sum_send, sum_recv,
+):
+    page_at, bits, seq, across, core = places_of(pages)
+    levels = len(bits)
+    count, span, width = tokens_ref.shape
+    patch_span = patches_ref.shape[1]
+    row_count = span + patch_span
+    total_rows = count * row_count
+    key_pad = key_buf.shape[1]
+    text_slots = 4 * span
+    pairs = weights_buf.shape[1]
+    heads = 2 * pairs
+    f32, bf16 = jnp.float32, jnp.bfloat16
+
+    sibling = (page_at, sibling_of(seq))
+    opposite = (page_at, across_of(seq))
+    diagonal = (page_at, sibling_of(across_of(seq)))
+    flips = [(1 - 2 * bit) * 2**level for level, bit in enumerate(bits)]
+    on_page = [(page_at + flip, seq) for flip in flips]
+    either = lambda first, second: first + core * (second - first)
+    early_partners = [
+        (page_at + either(flips[1], flips[0]), seq),
+        (page_at + either(flips[0], flips[1]), seq),
+        opposite,
+    ] + on_page[2:]
+    late_partners = [
+        (page_at + core * flips[0], seq + (1 - core) * (2 - 4 * across)),
+        (page_at + (1 - core) * flips[0], seq + core * (2 - 4 * across)),
+    ] + on_page[1:]
+    barrier = pltpu.get_barrier_semaphore()
+    everyone = [sibling, opposite, diagonal] + on_page
+    for peer in everyone:
+        pl.semaphore_signal(barrier, inc=1, device_id=peer, device_id_type=MESH)
+
+    keep_load = pltpu.make_async_copy(bundle_any.at[0], keep, load_sem.at[0])
+    later_loads = [
+        pltpu.make_async_copy(source, target, load_sem.at[1 + index])
+        for index, (source, target) in enumerate(
             (
-                ((hidden, query_back, None), (hidden, value_back, 0)),
-                ((hidden, key_back, None), (hidden, value_back, 1)),
-            ),
-            places,
-            pages,
+                (query_weight_any, matrices.at[0]), (key_weight_any, matrices.at[1]),
+                (value_weight_any, matrices.at[2]), (hidden_any, hidden), (first_back_any, total_back),
+            )
         )
+    ]
+
+    def page_loads(page):
+        slot = page % 2
+        return [
+            pltpu.make_async_copy(source.at[page], target.at[slot], page_sem.at[index, slot])
+            for index, (source, target) in enumerate(
+                ((weights_any, weights_buf), (key_any, key_buf), (value_any, value_buf))
+            )
+        ]
+
+    for copy in page_loads(0):
+        copy.start()
+    keep_load.start()
+    for copy in later_loads:
+        copy.start()
+    pl.semaphore_wait(barrier, len(everyone))
+    early = Halving(
+        keep, bundle_any.at[1], landing, landings, early_partners, sibling, (early_send, early_recv), 8
+    )
+    late_sum = Halving(
+        late.at[0], late.at[1], late_landing, late_landings, late_partners, sibling, (late_send, late_recv), 4
+    )
+    early.start()
+
+    lane128 = lax.broadcasted_iota(jnp.int32, (row_count, 128), 1)
+    place = query_places(seq, (row_count, 128), span, patch_span, text_slots)
+    aim = place + lane128 - 32
+    blocks_on = (aim >> 4) - (place >> 4)
+    near = (lane128 < 64) & (aim >= 0) & (aim < text_slots + patch_span * 4) & (blocks_on >= -1) & (blocks_on <= 1)
+    band_ref[...] = jnp.where(near, aim, -1)
+    table_acc[...] = jnp.zeros_like(table_acc)
+    band_acc[...] = jnp.zeros_like(band_acc)
+    lane_of_row = lax.broadcasted_iota(jnp.int32, (48, row_count), 1)
+    place_of_row = jnp.where(
+        lane_of_row < span, seq * span + lane_of_row, text_slots + seq * patch_span + lane_of_row - span
+    )
+    query_hot_ref[144:192, :] = (
+        ((place_of_row >> 4) == lax.broadcasted_iota(jnp.int32, (48, row_count), 0)).astype(f32).astype(bf16)
+    )
+    pair_width = 128
+
+    def start_page(page):
+        slot = page % 2
+        for copy in page_loads(page):
+            copy.wait()
+
+        @pl.when(page < count - 1)
+        def _():
+            for copy in page_loads(page + 1):
+                copy.start()
+
+        bin_at = lax.broadcasted_iota(jnp.int32, (128, key_pad), 0) - 1
+        key_block = lax.broadcasted_iota(jnp.int32, (128, key_pad), 1) >> 4
+        half_bin = lax.broadcasted_iota(jnp.int32, (72, row_count), 0)
+        for side in range(2):
+            key_row = rows_ref[page, side : side + 1, :]
+            query_column = columns_ref[page, :, 128 * side : 128 * side + 1]
+            mask_ref[:, side * key_pad : (side + 1) * key_pad] = (
+                ((key_row & 15) < (query_column & 15)).astype(f32).astype(bf16)
+            )
+            key_bin = key_row >> 4
+            plain = jnp.where(bin_at < 64, (key_bin == bin_at).astype(f32), 0.0)
+            lower = jnp.where(bin_at < 64, (key_bin - 1 == bin_at).astype(f32), 0.0)
+            mine = slice(128 * side, 128 * (side + 1))
+            other = slice(128 * (1 - side), 128 * (2 - side))
+            change = lower - plain
+            if side == 0:
+                plain = jnp.where(bin_at - 71 == key_block, 1.0, plain)
+            hot_ref[mine, 0:key_pad] = plain.astype(bf16)
+            hot_ref[mine, (1 + side) * key_pad : (2 + side) * key_pad] = change.astype(bf16)
+            hot_ref[other, (1 + side) * key_pad : (2 + side) * key_pad] = jnp.zeros((128, key_pad), bf16)
+            query_bin = query_rows_ref[page, side : side + 1, 0:row_count] >> 4
+            query_hot_ref[72 * side : 72 * (side + 1), :] = (71 - query_bin == half_bin).astype(f32).astype(bf16)
+
+    def attend(page, pair):
+        slot = page % 2
+        at = pl.ds(pl.multiple_of(pair * pair_width, pair_width), pair_width)
+        own_rows = pl.ds(pl.multiple_of(page * row_count, 16), row_count)
+        both_query = pair_masked(query_ref[own_rows, at])
+        both_back = pair_masked(mixture_back_ref[own_rows, at])
+        back[...] = dot_nt(both_back, value_buf[slot, :, at])
+        for start in range(0, 2 * row_count, CHUNK):
+            there = slice(start, start + CHUNK)
+            here = slice(start % row_count, start % row_count + CHUNK)
+            parts, total = [], None
+            for block_at in range(0, key_pad, 128):
+                lane = slice(block_at, block_at + 128)
+                part = weights_buf[slot, pair, there, lane].astype(f32)
+                product = part * back[there, lane]
+                total = product if total is None else total + product
+                parts.append(part)
+            mean = jnp.sum(total, axis=1, keepdims=True)
+            for index, part in enumerate(parts):
+                lane = slice(128 * index, 128 * (index + 1))
+                step = (part * (back[there, lane] - mean)).astype(bf16)
+                steps[there, lane] = step
+                steps[there, key_pad + 128 * index : key_pad + 128 * (index + 1)] = step * mask_ref[here, lane]
+                steps[there, 2 * key_pad + 128 * index : 2 * key_pad + 128 * (index + 1)] = (
+                    step * mask_ref[here, key_pad + 128 * index : key_pad + 128 * (index + 1)]
+                )
+        query_back[own_rows, at] = (
+            pair_merged(dot_nn(steps[:, 0:key_pad], key_buf[slot, :, at])) * 0.125
+        ).astype(bf16)
+        for kind, value in enumerate(
+            (dot_tn(steps[:, 0:key_pad], both_query), dot_tn(weights_buf[slot, pair], both_back))
+        ):
+            value = value.astype(bf16)
+            for where in range(4):
+                place_at = apart(where % 2, core) * 2 + apart(where // 2, across)
+                outgoing[page, place_at, kind, 0:span, at] = value[where * span : (where + 1) * span]
+                outgoing[page, place_at, kind, span:row_count, at] = value[
+                    text_slots + where * patch_span : text_slots + (where + 1) * patch_span
+                ]
+        bins = dot_nt(steps[...], hot_ref[...]).astype(bf16)
+        for side in range(2):
+            head = 2 * pair + side
+            base = side * row_count
+            both = dot_nn(query_hot_ref[...], bins[base : base + row_count])
+            table_acc[head, 0:72, :] += both[0:72, 0:128]
+            table_acc[head, 72:144, :] += both[72:144, 128:256]
+            table_acc[head, 144:192, :] += both[144:192, 0:128]
+            for first, rows_here, block, into in bands():
+                source = steps[
+                    base + first : base + first + rows_here, pl.ds(pl.multiple_of(block * 128, 128), 128)
+                ]
+                band_acc[head, into : into + rows_here, :] += source.astype(f32)
+
+    def bands():
+        before = seq - (seq + 3) // 4
+        return (
+            (0, span, seq, 0),
+            (0, 32, before, span),
+            (span - 32, 32, seq + 1, span + 32),
+            (span, patch_span, 3, span + 64),
+            (span, patch_span, 4, span + 64 + patch_span),
+        )
+
+    def sib_copy(page):
+        return remote(outgoing.at[page, 2:4], from_sib.at[page], sib_send.at[page], sib_recv.at[page], *sibling)
+
+    def far_copy(page):
+        return remote(outgoing.at[page, 1], from_far.at[page], far_send.at[page], far_recv.at[page], *opposite)
+
+    def pass_on(page):
+        sib_copy(page).wait_recv()
+        for kind in range(2):
+            outgoing[page, 1, kind] = outgoing[page, 1, kind] + from_sib[page, 1, kind]
+        far_copy(page).start()
+
+    events = {
+        1: [("core", 0), ("core", 1)], 2: [("core", 2), ("core", 3)], 4: [("core", 4), ("core", 5)],
+        6: [("core", 6), ("core", 7)], 8: [(0, 0)], 12: [(0, 1), (1, 0)], 17: [(0, 2), (1, 1)],
+    }
+
+    def step_body(turn, carry):
+        page, pair = turn // pairs, turn % pairs
+
+        @pl.when(pair == 0)
+        def _():
+            start_page(page)
+
+        for at_turn, names in events.items():
+
+            @pl.when(turn == at_turn)
+            def _(names=names, at_turn=at_turn):
+                if at_turn == min(events):
+                    keep_load.wait()
+                for name in names:
+                    early.take(*name)
+
+        @pl.when((pair == 2) & (page > 0))
+        def _():
+            pass_on(page - 1)
+
+        attend(page, pair)
+
+        @pl.when(pair == pairs - 1)
+        def _():
+            sib_copy(page).start()
+
+        return carry
+
+    lax.fori_loop(0, count * pairs, step_body, 0)
+
+    for copy in later_loads:
+        copy.wait()
+    flipped[...] = hidden[...].T
+    lanes = 384
+    rows = width // pages
+    half = rows // 2
+
+    def weight_columns(index, gradient):
+        def tile(column, carry):
+            at = pl.ds(pl.multiple_of(column * lanes, lanes), lanes)
+            result = dot_nn(flipped[...], gradient[:, at]).astype(bf16)
+            for page in range(pages):
+                far = [apart((page >> level) & 1, bit) for level, bit in enumerate(bits)]
+                slots = [slot_of_bits(order) for order in late_orders(far, apart(column, across))]
+                first = page * rows
+                if index < 2:
+                    late[core if index == 0 else 1 - core, slots[index], 0:rows, :] = result[first : first + rows]
+                else:
+                    late[core, slots[0], rows : rows + half, :] = result[first : first + half]
+                    late[1 - core, slots[1], rows : rows + half, :] = result[first + half : first + rows]
+            return carry
+
+        lax.fori_loop(0, 2, tile, 0)
+
+    def project_back(gradient, matrix):
+        def tile(column, carry):
+            at = pl.ds(pl.multiple_of(column * 256, 256), 256)
+            total_back[:, at] = total_back[:, at] + dot_nt(gradient[...], matrices[matrix, at, :])
+            return carry
+
+        lax.fori_loop(0, width // 256, tile, 0)
+
+    pass_on(count - 1)
+    weight_columns(0, query_back)
+    project_back(query_back, 0)
+    sums[0, 0:16, :] = middle_sums_ref[...]
+    sums[0, 10:11, :] = column_sum(query_back[...].astype(f32))
+
+    def head_tables(head, carry):
+        for plane in range(2):
+            table = table_acc[head, 72 * plane : 72 * (plane + 1), :]
+            lane = lax.broadcasted_iota(jnp.int32, table.shape, 1)
+            table = jnp.where(lane < 72, table, 0.0)
+            table = jnp.concatenate([table, jnp.zeros_like(table)], axis=1)
+            sheared = pltpu.roll(table, 0, 1, stride=1, stride_axis=0)
+            table_out[head, 0:1, 256 * plane : 256 * (plane + 1)] = column_sum(sheared)
+        table = table_acc[head, 144:192, :]
+        lane = lax.broadcasted_iota(jnp.int32, table.shape, 1)
+        apart_by = lane - 72 - lax.broadcasted_iota(jnp.int32, table.shape, 0)
+        in_line = (lane >= 72) & (lane < 72 + 36)
+        low_tail = jnp.sum(column_sum(jnp.where(in_line & (apart_by <= -2), table, 0.0)), axis=1, keepdims=True)
+        high_tail = jnp.sum(column_sum(jnp.where(in_line & (apart_by >= 2), table, 0.0)), axis=1, keepdims=True)
+        band = jnp.zeros((1, 128), f32)
+        for first, rows_here, block, into in bands():
+            aims = band_ref[first : first + rows_here, :]
+            taken = jnp.take_along_axis(band_acc[head, into : into + rows_here, :], aims & 127, axis=1)
+            right = (aims >> 7) == block
+            if into == span:
+                right = right & (seq > 0)
+            band = band + column_sum(jnp.where(right, taken, 0.0))
+        lane_one = lax.broadcasted_iota(jnp.int32, (1, 128), 1)
+        table_out[head, 0:1, 512:640] = (
+            band + jnp.where(lane_one == 0, low_tail, 0.0) + jnp.where(lane_one == 63, high_tail, 0.0)
+        )
+        table_out[head, 0:1, 640:768] = jnp.zeros((1, 128), f32)
+        return carry
+
+    lax.fori_loop(0, heads, head_tables, 0)
+    for head in range(heads):
+        at_row = 8 + head
+        sums[1, at_row : at_row + 1, :] = table_out[head, 0:1, :]
+    early.take(0, 3)
+
+    for page in range(count):
+        far_copy(page).wait_recv()
+        own_rows = slice(page * row_count, (page + 1) * row_count)
+        for kind, target in enumerate((key_back, value_back)):
+            target[own_rows, :] = (
+                (outgoing[page, 0, kind].astype(f32) + from_sib[page, 0, kind].astype(f32))
+                + from_far[page, kind].astype(f32)
+            ).astype(bf16)
+    weight_columns(1, key_back)
+    weight_columns(2, value_back)
+    late_sum.start()
+    project_back(key_back, 1)
+    project_back(value_back, 2)
+    sums[0, 11:12, :] = column_sum(value_back[...].astype(f32))
+    for page in range(count):
+        first = page * row_count
+        text_rim[page, 16 : 16 + span, :] = total_back[first : first + span, :].astype(bf16)
+        patch_rim[page, 16 : 16 + patch_span, :] = total_back[first + span : first + row_count, :].astype(bf16)
+    after, before = (page_at, (seq + 1) % 4), (page_at, (seq + 3) % 4)
+    rim_copies = [
+        remote(
+            source.at[:, start : start + 16], source.at[:, stop : stop + 16], rim_send.at[index], rim_recv.at[index],
+            *peer,
+        )
+        for index, (source, start, stop, peer) in enumerate(
+            (
+                (text_rim, span, 0, after), (text_rim, 16, 16 + span, before),
+                (patch_rim, 16, 0, after), (patch_rim, 16, 32, before),
+            )
+        )
+    ]
+    for copy in rim_copies:
+        copy.start()
+    for chunk in range(4):
+        late_sum.take("core", chunk)
+    early.take(2, 0)
+    for copy in rim_copies:
+        copy.wait()
+    sums[1, 0:8, :] = jnp.zeros((8, width), f32)
+    sums[1, 20:24, :] = jnp.zeros((4, width), f32)
+    sums[0, 16:24, :] = jnp.zeros((8, width), f32)
+
+    def position_tile(tile, carry):
+        at = pl.ds(pl.multiple_of(tile * 256, 256), 256)
+        text_taps = [jnp.zeros((1, 256), f32) for _ in range(7)]
+        patch_taps = [jnp.zeros((1, 256), f32) for _ in range(9)]
+        for page in range(count):
+            first = page * row_count
+            window = text_rim[page, :, at].astype(f32)
+            window_row = lax.broadcasted_iota(jnp.int32, (span + 32, 1), 0)
+            inside = ((window_row >= 16) | (seq > 0)) & ((window_row < 16 + span) | (seq < 3))
+            window = jnp.where(inside, window, 0.0)
+            live = seq * span + lax.broadcasted_iota(jnp.int32, (span, 1), 0) < length_ref[page]
+            masked = jnp.where(live, tokens_ref[page, :, at].astype(f32), 0.0)
+            total = jnp.zeros((span, 256), f32)
+            for distance in range(-3, 4):
+                shifted = window[16 - distance : 16 - distance + span]
+                if distance == 0:
+                    weight = taps_ref[1:2, at] + taps_ref[4:5, at] + taps_ref[7:8, at]
+                else:
+                    tap = 3 * (abs(distance) - 1) + (2 if distance > 0 else 0)
+                    weight = taps_ref[tap : tap + 1, at]
+                total = total + shifted * weight
+                text_taps[distance + 3] = text_taps[distance + 3] + column_sum(shifted * masked)
+            tokens_back_ref[page, :, at] = total_back[first : first + span, at] + jnp.where(live, total, 0.0)
+            window = patch_rim[page, :, at].astype(f32)
+            window_row = lax.broadcasted_iota(jnp.int32, (48, 1), 0)
+            inside = ((window_row >= 16) | (seq > 0)) & ((window_row < 32) | (seq < 3))
+            window = jnp.where(inside, window, 0.0)
+            cell = seq * patch_span + lax.broadcasted_iota(jnp.int32, (patch_span, 1), 0)
+            live = ((cell >> 3) < GRID_SIDE - 1) & ((cell & 7) < GRID_SIDE - 1)
+            masked = jnp.where(live, patches_ref[page, :, at].astype(f32), 0.0)
+            total = jnp.zeros((patch_span, 256), f32)
+            for tap in range(9):
+                distance = GRID_SIDE * (tap // 3 - 1) + tap % 3 - 1
+                shifted = window[16 - distance : 32 - distance]
+                total = total + shifted * taps_ref[9 + tap : 10 + tap, at]
+                patch_taps[tap] = patch_taps[tap] + column_sum(shifted * masked)
+            patches_back_ref[page, :, at] = total_back[first + span : first + row_count, at] + jnp.where(
+                live, total, 0.0
+            )
+        for index, value in enumerate(text_taps):
+            sums[0, 16 + index : 17 + index, at] = value
+        for index, value in enumerate(patch_taps):
+            if index == 0:
+                sums[0, 23:24, at] = value
+            else:
+                sums[1, index - 1 : index, at] = value
+        return carry
+
+    lax.fori_loop(0, width // 256, position_tile, 0)
+
+    sum_partners = [opposite] + on_page
+    sum_copies = [remote(sums.at[1 - core], sums_in.at[0], sum_send.at[0], sum_recv.at[0], *sibling)] + [
+        remote(sums.at[core], sums_in.at[1 + index], sum_send.at[1 + index], sum_recv.at[1 + index], *partner)
+        for index, partner in enumerate(sum_partners)
+    ]
+    last = remote(
+        sums.at[core], sums_in.at[2 + levels], sum_send.at[2 + levels], sum_recv.at[2 + levels], *sibling
+    )
+    sum_copies[0].start()
+
+    def sum_step(index):
+        sum_copies[index].wait()
+        sums[core] = sums[core] + sums_in[index]
+        (sum_copies + [last])[index + 1].start()
+
+    sum_step(0)
+    late_sum.take(0, 0)
+    sum_step(1)
+    late_sum.take(0, 1)
+    late_sum.take(1, 0)
+    sum_step(2)
+    for step in range(3, levels + 1):
+        early.take(step, 0)
+    for step in range(2, levels + 1):
+        late_sum.take(step, 0)
+        if step + 1 <= levels + 1:
+            sum_step(step + 1)
+    last.wait()
+    sums_ref[core] = sums[core]
+    sums_ref[1 - core] = sums_in[2 + levels]
+    early_ref[...] = keep[0]
+    late_ref[...] = late[0, 0]
+    early.finish()
+    late_sum.finish()
+    for page in range(count):
+        sib_copy(page).wait_send()
+        far_copy(page).wait_send()
+
+
+def backward(pages, lengths, local_values, far_values, tokens, patches):
+    count, span, width = tokens.shape
+    patch_span = patches.shape[1]
+    row_count = span + patch_span
+    total_rows = count * row_count
+    bundle, weights, keys = far_values[0], far_values[1], far_values[2]
+    pairs, key_pad = weights.shape[1], keys.shape[1]
+    blocks, early_rows, lanes = bundle.shape[1:]
+    late_rows = 3 * width // (2 * pages)
+    levels = pages.bit_length() - 1
+    bf16, f32, i32 = jnp.bfloat16, jnp.float32, jnp.int32
+    dma = pltpu.SemaphoreType.DMA
+
+    def landings(rows):
+        return [VMEM((blocks >> (step + 1), rows, lanes), bf16) for step in range(levels + 1)]
+
+    early_count = 8 + 4 + 2 + (levels - 1)
+    late_count = 4 + 2 + levels
     return pl.pallas_call(
-        functools.partial(attention_weight_kernel, pages),
-        out_shape=jax.ShapeDtypeStruct((2, 2 * pages, 3 * width // (2 * pages), 384), jnp.bfloat16),
-        in_specs=[pl.BlockSpec(memory_space=pltpu.SMEM)] + in_vmem(4),
-        out_specs=in_vmem(1)[0],
-        scratch_shapes=[pltpu.VMEM(hidden.shape[::-1], jnp.bfloat16)],
-        compiler_params=pltpu.CompilerParams(vmem_limit_bytes=KERNEL_VMEM),
-        cost_estimate=pl.CostEstimate(flops=1_600_000_000, bytes_accessed=10_000_000, transcendentals=0),
-        name="attention_weights",
-    )(places, *operands)
+        functools.partial(backward_kernel, pages),
+        out_shape=(
+            jax.ShapeDtypeStruct(tokens.shape, f32),
+            jax.ShapeDtypeStruct(patches.shape, f32),
+            jax.ShapeDtypeStruct((early_rows, lanes), bf16),
+            jax.ShapeDtypeStruct((late_rows, lanes), bf16),
+            jax.ShapeDtypeStruct((2, 24, width), f32),
+        ),
+        in_specs=[pl.BlockSpec(memory_space=pltpu.SMEM)]
+        + in_vmem(len(local_values))
+        + [pl.BlockSpec(memory_space=pl.ANY)] * len(far_values),
+        out_specs=tuple(in_vmem(5)),
+        scratch_shapes=[
+            VMEM((blocks, early_rows, lanes), bf16),
+            VMEM((blocks, early_rows, lanes), bf16),
+            landings(early_rows),
+            VMEM((2, blocks, late_rows, lanes), bf16),
+            VMEM((blocks, late_rows, lanes), bf16),
+            landings(late_rows),
+            VMEM((2, pairs, 2 * row_count, key_pad), bf16),
+            VMEM((2, key_pad, width), bf16),
+            VMEM((2, key_pad, width), bf16),
+            VMEM((count, 4, 2, row_count, width), bf16),
+            VMEM((count, 2, 2, row_count, width), bf16),
+            VMEM((count, 2, row_count, width), bf16),
+            VMEM((3, width, width), bf16),
+            VMEM((total_rows, width), bf16),
+            VMEM((width, total_rows), bf16),
+            VMEM((total_rows, width), f32),
+            VMEM((total_rows, width), bf16),
+            VMEM((total_rows, width), bf16),
+            VMEM((total_rows, width), bf16),
+            VMEM((2 * row_count, key_pad), f32),
+            VMEM((2 * row_count, 3 * key_pad), bf16),
+            VMEM((row_count, 2 * key_pad), bf16),
+            VMEM((256, 3 * key_pad), bf16),
+            VMEM((192, row_count), bf16),
+            VMEM((row_count, 128), i32),
+            VMEM((2 * pairs, 192, 128), f32),
+            VMEM((2 * pairs, span + 64 + 2 * patch_span, 128), f32),
+            VMEM((2 * pairs, 8, width), f32),
+            VMEM((count, span + 32, width), bf16),
+            VMEM((count, patch_span + 32, width), bf16),
+            VMEM((2, 24, width), f32),
+            VMEM((3 + levels, 24, width), f32),
+            dma((6,)), dma((3, 2)),
+            dma((early_count,)), dma((early_count,)), dma((late_count,)), dma((late_count,)),
+            dma((count,)), dma((count,)), dma((count,)), dma((count,)),
+            dma((4,)), dma((4,)), dma((3 + levels,)), dma((3 + levels,)),
+        ],
+        compiler_params=pltpu.CompilerParams(
+            collective_id=1, has_side_effects=True, vmem_limit_bytes=62 * 1024 * 1024
+        ),
+        cost_estimate=pl.CostEstimate(flops=12_000_000_000, bytes_accessed=40_000_000, transcendentals=0),
+        name="backward",
+    )(lengths, *local_values, *far_values)
 
 
 def exchange(value, pages, step):
@@ -1013,6 +1558,18 @@
         [jnp.where(first, kept_tail, got[wide_rows:]), jnp.where(first, got[wide_rows:], kept_tail)], axis=0
     )
     return [value.astype(jnp.float32) for value in (one, two, three)]
+
+
+def clipped(sums, centre, bins):
+    first, last = centre + 1 - bins // 2, centre - 1 + bins // 2
+    return jnp.concatenate(
+        [
+            jnp.sum(sums[..., :first], axis=-1, keepdims=True),
+            sums[..., first:last],
+            jnp.sum(sums[..., last:], axis=-1, keepdims=True),
+        ],
+        axis=-1,
+    )
 
 
 def grid_live(cells):
@@ -1131,6 +1688,61 @@
         places, hidden, mixture_low, cotangent, patch_cotangent,
         (out_weight, up_weight, down_weight), vectors, pages,
     )
+    if in_tiles(model_width, pages):
+        tokens_gradient, patches_gradient, early_state, late_state, sums = backward(
+            pages,
+            page_length,
+            (
+                queries, delta_mixture, columns, key_rows, query_rows, tokens, patches, taps, middle_sums,
+            ),
+            (
+                feedforward_bundle, weights, keys, values, hidden_low, delta_first, query_weight, key_weight,
+                value_weight,
+            ),
+            tokens,
+            patches,
+        )
+        query_part, key_part, value_part = bundle_parts(late_state, model_width // pages, places[1])
+        up_part, down_part, out_part = bundle_parts(early_state, up_weight.shape[1] // pages, places[1])
+        front, late_sums = sums[0], sums[1]
+        text_columns = front[16:23]
+        centre = text_columns[3]
+        head_sums = late_sums[8 : 8 + head_count]
+        plane_sums = head_sums[:, :512].reshape(head_count, 2, 256).transpose(1, 0, 2)
+        plane_sums = clipped(plane_sums, 72, plane_bins)
+        return (
+            output,
+            patch_output,
+            tokens_gradient,
+            patches_gradient,
+            query_part,
+            key_part,
+            value_part,
+            out_part,
+            up_part.reshape(model_width // pages, -1),
+            down_part,
+            jnp.stack(
+                [
+                    text_columns[2], centre, text_columns[4],
+                    text_columns[1], centre, text_columns[5],
+                    text_columns[0], centre, text_columns[6],
+                ],
+                axis=1,
+            ),
+            jnp.concatenate([front[23:24], late_sums[0:8]], axis=0).T,
+            front[10],
+            front[11],
+            front[OUT_BIAS],
+            front[UP_BIAS : UP_BIAS + 4].reshape(-1),
+            front[DOWN_BIAS],
+            front[FIRST_GAIN],
+            front[FIRST_SHIFT],
+            front[SECOND_GAIN],
+            front[SECOND_SHIFT],
+            clipped(head_sums[:, 512:640], 32, line_bins),
+            plane_sums[0],
+            plane_sums[1],
+        )
     delta_first = delta_first.reshape(page_count, row_count, model_width)
     delta_mixture = delta_mixture.reshape(page_count, row_count, model_width)
     early_state = added(feedforward_bundle[0], swap(feedforward_bundle[1], "seq", 1))
@@ -1161,17 +1773,6 @@
     delta_queries = jnp.stack(delta_query_pages)
     delta_keys = jnp.stack(delta_key_pages)
     delta_values = jnp.stack(delta_value_pages)
-    def clipped(sums, centre, bins):
-        first, last = centre + 1 - bins // 2, centre - 1 + bins // 2
-        return jnp.concatenate(
-            [
-                jnp.sum(sums[..., :first], axis=-1, keepdims=True),
-                sums[..., first:last],
-                jnp.sum(sums[..., last:], axis=-1, keepdims=True),
-            ],
-            axis=-1,
-        )
-
     delta_plane = clipped(delta_plane, 72, plane_bins)
     delta_line = clipped(delta_line, 32, line_bins)
     delta_across, delta_upward = delta_plane[0], delta_plane[1]
@@ -1232,8 +1833,14 @@
     patches_gradient = delta_hidden[:, span_size:] + delta_patch_masked * patch_factor.astype(
         jnp.float32
     )
-    tail_bundle = attention_bundle(
-        places, [flat(value) for value in (hidden_low, delta_queries, delta_keys, delta_values)], pages
+    operands = [flat(value) for value in (hidden_low, delta_queries, delta_keys, delta_values)]
+    tail_bundle = indexed_bundle(
+        (
+            ((operands[0], operands[1], None), (operands[0], operands[3], 0)),
+            ((operands[0], operands[2], None), (operands[0], operands[3], 1)),
+        ),
+        places,
+        pages,
     )
     tail_state = added(tail_bundle[0], swap(tail_bundle[1], "seq", 1))
     query_part, key_part, value_part = bundle_parts(

time: 352 us -> 257 us (0.73)
  Pallas kernels: 136 us -> 220 us
  waiting for transfers between devices: 74.5 us -> 0.01 us
  starting transfers between devices: 40 us -> 0.64 us
  local copies, waits for them, and re-layouts: 63.8 us -> 25.5 us
  other arithmetic: 31.7 us -> 8.6 us
    pallas_call x4 -> x1, Pallas kernels: 39.2 us -> 123 us  [backward(): pl.pallas_call(functools.partial(backward_kernel, pages), out_shape=(jax....]
    ppermute x15 -> x2, waiting for transfers between devices: 39.6 us -> 0.01 us  [swap(): return lax.ppermute(value, axis, [(i, i ^ bit) for i in range(count)])]
    ppermute x16 -> x0, waiting for transfers between devices: 34.9 us -> none  [the longest x8 34.9 us: exchange(): return lax.ppermute(value, ('page', 'seq'), moves)]
    ppermute x16 -> x0, starting transfers between devices: 27.1 us -> none  [the longest x4 11.5 us: with_halo(): lax.ppermute(tail, axis, [(i, (i + 1) % count) for i in range(ends)])]
    slice x33 -> x5, local copies, waits for them, and re-layouts: 15.6 us -> 0.69 us  [the longest x1 0.68 us: shards(): front[SECOND_SHIFT]]
    convert_element_type x18 -> x0, other arithmetic: 12.8 us -> none  [the longest x10 11.8 us: added(): (kept.astype(jnp.float32) + got.astype(jnp.float32)).astype(jnp.bfloat16)]
    ppermute x15 -> x2, starting transfers between devices: 12.8 us -> 0.64 us  [swap(): return lax.ppermute(value, axis, [(i, i ^ bit) for i in range(count)])]
    squeeze x8 -> x1, local copies, waits for them, and re-layouts: 11.9 us -> 0.62 us  [shards(): plane_sums[1]]
  transfers between devices with their start and end apart: 31 -> 2, of which waited for: 14 -> 0; matrix products, arithmetic and copies ran while one was open for 18% -> 4% of each run, Pallas kernels for 11% -> 0%
where the time goes in v1:
time: 257 us; the launch traced here: 256 us
  Pallas kernels  220 us (86%)
  local copies, waits for them, and re-layouts  25.5 us (10%)
  other arithmetic  8.6 us (3%)
    pallas_call x1, Pallas kernels, backward(): pl.pallas_call(functools.partial(backward_kernel, pages), out_shape=(jax....  123 us
    pallas_call x1, Pallas kernels, forward(): pl.pallas_call(functools.partial(forward_kernel, pages), out_shape=(jax.S...  50.7 us
    pallas_call x1, Pallas kernels, middle(): pl.pallas_call(functools.partial(middle_kernel, pages, direct), out_shape...  46 us
    unnamed x40, local copies, waits for them, and re-layouts  13 us
    another operation x8, local copies, waits for them, and re-layouts, shards(): jnp.stack([query_bias, value_bias, out_bias, down_bias, attention_gain, a...  5.48 us
  transfers between devices with their start and end apart: 2, of which 0 were waited for; matrix products, arithmetic and copies ran while one was open for 4% of the time, Pallas kernels for 0%

profile of v1, /device:TPU:0, one launch (start us, length us, event | category | flops | bytes accessed | tf_op | source)
XLA Modules:
  0.0 255.7 jit_solution(5583704438268617454)
XLA Ops:
  0.7 0.7 stack.47
  1.4 0.7 stack.48
  2.0 0.7 stack.49
  2.7 0.7 stack.50
  3.4 0.7 stack.51
  4.1 0.7 stack.52
  4.8 0.7 stack.53
  5.5 0.7 stack.54
  6.2 0.7 reshape.108
  6.9 0.7 copy.59.box_ref
  7.7 0.8 maximum_bitcast_fusion.1
  9.2 0.8 maximum_convert_fusion.2.table_ref
  10.0 1.3 copy-done.2
  11.2 1.3 copy-done.3
  12.5 1.1 copy-done.4
  13.6 0.9 copy-done.5
  15.1 50.7 %forward.1 = (f32[432,768]{1,0:T(8,128)}, bf16[432,768]{1,0:T(8,128)(2,1)S(1)}, bf16[432,768]{1,0:T(8,128)(2,1)S(1)}, bf16[3,640,768]{2,1,0:T(8,128)(2,1)}, bf16...) custom-call(s32[3]{0:T(128)S(1)} %copy-done.6, ...), custom_call_target="tpu_custom_call" | custom-call | flops 8000000000 | bytes 25000000 | tf_op jit(solution)/shard_map/forward/pallas_call | solution.py:431
  65.9 0.9 copy-done.7
  66.7 0.8 copy-done.8
  67.6 0.8 copy-done.9
  68.3 0.8 copy-done.10
  70.4 46.0 %middle.1 = (f32[3,128,768]{2,1,0:T(8,128)}, f32[3,16,768]{2,1,0:T(8,128)}, f32[432,768]{1,0:T(8,128)}, bf16[432,768]{1,0:T(8,128)(2,1)}, f32[16,768]{1,0:T(8,128)}, /*index=5*/bf16[2,16,432,384]{3,2,1,0:T(8,128)(2,1)}) custom-call(s32[4]{0:T(128)} %pad_add_fusion.scalar_ref, f32[432,768]{1,0:T(8,128)} %get-tuple-element.45.hidden_ref, ...), custom_call_target="tpu_custom_call" | custom-call | flops 14000000000 | bytes 30000000 | tf_op jit(solution)/shard_map/middle/pallas_call | solution.py:862
  116.4 123.3 %backward.1 = (f32[3,128,768]{2,1,0:T(8,128)}, f32[3,16,768]{2,1,0:T(8,128)}, bf16[432,384]{1,0:T(8,128)(2,1)}, bf16[144,384]{1,0:T(8,128)(2,1)}, f32[2,24,768]{2,1,0:T(8,128)}) custom-call(s32[3]{0:T(128)} %length_ref.3, bf16[432,768]{1,0:T(8,128)(2,1)} %copy-done.8, bf16[432,768]{1,0:T(8,128)(2,1)} %get-tuple-element.50.mixture_back_ref, ...), custom_call_target="tpu_custom_call" | custom-call | flops 12000000000 | bytes 40000000 | tf_op jit(solution)/shard_map/backward/pallas_call | solution.py:1456
  239.7 0.9 broadcast_select_fusion.8
  240.6 1.0 broadcast_select_fusion
  242.0 0.9 broadcast_select_fusion.3
  242.9 1.0 fusion
  249.3 1.3 stack.55
  250.6 0.7 select_convert_fusion.2
  251.5 0.9 copy.67
  252.4 0.9 reshape.116
  254.0 1.0 copy.76
  (72 shorter events, 10.0 us)
Async XLA Ops:
  7.6 58.2 %copy-start.1 = (f32[12,768]{1,0:T(8,128)}, f32[12,768]{1,0:T(8,128)S(1)}, u32[]{:S(2)}) copy-start(f32[12,768]{1,0:T(8,128)S(1)} %convert_element_type.25.vector_ref) | copy-start | bytes 110596
  8.5 57.4 %copy-start = (f32[24,768]{1,0:T(8,128)}, f32[24,768]{1,0:T(8,128)S(1)}, u32[]{:S(2)}) copy-start(f32[24,768]{1,0:T(8,128)S(1)} %pad_convert_fusion.taps_ref) | copy-start | bytes 221188
  10.0 1.3 copy-start.2
  11.2 1.3 copy-start.3
  12.5 1.1 copy-start.4
  13.6 0.9 copy-start.5
  14.4 0.7 copy-start.6
  65.8 0.9 copy-start.7
  66.7 0.8 copy-start.8
  67.6 0.8 copy-start.9
  68.3 0.8 copy-start.10
  69.2 0.6 copy-start.11
  69.8 0.6 copy-start.12
  239.7 4.5 %copy-start.13 = (bf16[432,384]{1,0:T(8,128)(2,1)S(1)}, bf16[432,384]{1,0:T(8,128)(2,1)}, u32[]{:S(2)}) copy-start(bf16[432,384]{1,0:T(8,128)(2,1)} %get-tuple-element.64) | copy-start | bytes 995332
  240.6 4.0 %copy-start.17 = (f32[2,24,768]{2,1,0:T(8,128)S(1)}, f32[2,24,768]{2,1,0:T(8,128)}, u32[]{:S(2)}) copy-start(f32[2,24,768]{2,1,0:T(8,128)} %get-tuple-element.65) | copy-start | bytes 442372
  241.6 9.0 %collective-permute-start = (bf16[144,192]{1,0:T(8,128)(2,1)S(1)}, bf16[144,192]{1,0:T(8,128)(2,1)S(1)}, u32[]{:S(2)}, u32[]{:S(2)}) collective-permute-start(bf16[144,192]{1,0:T(8,128)(2,1)S(1)} %pad_maximum_fusion.1), channel_id=1, source_target_pairs={{0,1},{1,0},{2,3},{3,2},{4,5},{5,4},{6,7},{7,6},{8,9},{9,8},{10,11... | collective-permute-start | bytes 165896 | tf_op jit(solution)/shard_map/ppermute | solution.py:82
  244.2 6.3 %copy-start.15 = (bf16[144,384]{1,0:T(8,128)(2,1)S(1)}, bf16[144,384]{1,0:T(8,128)(2,1)}, u32[]{:S(2)}) copy-start(bf16[144,384]{1,0:T(8,128)(2,1)} %get-tuple-element.63) | copy-start | bytes 331780
  244.3 7.1 %collective-permute-start.1 = (bf16[432,192]{1,0:T(8,128)(2,1)S(1)}, bf16[432,192]{1,0:T(8,128)(2,1)S(1)}, u32[]{:S(2)}, u32[]{:S(2)}) collective-permute-start(bf16[432,192]{1,0:T(8,128)(2,1)S(1)} %pad_maximum_fusion), channel_id=1, source_target_pairs={{0,1},{1,0},{2,3},{3,2},{4,5},{5,4},{6,7},{7,6},{8,9},{9,8},{10,11... | collective-permute-start | bytes 497672 | tf_op jit(solution)/shard_map/ppermute | solution.py:82
  251.4 2.6 %copy-start.14 = (f32[3,128,768]{2,1,0:T(8,128)S(1)}, f32[3,128,768]{2,1,0:T(8,128)}, u32[]{:S(2)}) copy-start(f32[3,128,768]{2,1,0:T(8,128)} %get-tuple-element.169) | copy-start | bytes 3538948
  253.2 1.8 copy-start.16

commit v2 on v1

--- a/solution.py
+++ b/solution.py
@@ -178,20 +178,41 @@
 
 def forward_kernel(
     pages,
-    length_ref, tokens_ref, patches_ref, box_ref, taps_ref, query_weight_ref, key_weight_ref, value_weight_ref,
-    vector_ref, table_ref,
-    hidden_ref, hidden_low_ref, query_ref, key_ref, value_ref, mixture_ref, weights_ref, columns_ref, rows_ref,
-    query_rows_ref,
-    arrived, text, grid, low, scores, across_ref, upward_ref, live_ref, line_ref, packed_ref,
-    send_sem, recv_sem,
+    staging, length_ref, box_ref, taps_ref, vector_ref, table_ref, tokens_any, patches_any, query_weight_any, key_weight_any,
+    value_weight_any,
+    hidden_ref, hidden_low_ref, query_ref, mixture_ref, columns_ref, rows_ref, query_rows_ref, key_any, value_any,
+    weights_any,
+    own, matrices, key_ref, value_ref, weights_ref, arrived, text, grid, low, scores, across_ref, upward_ref,
+    live_ref, line_ref, packed_ref,
+    load_sem, store_sem, send_sem, recv_sem,
 ):
     page_at, _, seq, _, _ = places_of(pages)
-    count, span, width = tokens_ref.shape
-    patch_span = patches_ref.shape[1]
+    count, span, width = tokens_any.shape
+    patch_span = patches_any.shape[1]
     row_count = span + patch_span
     key_pad = key_ref.shape[1]
     text_slots = 4 * span
     rim = 8
+    loads = [
+        pltpu.make_async_copy(source, target, load_sem.at[index])
+        for index, (source, target) in enumerate(
+            (
+                (tokens_any, own.at[:, 0:span]), (patches_any, own.at[:, span:row_count]),
+                (key_weight_any, matrices.at[1]), (value_weight_any, matrices.at[2]), (query_weight_any, matrices.at[0]),
+            )
+        )
+    ]
+    for copy in loads:
+        copy.start()
+
+    def stores(page):
+        return [
+            pltpu.make_async_copy(source.at[page], target.at[page], store_sem.at[index, page])
+            for index, (source, target) in enumerate(
+                ((key_ref, key_any), (value_ref, value_any), (weights_ref, weights_any))
+            )
+        ]
+
     pairs = weights_ref.shape[1]
     peers = (sibling_of(seq), across_of(seq))
     barrier = pltpu.get_barrier_semaphore()
@@ -202,11 +223,11 @@
     def first_copies(page, side):
         return (
             remote(
-                tokens_ref.at[page], arrived.at[side, page, 0:span], send_sem.at[2 * side, page],
+                tokens_any.at[page], arrived.at[side, page, 0:span], send_sem.at[2 * side, page],
                 recv_sem.at[2 * side, page], page_at, peers[side],
             ),
             remote(
-                patches_ref.at[page], arrived.at[side, page, span:row_count], send_sem.at[2 * side + 1, page],
+                patches_any.at[page], arrived.at[side, page, span:row_count], send_sem.at[2 * side + 1, page],
                 recv_sem.at[2 * side + 1, page], page_at, peers[side],
             ),
         )
@@ -221,6 +242,8 @@
             for copy in first_copies(page, side):
                 copy.start()
 
+    for copy in staging:
+        copy.wait()
     steps = jnp.floor(table_ref[...].astype(jnp.float32) * FIXED + 0.5).astype(jnp.int32)
     for pair in range(pairs):
         words = (steps[2 * pair : 2 * pair + 1] + 8192) + steps[2 * pair + 1 : 2 * pair + 2] * 65536
@@ -248,6 +271,8 @@
     for copy in first_copies(0, 1):
         copy.wait_recv()
     onward_copy(0).start()
+    for copy in loads:
+        copy.wait()
 
     def page_step(page, carry):
         length = length_ref[page]
@@ -264,10 +289,12 @@
             column_patch = 146 * ((row_cell % GRID_SIDE) if plane == 0 else (row_cell // GRID_SIDE)) + 73
             rows_ref[page, plane : plane + 1, 0:text_slots] = box
             rows_ref[page, plane : plane + 1, text_slots:key_pad] = patch
-            own = rows_ref[page, plane : plane + 1, pl.ds(pl.multiple_of(seq * span, 128), span)]
-            query_rows_ref[page, plane : plane + 1, 0:span] = own
+            own_box = rows_ref[page, plane : plane + 1, pl.ds(pl.multiple_of(seq * span, 128), span)]
+            query_rows_ref[page, plane : plane + 1, 0:span] = own_box
             query_rows_ref[page, plane : plane + 1, span:256] = own_patch
-            columns_ref[page, 0:span, plane * 128 : (plane + 1) * 128] = jnp.broadcast_to(column_of(own), (span, 128))
+            columns_ref[page, 0:span, plane * 128 : (plane + 1) * 128] = jnp.broadcast_to(
+                column_of(own_box), (span, 128)
+            )
             columns_ref[page, span:row_count, plane * 128 : (plane + 1) * 128] = jnp.broadcast_to(
                 column_patch, (patch_span, 128)
             )
@@ -288,8 +315,8 @@
             if step:
                 return arrived[step - 1, page, start:stop, at].astype(jnp.float32)
             if start:
-                return patches_ref[page, :, at].astype(jnp.float32)
-            return tokens_ref[page, :, at].astype(jnp.float32)
+                return own[page, span:row_count, at].astype(jnp.float32)
+            return own[page, 0:span, at].astype(jnp.float32)
 
         def slot_of(step):
             return (seq, peers[0], peers[1], sibling_of(peers[1]))[step]
@@ -342,12 +369,12 @@
 
         def project(tile, carry):
             at = pl.ds(pl.multiple_of(tile * lanes, lanes), lanes)
-            key_ref[page, :, at] = dot_nn(low[...], key_weight_ref[:, at]).astype(jnp.bfloat16)
-            value_ref[page, :, at] = (dot_nn(low[...], value_weight_ref[:, at]) + vector_ref[1:2, at]).astype(
+            key_ref[page, :, at] = dot_nn(low[...], matrices[1, :, at]).astype(jnp.bfloat16)
+            value_ref[page, :, at] = (dot_nn(low[...], matrices[2, :, at]) + vector_ref[1:2, at]).astype(
                 jnp.bfloat16
             )
             query_ref[own_rows, at] = (
-                (dot_nn(hidden_low_ref[own_rows, :], query_weight_ref[:, at]) + vector_ref[0:1, at])
+                (dot_nn(hidden_low_ref[own_rows, :], matrices[0, :, at]) + vector_ref[0:1, at])
                 .astype(jnp.bfloat16)
                 * jnp.bfloat16(0.125)
             )
@@ -400,6 +427,8 @@
             return carry
 
         lax.fori_loop(0, pairs, attend, 0)
+        for copy in stores(page):
+            copy.start()
         return carry
 
     lax.fori_loop(0, count, page_step, 0)
@@ -408,14 +437,44 @@
             for copy in first_copies(page, side):
                 copy.wait_send()
         onward_copy(page).wait_send()
+        for copy in stores(page):
+            copy.wait()
 
 
 VMEM = pltpu.VMEM
-KERNEL_VMEM = 48 * 1024 * 1024
+KERNEL_VMEM = 62 * 1024 * 1024
 
 
 def in_vmem(count):
     return [pl.BlockSpec(memory_space=VMEM)] * count
+
+
+def staged(kernel, first, count):
+    def run(*refs):
+        *refs, semaphore = refs
+        refs, buffers = list(refs[:-count]), refs[-count:]
+        copies = [
+            pltpu.make_async_copy(refs[first + index], buffers[index], semaphore.at[index]) for index in range(count)
+        ]
+        for copy in copies:
+            copy.start()
+        refs[first : first + count] = buffers
+        kernel(copies, *refs)
+
+    return run
+
+
+def stage_for(values):
+    return [VMEM(value.shape, value.dtype) for value in values] + [pltpu.SemaphoreType.DMA((len(values),))]
+
+
+def position():
+    seq = lax.axis_index("seq")
+    return seq, seq % 2, lax.axis_index("page"), seq // 2
+
+
+def anywhere(count):
+    return [pl.BlockSpec(memory_space=pl.ANY)] * count
 
 
 def forward(pages, lengths, tokens, patches, box, taps, matrices, vectors, table):
@@ -429,17 +488,23 @@
     own = jax.ShapeDtypeStruct((total_rows, width), bf16)
     every = jax.ShapeDtypeStruct((count, key_pad, width), bf16)
     return pl.pallas_call(
-        functools.partial(forward_kernel, pages),
+        staged(functools.partial(forward_kernel, pages), 1, 4),
         out_shape=(
-            jax.ShapeDtypeStruct((total_rows, width), f32), own, own, every, every, own,
-            jax.ShapeDtypeStruct((count, pairs, 2 * row_count, key_pad), bf16),
+            jax.ShapeDtypeStruct((total_rows, width), f32), own, own, own,
             jax.ShapeDtypeStruct((count, row_count, 256), i32),
             jax.ShapeDtypeStruct((count, 8, key_pad), i32),
             jax.ShapeDtypeStruct((count, 8, 256), i32),
+            every, every,
+            jax.ShapeDtypeStruct((count, pairs, 2 * row_count, key_pad), bf16),
         ),
-        in_specs=[pl.BlockSpec(memory_space=pltpu.SMEM)] + in_vmem(9),
-        out_specs=tuple(in_vmem(10)),
+        in_specs=[pl.BlockSpec(memory_space=pltpu.SMEM)] + anywhere(9),
+        out_specs=tuple(in_vmem(7) + anywhere(3)),
         scratch_shapes=[
+            VMEM((count, row_count, width), bf16),
+            VMEM((3, width, width), bf16),
+            VMEM((count, key_pad, width), bf16),
+            VMEM((count, key_pad, width), bf16),
+            VMEM((count, pairs, 2 * row_count, key_pad), bf16),
             VMEM((3, count, row_count, width), bf16),
             VMEM((4 * span + 16, width), f32),
             VMEM((6 * patch_span, width), f32),
@@ -450,15 +515,18 @@
             VMEM((8, key_pad), f32),
             VMEM((pairs, row_count, key_pad), i32),
             VMEM((2, 8, 128), i32),
+            pltpu.SemaphoreType.DMA((5,)),
+            pltpu.SemaphoreType.DMA((3, count)),
             pltpu.SemaphoreType.DMA((5, count)),
             pltpu.SemaphoreType.DMA((5, count)),
-        ],
+        ]
+        + stage_for((box, taps, vectors, table)),
         compiler_params=pltpu.CompilerParams(
             collective_id=0, has_side_effects=True, vmem_limit_bytes=KERNEL_VMEM
         ),
         cost_estimate=pl.CostEstimate(flops=8_000_000_000, bytes_accessed=25_000_000, transcendentals=3_000_000),
         name="forward",
-    )(lengths, tokens, patches, box, taps, *matrices, vectors, table)
+    )(lengths, box, taps, vectors, table, tokens, patches, *matrices)
 
 
 def backward_page_kernel(
@@ -622,10 +690,6 @@
     return (far[1], far[0], side) + tuple(far[2:]), (far[0], far[1], side) + tuple(far[2:])
 
 
-def late_orders(far, side):
-    return (side,) + tuple(far), (far[0], side) + tuple(far[1:])
-
-
 def slot_of_bits(bits):
     slot = 0
     for bit in bits:
@@ -671,12 +735,24 @@
 
 def middle_kernel(
     pages, direct,
-    scalar_ref, hidden_ref, mixture_ref, cotangent_ref, patch_cotangent_ref, out_weight_ref, up_weight_ref,
-    down_weight_ref, vector_ref,
-    output_ref, patch_output_ref, first_back_ref, mixture_back_ref, sums_ref, *rest,
+    vector_any, *rest,
 ):
+    scalar_ref = position()
+    arguments, rest = (*rest[:7], vector_any), rest[7:]
+    output_ref, patch_output_ref, first_back_ref, mixture_back_ref, sums_ref, *rest = rest
+    *rest, load_sem, store_sem = rest
+    copied, rest = rest[-8:], rest[:-8]
+    hidden_ref, mixture_ref, cotangent_ref, patch_cotangent_ref, out_weight_ref, up_weight_ref, down_weight_ref, vector_ref = (
+        copied
+    )
+    loads = [
+        pltpu.make_async_copy(source, target, load_sem.at[index])
+        for index, (source, target) in enumerate(zip(arguments, copied, strict=True))
+    ]
+    for index in (7, 1, 4, 0, 5, 6, 2, 3):
+        loads[index].start()
     if direct:
-        bundle_ref, *rest = rest
+        bundle_any, *rest, bundle_ref = rest
     else:
         normed_out_ref, up_out_ref, activated_out_ref, down_out_ref, attention_out_ref, *rest = rest
     state, unit, scale_ref, normed, activated, slope, up_back, down_back, attention_back, flipped = rest
@@ -696,6 +772,8 @@
         state[:, at] = hidden_ref[:, at] + (dot_nn(mixture_ref[...], out_weight_ref[:, at]) + vector_ref[2:3, at])
         return carry
 
+    for index in (0, 1, 4, 7):
+        loads[index].wait()
     lax.fori_loop(0, width // lanes, attention_tile, 0)
 
     def first_norm(chunk, carry):
@@ -718,6 +796,7 @@
         slope[:, at] = chance + branch * (jnp.exp(branch * branch * -0.5) * 0.3989422804014327)
         return carry
 
+    loads[5].wait()
     lax.fori_loop(0, wide // lanes, up_tile, 0)
 
     def down_tile(tile, carry):
@@ -725,6 +804,8 @@
         state[:, at] = state[:, at] + (dot_nn(activated[...], down_weight_ref[:, at]) + vector_ref[3:4, at])
         return carry
 
+    for index in (2, 3, 6):
+        loads[index].wait()
     lax.fori_loop(0, width // lanes, down_tile, 0)
 
     def second_norm(start, rows_here, page, out_ref, delta_ref):
@@ -814,6 +895,16 @@
         return carry
 
     lax.fori_loop(0, 2 * groups, up_weight_tile, 0)
+    stores = [
+        pltpu.make_async_copy(bundle_ref.at[part], bundle_any.at[part], store_sem.at[index])
+        for index, part in enumerate(
+            (
+                (core, slice(None), slice(0, tall)), (1 - core, slice(None), slice(0, tall)),
+                (slice(None), slice(None), slice(tall, tall + rows // 2)),
+            )
+        )
+    ]
+    stores[0].start()
 
     def down_weight_tile(page, carry):
         at = pl.ds(pl.multiple_of(page * tall, 128), tall)
@@ -824,6 +915,7 @@
         return carry
 
     lax.fori_loop(0, pages, down_weight_tile, 0)
+    stores[1].start()
     flipped[...] = mixture_ref[...].T
     half = rows // 2
 
@@ -840,6 +932,9 @@
         return carry
 
     lax.fori_loop(0, 2, out_weight_tile, 0)
+    stores[2].start()
+    for copy in stores:
+        copy.wait()
 
 
 def in_tiles(width, pages):
@@ -869,8 +964,8 @@
             jax.ShapeDtypeStruct((16, width), f32),
         )
         + extra,
-        in_specs=[pl.BlockSpec(memory_space=pltpu.SMEM)] + in_vmem(8),
-        out_specs=tuple(in_vmem(5 + len(extra))),
+        in_specs=anywhere(8),
+        out_specs=tuple(in_vmem(5) + (anywhere(1) if direct else in_vmem(len(extra)))),
         scratch_shapes=[
             pltpu.VMEM((total_rows, width), f32),
             pltpu.VMEM((total_rows, width), f32),
@@ -882,11 +977,17 @@
             pltpu.VMEM((total_rows, width), bf16),
             pltpu.VMEM((total_rows, width), bf16),
             pltpu.VMEM((width, total_rows), bf16),
-        ],
-        compiler_params=pltpu.CompilerParams(vmem_limit_bytes=56 * 1024 * 1024),
+        ]
+        + [pltpu.VMEM(value.shape, value.dtype) for value in (extra if direct else ())]
+        + [
+            pltpu.VMEM(value.shape, value.dtype)
+            for value in (hidden, mixture, cotangent, patch_cotangent, *matrices, vectors)
+        ]
+        + [pltpu.SemaphoreType.DMA((8,)), pltpu.SemaphoreType.DMA((3,))],
+        compiler_params=pltpu.CompilerParams(vmem_limit_bytes=KERNEL_VMEM),
         cost_estimate=pl.CostEstimate(flops=14_000_000_000, bytes_accessed=30_000_000, transcendentals=2_600_000),
         name="middle",
-    )(places, hidden, mixture, cotangent, patch_cotangent, *matrices, vectors)
+    )(vectors, hidden, mixture, cotangent, patch_cotangent, *matrices)
     first, rest = result[:5], result[5:]
     if direct:
         return first + rest
@@ -995,15 +1096,16 @@
 
 def backward_kernel(
     pages,
-    length_ref, query_ref, mixture_back_ref, columns_ref, rows_ref, query_rows_ref, tokens_ref, patches_ref, taps_ref,
+    staging, length_ref, query_ref, mixture_back_ref, columns_ref, rows_ref, query_rows_ref, tokens_ref, patches_ref, taps_ref,
     middle_sums_ref, bundle_any, weights_any, key_any, value_any, hidden_any, first_back_any, query_weight_any,
     key_weight_any, value_weight_any,
-    tokens_back_ref, patches_back_ref, early_ref, late_ref, sums_ref,
+    tokens_back_ref, patches_back_ref, early_ref, late_ref, sums_ref, up_in_ref, down_in_ref, mixed_in_ref,
     keep, landing, landings, late, late_landing, late_landings, weights_buf, key_buf, value_buf, outgoing, from_sib,
     from_far, matrices, hidden, flipped, total_back, query_back, key_back, value_back, back, steps, mask_ref, hot_ref,
     query_hot_ref, band_ref, table_acc, band_acc, table_out, text_rim, patch_rim, sums, sums_in,
+    up_in, down_out, down_in, mixed_out, mixed_in,
     load_sem, page_sem, early_send, early_recv, late_send, late_recv, sib_send, sib_recv, far_send, far_recv, rim_send,
-    rim_recv, sum_send, sum_recv,
+    rim_recv, sum_send, sum_recv, swap_send, swap_recv,
 ):
     page_at, bits, seq, across, core = places_of(pages)
     levels = len(bits)
@@ -1028,10 +1130,6 @@
         (page_at + either(flips[0], flips[1]), seq),
         opposite,
     ] + on_page[2:]
-    late_partners = [
-        (page_at + core * flips[0], seq + (1 - core) * (2 - 4 * across)),
-        (page_at + (1 - core) * flips[0], seq + core * (2 - 4 * across)),
-    ] + on_page[1:]
     barrier = pltpu.get_barrier_semaphore()
     everyone = [sibling, opposite, diagonal] + on_page
     for peer in everyone:
@@ -1067,9 +1165,11 @@
         keep, bundle_any.at[1], landing, landings, early_partners, sibling, (early_send, early_recv), 8
     )
     late_sum = Halving(
-        late.at[0], late.at[1], late_landing, late_landings, late_partners, sibling, (late_send, late_recv), 4
+        late.at[0], late.at[1], late_landing, late_landings, early_partners, sibling, (late_send, late_recv), 4
     )
     early.start()
+    for copy in staging:
+        copy.wait()
 
     lane128 = lax.broadcasted_iota(jnp.int32, (row_count, 128), 1)
     place = query_places(seq, (row_count, 128), span, patch_span, text_slots)
@@ -1198,7 +1298,7 @@
 
     events = {
         1: [("core", 0), ("core", 1)], 2: [("core", 2), ("core", 3)], 4: [("core", 4), ("core", 5)],
-        6: [("core", 6), ("core", 7)], 8: [(0, 0)], 12: [(0, 1), (1, 0)], 17: [(0, 2), (1, 1)],
+        6: [("core", 6), ("core", 7)], 8: [(0, 0)], 12: [(0, 1)],
     }
 
     def step_body(turn, carry):
@@ -1244,7 +1344,7 @@
             result = dot_nn(flipped[...], gradient[:, at]).astype(bf16)
             for page in range(pages):
                 far = [apart((page >> level) & 1, bit) for level, bit in enumerate(bits)]
-                slots = [slot_of_bits(order) for order in late_orders(far, apart(column, across))]
+                slots = [slot_of_bits(order) for order in early_orders(far, apart(column, across))]
                 first = page * rows
                 if index < 2:
                     late[core if index == 0 else 1 - core, slots[index], 0:rows, :] = result[first : first + rows]
@@ -1302,7 +1402,6 @@
     for head in range(heads):
         at_row = 8 + head
         sums[1, at_row : at_row + 1, :] = table_out[head, 0:1, :]
-    early.take(0, 3)
 
     for page in range(count):
         far_copy(page).wait_recv()
@@ -1315,6 +1414,8 @@
     weight_columns(1, key_back)
     weight_columns(2, value_back)
     late_sum.start()
+    for name in ((0, 2), (1, 0)):
+        early.take(*name)
     project_back(key_back, 1)
     project_back(value_back, 2)
     sums[0, 11:12, :] = column_sum(value_back[...].astype(f32))
@@ -1339,7 +1440,8 @@
         copy.start()
     for chunk in range(4):
         late_sum.take("core", chunk)
-    early.take(2, 0)
+    for name in ((0, 3), (1, 1)):
+        early.take(*name)
     for copy in rim_copies:
         copy.wait()
     sums[1, 0:8, :] = jnp.zeros((8, width), f32)
@@ -1411,23 +1513,44 @@
         sums[core] = sums[core] + sums_in[index]
         (sum_copies + [last])[index + 1].start()
 
+    late_sum.take(0, 0)
     sum_step(0)
-    late_sum.take(0, 0)
+    late_sum.take(0, 1)
+    early.take(2, 0)
     sum_step(1)
-    late_sum.take(0, 1)
     late_sum.take(1, 0)
     sum_step(2)
+    for step in range(2, levels + 1):
+        late_sum.take(step, 0)
+        sum_step(step + 1)
     for step in range(3, levels + 1):
         early.take(step, 0)
-    for step in range(2, levels + 1):
-        late_sum.take(step, 0)
-        if step + 1 <= levels + 1:
-            sum_step(step + 1)
     last.wait()
     sums_ref[core] = sums[core]
     sums_ref[1 - core] = sums_in[2 + levels]
+    wide_rows = 4 * rows
+    block = keep[0].astype(f32)
+    low, high = block[:, 0 : lanes // 2], pltpu.roll(block, lanes // 2, 1)[:, 0 : lanes // 2]
+    down_out[...] = low[0:wide_rows].astype(bf16)
+    mixed_out[0:half, :] = jnp.where(core == 0, high[wide_rows:], low[wide_rows:]).astype(bf16)
+    block = late[0, 0].astype(f32)
+    low, high = block[:, 0 : lanes // 2], pltpu.roll(block, lanes // 2, 1)[:, 0 : lanes // 2]
+    mixed_out[half:, :] = jnp.where(core == 0, high, low).astype(bf16)
+    swaps = [
+        remote(source, target, swap_send.at[index], swap_recv.at[index], *sibling)
+        for index, (source, target) in enumerate(
+            ((keep.at[0, 2 * rows : 4 * rows], up_in), (down_out, down_in), (mixed_out, mixed_in))
+        )
+    ]
+    for copy in swaps:
+        copy.start()
     early_ref[...] = keep[0]
     late_ref[...] = late[0, 0]
+    for copy in swaps:
+        copy.wait()
+    up_in_ref[...] = up_in[...]
+    down_in_ref[...] = down_in[...]
+    mixed_in_ref[...] = mixed_in[...]
     early.finish()
     late_sum.finish()
     for page in range(count):
@@ -1454,18 +1577,20 @@
     early_count = 8 + 4 + 2 + (levels - 1)
     late_count = 4 + 2 + levels
     return pl.pallas_call(
-        functools.partial(backward_kernel, pages),
+        staged(functools.partial(backward_kernel, pages), 1, len(local_values)),
         out_shape=(
             jax.ShapeDtypeStruct(tokens.shape, f32),
             jax.ShapeDtypeStruct(patches.shape, f32),
             jax.ShapeDtypeStruct((early_rows, lanes), bf16),
             jax.ShapeDtypeStruct((late_rows, lanes), bf16),
             jax.ShapeDtypeStruct((2, 24, width), f32),
+            jax.ShapeDtypeStruct((early_rows // 9 * 4, lanes), bf16),
+            jax.ShapeDtypeStruct((early_rows // 9 * 8, lanes // 2), bf16),
+            jax.ShapeDtypeStruct((early_rows // 9 + late_rows, lanes // 2), bf16),
         ),
         in_specs=[pl.BlockSpec(memory_space=pltpu.SMEM)]
-        + in_vmem(len(local_values))
-        + [pl.BlockSpec(memory_space=pl.ANY)] * len(far_values),
-        out_specs=tuple(in_vmem(5)),
+        + anywhere(len(local_values) + len(far_values)),
+        out_specs=tuple(in_vmem(8)),
         scratch_shapes=[
             VMEM((blocks, early_rows, lanes), bf16),
             VMEM((blocks, early_rows, lanes), bf16),
@@ -1499,17 +1624,100 @@
             VMEM((count, patch_span + 32, width), bf16),
             VMEM((2, 24, width), f32),
             VMEM((3 + levels, 24, width), f32),
+            VMEM((early_rows // 9 * 4, lanes), bf16),
+            VMEM((early_rows // 9 * 8, lanes // 2), bf16),
+            VMEM((early_rows // 9 * 8, lanes // 2), bf16),
+            VMEM((early_rows // 9 + late_rows, lanes // 2), bf16),
+            VMEM((early_rows // 9 + late_rows, lanes // 2), bf16),
             dma((6,)), dma((3, 2)),
             dma((early_count,)), dma((early_count,)), dma((late_count,)), dma((late_count,)),
             dma((count,)), dma((count,)), dma((count,)), dma((count,)),
-            dma((4,)), dma((4,)), dma((3 + levels,)), dma((3 + levels,)),
-        ],
+            dma((4,)), dma((4,)), dma((3 + levels,)), dma((3 + levels,)), dma((3,)), dma((3,)),
+        ]
+        + stage_for(local_values),
         compiler_params=pltpu.CompilerParams(
-            collective_id=1, has_side_effects=True, vmem_limit_bytes=62 * 1024 * 1024
+            collective_id=1, has_side_effects=True, vmem_limit_bytes=KERNEL_VMEM
         ),
         cost_estimate=pl.CostEstimate(flops=12_000_000_000, bytes_accessed=40_000_000, transcendentals=0),
         name="backward",
     )(lengths, *local_values, *far_values)
+
+
+def clip_lanes(sums, centre, bins):
+    first, last = centre + 1 - bins // 2, centre - 1 + bins // 2
+    lane = lax.broadcasted_iota(jnp.int32, sums.shape, 1)
+    below = jnp.sum(jnp.where(lane < first, sums, 0.0), axis=1, keepdims=True)
+    above = jnp.sum(jnp.where(lane >= last, sums, 0.0), axis=1, keepdims=True)
+    moved = pltpu.roll(sums, sums.shape[1] - (first - 1), 1)
+    moved = jnp.where(lane == 0, below, jnp.where(lane == bins - 1, above, moved))
+    return moved[:, :bins]
+
+
+def finish_kernel(
+    staging, early_ref, late_ref, sums_ref, up_in_ref, down_in_ref, mixed_in_ref,
+    query_ref, key_ref, value_ref, out_ref, up_ref, down_ref, taps_ref, patch_taps_ref, line_ref, across_ref,
+    upward_ref, vector_ref,
+):
+    f32 = jnp.float32
+    rows, columns = query_ref.shape
+    half = rows // 2
+    wide_rows = 4 * rows
+    first = position()[1] == 0
+    for copy in staging:
+        copy.wait()
+    heads = line_ref.shape[0]
+    block = early_ref[...].astype(f32)
+    low, high = block[:, 0:columns], pltpu.roll(block, columns, 1)[:, 0:columns]
+    up = jnp.where(first, block[0 : 2 * rows], up_in_ref[...].astype(f32))
+    up_ref[:, 0 : 2 * columns] = up[0:rows]
+    up_ref[:, 2 * columns : 4 * columns] = up[rows : 2 * rows]
+    down_ref[...] = jnp.where(first, down_in_ref[...].astype(f32), high[0:wide_rows])
+    kept = jnp.where(first, low[wide_rows:], high[wide_rows:])
+    got = mixed_in_ref[0:half, :].astype(f32)
+    out_ref[0:half, :] = jnp.where(first, kept, got)
+    out_ref[half:rows, :] = jnp.where(first, got, kept)
+    block = late_ref[...].astype(f32)
+    low, high = block[:, 0:columns], pltpu.roll(block, columns, 1)[:, 0:columns]
+    kept = jnp.where(first, low, high)
+    got = mixed_in_ref[half:, :].astype(f32)
+    query_ref[...] = jnp.where(first, kept[0:rows], got[0:rows])
+    key_ref[...] = jnp.where(first, got[0:rows], kept[0:rows])
+    value_ref[0:half, :] = jnp.where(first, kept[rows:], got[rows:])
+    value_ref[half:rows, :] = jnp.where(first, got[rows:], kept[rows:])
+    front, back = sums_ref[0], sums_ref[1]
+    width = front.shape[1]
+    text = [front[16 + index : 17 + index] for index in range(7)]
+    order = [text[2], text[3], text[4], text[1], text[3], text[5], text[0], text[3], text[6]]
+    taps_ref[...] = jnp.concatenate(order, axis=0)
+    patch_taps_ref[...] = jnp.concatenate([front[23:24], back[0:8]], axis=0)
+    across_ref[...] = clip_lanes(back[8:24, 0:256], 72, across_ref.shape[1])[0:heads]
+    upward_ref[...] = clip_lanes(back[8:24, 256:512], 72, upward_ref.shape[1])[0:heads]
+    line_ref[...] = clip_lanes(back[8:24, 512:640], 32, line_ref.shape[1])[0:heads]
+    vector_ref[...] = front[0:16]
+
+
+def finish(values, width, heads, line_bins, plane_bins):
+    rows, columns = values[1].shape[0] * 2 // 3, values[1].shape[1] // 2
+    f32 = jnp.float32
+    square = jax.ShapeDtypeStruct((rows, columns), f32)
+    taps = jax.ShapeDtypeStruct((9, width), f32)
+    plane = jax.ShapeDtypeStruct((heads, plane_bins), f32)
+    return pl.pallas_call(
+        staged(finish_kernel, 0, len(values)),
+        out_shape=(
+            square, square, square, square,
+            jax.ShapeDtypeStruct((rows, 4 * columns), f32),
+            jax.ShapeDtypeStruct((4 * rows, columns), f32),
+            taps, taps,
+            jax.ShapeDtypeStruct((heads, line_bins), f32), plane, plane,
+            jax.ShapeDtypeStruct((16, width), f32),
+        ),
+        in_specs=anywhere(len(values)),
+        out_specs=tuple(in_vmem(12)),
+        scratch_shapes=stage_for(values),
+        compiler_params=pltpu.CompilerParams(vmem_limit_bytes=KERNEL_VMEM),
+        name="finish",
+    )(*values)
 
 
 def exchange(value, pages, step):
@@ -1661,19 +1869,18 @@
     taps = jnp.pad(
         jnp.concatenate([conv_weight, patch_conv_weight], axis=1).astype(jnp.float32).T, ((0, 6), (0, 0))
     )
-    vectors = jnp.concatenate(
-        [
-            jnp.stack(
-                [
-                    query_bias, value_bias, out_bias, down_bias,
-                    attention_gain, attention_shift, feedforward_gain, feedforward_shift,
-                ]
-            ),
-            up_bias.reshape(-1, model_width),
-        ]
-    ).astype(jnp.float32)
+    vector_row = jnp.arange(8 + up_bias.shape[0] // model_width, dtype=jnp.int32)[:, None]
+    vectors = jnp.pad(up_bias.reshape(-1, model_width), ((8, 0), (0, 0)))
+    for index, vector in enumerate(
+        (
+            query_bias, value_bias, out_bias, down_bias, attention_gain, attention_shift, feedforward_gain,
+            feedforward_shift,
+        )
+    ):
+        vectors = jnp.where(vector_row == index, vector[None, :], vectors)
+    vectors = vectors.astype(jnp.float32)
     (
-        hidden, hidden_low, queries, keys, values, mixture_low, weights, columns, key_rows, query_rows,
+        hidden, hidden_low, queries, mixture_low, columns, key_rows, query_rows, keys, values, weights,
     ) = forward(
         pages, page_length, tokens, patches, box_position, taps, (query_weight, key_weight, value_weight),
         vectors, table,
@@ -1689,7 +1896,7 @@
         (out_weight, up_weight, down_weight), vectors, pages,
     )
     if in_tiles(model_width, pages):
-        tokens_gradient, patches_gradient, early_state, late_state, sums = backward(
+        tokens_gradient, patches_gradient, early_state, late_state, sums, up_in, down_in, mixed_in = backward(
             pages,
             page_length,
             (
@@ -1702,14 +1909,13 @@
             tokens,
             patches,
         )
-        query_part, key_part, value_part = bundle_parts(late_state, model_width // pages, places[1])
-        up_part, down_part, out_part = bundle_parts(early_state, up_weight.shape[1] // pages, places[1])
-        front, late_sums = sums[0], sums[1]
-        text_columns = front[16:23]
-        centre = text_columns[3]
-        head_sums = late_sums[8 : 8 + head_count]
-        plane_sums = head_sums[:, :512].reshape(head_count, 2, 256).transpose(1, 0, 2)
-        plane_sums = clipped(plane_sums, 72, plane_bins)
+        (
+            query_part, key_part, value_part, out_part, up_part, down_part, text_part, patch_part, line_part,
+            across_part, upward_part, vector_rows,
+        ) = finish(
+            (early_state, late_state, sums, up_in, down_in, mixed_in), model_width, head_count, line_bins,
+            plane_bins,
+        )
         return (
             output,
             patch_output,
@@ -1719,29 +1925,22 @@
             key_part,
             value_part,
             out_part,
-            up_part.reshape(model_width // pages, -1),
+            up_part,
             down_part,
-            jnp.stack(
-                [
-                    text_columns[2], centre, text_columns[4],
-                    text_columns[1], centre, text_columns[5],
-                    text_columns[0], centre, text_columns[6],
-                ],
-                axis=1,
-            ),
-            jnp.concatenate([front[23:24], late_sums[0:8]], axis=0).T,
-            front[10],
-            front[11],
-            front[OUT_BIAS],
-            front[UP_BIAS : UP_BIAS + 4].reshape(-1),
-            front[DOWN_BIAS],
-            front[FIRST_GAIN],
-            front[FIRST_SHIFT],
-            front[SECOND_GAIN],
-            front[SECOND_SHIFT],
-            clipped(head_sums[:, 512:640], 32, line_bins),
-            plane_sums[0],
-            plane_sums[1],
+            text_part.T,
+            patch_part.T,
+            vector_rows[10],
+            vector_rows[11],
+            vector_rows[OUT_BIAS],
+            vector_rows[UP_BIAS : UP_BIAS + 4].reshape(-1),
+            vector_rows[DOWN_BIAS],
+            vector_rows[FIRST_GAIN],
+            vector_rows[FIRST_SHIFT],
+            vector_rows[SECOND_GAIN],
+            vector_rows[SECOND_SHIFT],
+            line_part,
+            across_part,
+            upward_part,
         )
     delta_first = delta_first.reshape(page_count, row_count, model_width)
     delta_mixture = delta_mixture.reshape(page_count, row_count, model_width)

time: 257 us -> 218 us (0.85)
  local copies, waits for them, and re-layouts: 25.5 us -> 8.7 us
  Pallas kernels: 220 us -> 204 us
  other arithmetic: 8.6 us -> 4.35 us
    pallas_call x2 -> x3, Pallas kernels: 174 us -> 163 us  [the longest x1 111 us: backward(): pl.pallas_call(staged(functools.partial(backward_kernel, pages), 1, len(l...]
    unnamed x40 -> x8, local copies, waits for them, and re-layouts: 13 us -> 4.86 us
    another operation x9 -> x0, local copies, waits for them, and re-layouts: 6.75 us -> none  [the longest x8 5.48 us: shards(): jnp.stack([query_bias, value_bias, out_bias, down_bias, attention_gain, a...]
    pallas_call x1, Pallas kernels: 46 us -> 41 us  [middle(): pl.pallas_call(functools.partial(middle_kernel, pages, direct), out_shape...]
    select_n x6 -> x0, other arithmetic: 2.93 us -> none  [the longest x2 1.78 us: bundle_parts(): jnp.where(first, tail[:, lanes:], tail[:, :lanes])]
  transfers between devices with their start and end apart: 2 -> 0, of which waited for: 0 -> 0; matrix products, arithmetic and copies ran while one was open for 4% -> 0% of each run, Pallas kernels for 0% -> 0%
where the time goes in v2:
time: 218 us
  Pallas kernels  204 us (94%)
  local copies, waits for them, and re-layouts  8.7 us (4%)
  other arithmetic  4.35 us (2%)
    pallas_call x1, Pallas kernels, backward(): pl.pallas_call(staged(functools.partial(backward_kernel, pages), 1, len(l...  111 us
    pallas_call x1, Pallas kernels, forward(): pl.pallas_call(staged(functools.partial(forward_kernel, pages), 1, 4), ou...  49 us
    pallas_call x1, Pallas kernels, middle(): pl.pallas_call(functools.partial(middle_kernel, pages, direct), out_shape...  41 us
    unnamed x8, local copies, waits for them, and re-layouts  4.86 us

profile of v2, /device:TPU:0, one launch (start us, length us, event | category | flops | bytes accessed | tf_op | source)
XLA Modules:
  0.0 217.5 jit_solution(3934606064171157367)
XLA Ops:
  0.7 0.7 reshape.102
  1.4 1.5 select_convert_fusion.refs_3_.vector_any
  2.9 1.3 copy.50.refs_1_
  4.2 0.8 maximum_bitcast_fusion
  5.0 0.6 pad_convert_fusion.refs_2_.refs_8_
  5.6 0.1 pad.16.clone
  5.7 1.4 maximum_convert_fusion.refs_4_
  7.1 49.0 %forward.1 = (f32[432,768]{1,0:T(8,128)}, bf16[432,768]{1,0:T(8,128)(2,1)}, bf16[432,768]{1,0:T(8,128)(2,1)}, bf16[432,768]{1,0:T(8,128)(2,1)}, s32[3,144,256]{2...) custom-call(s32[3]{0:T(128)} %refs_0_.3, ...), custom_call_target="tpu_custom_call" | custom-call | flops 8000000000 | bytes 25000000 | tf_op jit(solution)/shard_map/forward/pallas_call | solution.py:490
  56.1 41.0 %middle.1 = (f32[3,128,768]{2,1,0:T(8,128)}, f32[3,16,768]{2,1,0:T(8,128)}, f32[432,768]{1,0:T(8,128)}, bf16[432,768]{1,0:T(8,128)(2,1)}, f32[16,768]{1,0:T(8,128)}, /*index=5*/bf16[2,16,432,384]{3,2,1,0:T(8,128)(2,1)}) custom-call(f32[12,768]{1,0:T(8,128)} %select_convert_fusion.refs_3_.vector_any, f32[432,768]{1,0:T(8,128)} %get-tuple-element.60.rest_0_, ...), custom_call_target="tpu_custom_call" | custom-call | flops 14000000000 | bytes 30000000 | tf_op jit(solution)/shard_map/middle/pallas_call | solution.py:957
  97.1 111.2 %backward.1 = (f32[3,128,768]{2,1,0:T(8,128)}, f32[3,16,768]{2,1,0:T(8,128)}, bf16[432,384]{1,0:T(8,128)(2,1)}, bf16[144,384]{1,0:T(8,128)(2,1)}, f32[2,24,768]{...) custom-call(s32[3]{0:T(128)} %refs_0_.3, ...), custom_call_target="tpu_custom_call" | custom-call | flops 12000000000 | bytes 40000000 | tf_op jit(solution)/shard_map/backward/pallas_call | solution.py:1579
  208.3 0.0 copy-start
  208.3 2.6 %finish.1 = (f32[96,192]{1,0:T(8,128)}, f32[96,192]{1,0:T(8,128)}, f32[96,192]{1,0:T(8,128)}, f32[96,192]{1,0:T(8,128)}, f32[96,768]{1,0:T(8,128)}, /*index=5*/f...) custom-call(bf16[432,384]{1,0:T(8,128)(2,1)} %get-tuple-element.78.r, ...), custom_call_target="tpu_custom_call" | custom-call | tf_op jit(solution)/shard_map/finish/pallas_call | solution.py:1705
  210.9 1.9 copy.51
  212.8 0.0 copy-start.1
  212.8 1.6 slice_reduce_fusion
  214.4 0.8 slice.30
  215.2 0.6 reshape.103
  215.8 0.0 copy-done
  215.8 1.0 copy.54
  216.8 0.0 copy-done.1
  216.8 0.7 copy.55
  (5 shorter events, 0.0 us)
Async XLA Ops:
  208.3 7.5 %copy-start = (f32[3,128,768]{2,1,0:T(8,128)S(1)}, f32[3,128,768]{2,1,0:T(8,128)}, u32[]{:S(2)}) copy-start(f32[3,128,768]{2,1,0:T(8,128)} %get-tuple-element.162) | copy-start | bytes 3538948
  212.8 4.1 %copy-start.1 = (f32[3,16,768]{2,1,0:T(8,128)S(1)}, f32[3,16,768]{2,1,0:T(8,128)}, u32[]{:S(2)}) copy-start(f32[3,16,768]{2,1,0:T(8,128)} %get-tuple-element.163) | copy-start | bytes 442372

commit v3 on v2

--- a/solution.py
+++ b/solution.py
@@ -113,19 +113,25 @@
     return jnp.take_along_axis(jnp.broadcast_to(table_row, lanes.shape), lanes, axis=1)
 
 
-def pair_masked(pair):
-    lane = lax.broadcasted_iota(jnp.int32, pair.shape, 1)
-    half = pair.shape[1] // 2
-    zero = jnp.zeros_like(pair)
+HEAD_LANES = 64
+
+
+def split_heads(group):
+    lane = lax.broadcasted_iota(jnp.int32, group.shape, 1) // HEAD_LANES
+    zero = jnp.zeros_like(group)
     return jnp.concatenate(
-        [jnp.where(lane < half, pair, zero), jnp.where(lane < half, zero, pair)], axis=0
-    )
-
-
-def pair_merged(both):
-    rows, width = both.shape[0] // 2, both.shape[1]
-    lane = lax.broadcasted_iota(jnp.int32, (rows, width), 1)
-    return jnp.where(lane < width // 2, both[:rows], both[rows:])
+        [jnp.where(lane == head, group, zero) for head in range(group.shape[1] // HEAD_LANES)], axis=0
+    )
+
+
+def merge_heads(rows):
+    heads = rows.shape[1] // HEAD_LANES
+    count = rows.shape[0] // heads
+    lane = lax.broadcasted_iota(jnp.int32, (count, rows.shape[1]), 1) // HEAD_LANES
+    merged = rows[:count]
+    for head in range(1, heads):
+        merged = jnp.where(lane == head, rows[head * count : (head + 1) * count], merged)
+    return merged
 
 
 def dot_nt(left, right):
@@ -213,7 +219,9 @@
             )
         ]
 
-    pairs = weights_ref.shape[1]
+    groups = weights_ref.shape[1]
+    members = weights_ref.shape[2] // row_count
+    pairs = groups * members // 2
     peers = (sibling_of(seq), across_of(seq))
     barrier = pltpu.get_barrier_semaphore()
     for peer in peers:
@@ -266,7 +274,7 @@
     grid[patch_span * 5 :, :] = jnp.zeros((patch_span, width), jnp.float32)
     low[row_count * 4 :, :] = jnp.zeros((key_pad - row_count * 4, width), jnp.bfloat16)
     lanes = 256
-    pair_width = 128
+    group_width = members * HEAD_LANES
     power = 1.4426950408889634 / FIXED
     for copy in first_copies(0, 1):
         copy.wait_recv()
@@ -367,20 +375,12 @@
             lax.fori_loop(0, width // lanes, convolve, 0)
         own_rows = pl.ds(pl.multiple_of(base, 16), row_count)
 
-        def project(tile, carry):
-            at = pl.ds(pl.multiple_of(tile * lanes, lanes), lanes)
-            key_ref[page, :, at] = dot_nn(low[...], matrices[1, :, at]).astype(jnp.bfloat16)
-            value_ref[page, :, at] = (dot_nn(low[...], matrices[2, :, at]) + vector_ref[1:2, at]).astype(
-                jnp.bfloat16
-            )
-            query_ref[own_rows, at] = (
-                (dot_nn(hidden_low_ref[own_rows, :], matrices[0, :, at]) + vector_ref[0:1, at])
-                .astype(jnp.bfloat16)
-                * jnp.bfloat16(0.125)
-            )
-            return carry
-
-        lax.fori_loop(0, width // lanes, project, 0)
+        key_ref[page] = dot_nn(low[...], matrices[1]).astype(jnp.bfloat16)
+        value_ref[page] = (dot_nn(low[...], matrices[2]) + vector_ref[1:2, :]).astype(jnp.bfloat16)
+        query_ref[own_rows, :] = (
+            (dot_nn(hidden_low_ref[own_rows, :], matrices[0]) + vector_ref[0:1, :]).astype(jnp.bfloat16)
+            * jnp.bfloat16(0.125)
+        )
 
         @pl.when(page < count - 1)
         def _():
@@ -388,11 +388,12 @@
                 copy.wait_recv()
             onward_copy(page + 1).start()
 
-        def attend(pair, carry):
-            at = pl.ds(pl.multiple_of(pair * pair_width, pair_width), pair_width)
-            scores[...] = dot_nt(pair_masked(query_ref[own_rows, at] * jnp.bfloat16(FIXED)), key_ref[page, :, at])
-            plane_row = packed_ref[0, pl.ds(pair, 1), :]
-            for start in range(0, row_count, CHUNK):
+        def attend(group, carry):
+            at = pl.ds(pl.multiple_of(group * group_width, group_width), group_width)
+            scores[...] = dot_nt(split_heads(query_ref[own_rows, at] * jnp.bfloat16(FIXED)), key_ref[page, :, at])
+            for start, sub in ((start, sub) for start in range(0, row_count, CHUNK) for sub in range(members // 2)):
+                pair = group * (members // 2) + sub
+                plane_row = packed_ref[0, pl.ds(pair, 1), :]
                 here = slice(start, start + CHUNK)
                 packed = []
                 for block_at in range(0, key_pad, 128):
@@ -403,7 +404,8 @@
                         + lookup(plane_row, upward_ref[here, lane])
                     )
                 for side in range(2):
-                    there = slice(side * row_count + start, side * row_count + start + CHUNK)
+                    first = (2 * sub + side) * row_count + start
+                    there = slice(first, first + CHUNK)
                     parts, top = [], None
                     for index, word in enumerate(packed):
                         lane = slice(128 * index, 128 * (index + 1))
@@ -418,15 +420,15 @@
                         total = total + part
                     inverse = 1.0 / jnp.sum(total, axis=1, keepdims=True)
                     for index, part in enumerate(parts):
-                        weights_ref[page, pair, there, 128 * index : 128 * (index + 1)] = (part * inverse).astype(
+                        weights_ref[page, group, there, 128 * index : 128 * (index + 1)] = (part * inverse).astype(
                             jnp.bfloat16
                         )
-            mixture_ref[own_rows, at] = pair_merged(
-                dot_nn(weights_ref[page, pair], value_ref[page, :, at])
+            mixture_ref[own_rows, at] = merge_heads(
+                dot_nn(weights_ref[page, group], value_ref[page, :, at])
             ).astype(jnp.bfloat16)
             return carry
 
-        lax.fori_loop(0, pairs, attend, 0)
+        lax.fori_loop(0, groups, attend, 0)
         for copy in stores(page):
             copy.start()
         return carry
@@ -484,6 +486,8 @@
     total_rows = count * row_count
     key_pad = -(-4 * row_count // 128) * 128
     pairs = table.shape[0] // 2
+    members = 4 if table.shape[0] % 4 == 0 else 2
+    groups = table.shape[0] // members
     bf16, f32, i32 = jnp.bfloat16, jnp.float32, jnp.int32
     own = jax.ShapeDtypeStruct((total_rows, width), bf16)
     every = jax.ShapeDtypeStruct((count, key_pad, width), bf16)
@@ -495,7 +499,7 @@
             jax.ShapeDtypeStruct((count, 8, key_pad), i32),
             jax.ShapeDtypeStruct((count, 8, 256), i32),
             every, every,
-            jax.ShapeDtypeStruct((count, pairs, 2 * row_count, key_pad), bf16),
+            jax.ShapeDtypeStruct((count, groups, members * row_count, key_pad), bf16),
         ),
         in_specs=[pl.BlockSpec(memory_space=pltpu.SMEM)] + anywhere(9),
         out_specs=tuple(in_vmem(7) + anywhere(3)),
@@ -504,12 +508,12 @@
             VMEM((3, width, width), bf16),
             VMEM((count, key_pad, width), bf16),
             VMEM((count, key_pad, width), bf16),
-            VMEM((count, pairs, 2 * row_count, key_pad), bf16),
+            VMEM((count, groups, members * row_count, key_pad), bf16),
             VMEM((3, count, row_count, width), bf16),
             VMEM((4 * span + 16, width), f32),
             VMEM((6 * patch_span, width), f32),
             VMEM((key_pad, width), bf16),
-            VMEM((2 * row_count, key_pad), f32),
+            VMEM((members * row_count, key_pad), f32),
             VMEM((row_count, key_pad), i32),
             VMEM((row_count, key_pad), i32),
             VMEM((8, key_pad), f32),
@@ -577,8 +581,8 @@
 
     def attend(pair, carry):
         at = pl.ds(pl.multiple_of(pair * pair_width, pair_width), pair_width)
-        both_query = pair_masked(query_ref[:, at])
-        both_back = pair_masked(mixture_back_ref[:, at])
+        both_query = split_heads(query_ref[:, at])
+        both_back = split_heads(mixture_back_ref[:, at])
         back[...] = dot_nt(both_back, value_ref[:, at])
         for start in range(0, 2 * row_count, CHUNK):
             there = slice(start, start + CHUNK)
@@ -599,7 +603,7 @@
                 steps[there, 2 * key_pad + 128 * index : 2 * key_pad + 128 * (index + 1)] = (
                     step * mask_ref[here, key_pad + 128 * index : key_pad + 128 * (index + 1)]
                 )
-        query_back_ref[:, at] = (pair_merged(dot_nn(steps[:, 0:key_pad], key_ref[:, at])) * 0.125).astype(
+        query_back_ref[:, at] = (merge_heads(dot_nn(steps[:, 0:key_pad], key_ref[:, at])) * 0.125).astype(
             jnp.bfloat16
         )
         for kind, value in enumerate(
@@ -761,7 +765,7 @@
     row_count = span + patch_span
     total_rows = count * row_count
     wide = up_weight_ref.shape[1]
-    lanes = 256
+    lanes = width
     sums_ref[...] = jnp.zeros_like(sums_ref)
 
     def tile_at(tile):
@@ -790,7 +794,7 @@
 
     def up_tile(tile, carry):
         at = tile_at(tile)
-        branch = dot_nn(normed[...], up_weight_ref[:, at]) + vector_ref[pl.ds(8 + tile // 3, 1), tile_at(tile % 3)]
+        branch = dot_nn(normed[...], up_weight_ref[:, at]) + vector_ref[pl.ds(8 + tile, 1), :]
         chance = 0.5 * (1.0 + lax.erf(branch * 0.7071067811865476))
         activated[:, at] = (branch * chance).astype(jnp.bfloat16)
         slope[:, at] = chance + branch * (jnp.exp(branch * branch * -0.5) * 0.3989422804014327)
@@ -835,7 +839,7 @@
         at = tile_at(tile)
         low = (dot_nt(down_back[...], down_weight_ref[at, :]) * slope[:, at]).astype(jnp.bfloat16)
         up_back[:, at] = low
-        sums_ref[pl.ds(UP_BIAS + tile // 3, 1), tile_at(tile % 3)] = column_sum(low.astype(jnp.float32))
+        sums_ref[pl.ds(UP_BIAS + tile, 1), :] = column_sum(low.astype(jnp.float32))
         return carry
 
     lax.fori_loop(0, wide // lanes, up_back_tile, 0)
@@ -884,17 +888,18 @@
     flipped[...] = normed[...].T
 
     def up_weight_tile(tile, carry):
-        column, group = tile // groups, tile % groups
-        at = pl.ds(pl.multiple_of(tile * block, block), block)
+        at = pl.ds(pl.multiple_of(tile * 2 * block, 2 * block), 2 * block)
         result = dot_nn(flipped[...], up_back[:, at]).astype(jnp.bfloat16)
-        for page in range(pages):
-            slot = early_slots(scalar_ref, page, column, levels)[0]
-            bundle_ref[core, slot, pl.ds(pl.multiple_of(group * rows, 16), rows), :] = result[
-                page * rows : (page + 1) * rows
-            ]
+        for part in range(2):
+            column, group = (2 * tile + part) // groups, (2 * tile + part) % groups
+            for page in range(pages):
+                slot = early_slots(scalar_ref, page, column, levels)[0]
+                bundle_ref[core, slot, pl.ds(pl.multiple_of(group * rows, 16), rows), :] = result[
+                    page * rows : (page + 1) * rows, part * block : (part + 1) * block
+                ]
         return carry
 
-    lax.fori_loop(0, 2 * groups, up_weight_tile, 0)
+    lax.fori_loop(0, groups, up_weight_tile, 0)
     stores = [
         pltpu.make_async_copy(bundle_ref.at[part], bundle_any.at[part], store_sem.at[index])
         for index, part in enumerate(
@@ -919,19 +924,15 @@
     flipped[...] = mixture_ref[...].T
     half = rows // 2
 
-    def out_weight_tile(column, carry):
-        at = pl.ds(pl.multiple_of(column * block, block), block)
-        result = dot_nn(flipped[...], attention_back[:, at]).astype(jnp.bfloat16)
+    result = dot_nn(flipped[...], attention_back[...]).astype(jnp.bfloat16)
+    for column in range(2):
         for page in range(pages):
             slots = early_slots(scalar_ref, page, column, levels)
             for order in range(2):
                 first = page * rows + order * half
                 bundle_ref[core if order == 0 else 1 - core, slots[order], tall : tall + half, :] = result[
-                    first : first + half
+                    first : first + half, column * block : (column + 1) * block
                 ]
-        return carry
-
-    lax.fori_loop(0, 2, out_weight_tile, 0)
     stores[2].start()
     for copy in stores:
         copy.wait()
@@ -1101,7 +1102,7 @@
     key_weight_any, value_weight_any,
     tokens_back_ref, patches_back_ref, early_ref, late_ref, sums_ref, up_in_ref, down_in_ref, mixed_in_ref,
     keep, landing, landings, late, late_landing, late_landings, weights_buf, key_buf, value_buf, outgoing, from_sib,
-    from_far, matrices, hidden, flipped, total_back, query_back, key_back, value_back, back, steps, mask_ref, hot_ref,
+    from_far, matrices, flipped, total_back, query_back, key_back, value_back, back, steps, mask_ref, hot_ref,
     query_hot_ref, band_ref, table_acc, band_acc, table_out, text_rim, patch_rim, sums, sums_in,
     up_in, down_out, down_in, mixed_out, mixed_in,
     load_sem, page_sem, early_send, early_recv, late_send, late_recv, sib_send, sib_recv, far_send, far_recv, rim_send,
@@ -1115,8 +1116,10 @@
     total_rows = count * row_count
     key_pad = key_buf.shape[1]
     text_slots = 4 * span
-    pairs = weights_buf.shape[1]
-    heads = 2 * pairs
+    groups = weights_buf.shape[1]
+    members = weights_buf.shape[2] // row_count
+    heads = groups * members
+    group_width = members * HEAD_LANES
     f32, bf16 = jnp.float32, jnp.bfloat16
 
     sibling = (page_at, sibling_of(seq))
@@ -1141,7 +1144,7 @@
         for index, (source, target) in enumerate(
             (
                 (query_weight_any, matrices.at[0]), (key_weight_any, matrices.at[1]),
-                (value_weight_any, matrices.at[2]), (hidden_any, hidden), (first_back_any, total_back),
+                (value_weight_any, matrices.at[2]), (hidden_any, key_back), (first_back_any, total_back),
             )
         )
     ]
@@ -1158,8 +1161,6 @@
     for copy in page_loads(0):
         copy.start()
     keep_load.start()
-    for copy in later_loads:
-        copy.start()
     pl.semaphore_wait(barrier, len(everyone))
     early = Halving(
         keep, bundle_any.at[1], landing, landings, early_partners, sibling, (early_send, early_recv), 8
@@ -1186,8 +1187,6 @@
     query_hot_ref[144:192, :] = (
         ((place_of_row >> 4) == lax.broadcasted_iota(jnp.int32, (48, row_count), 0)).astype(f32).astype(bf16)
     )
-    pair_width = 128
-
     def start_page(page):
         slot = page % 2
         for copy in page_loads(page):
@@ -1221,20 +1220,20 @@
             query_bin = query_rows_ref[page, side : side + 1, 0:row_count] >> 4
             query_hot_ref[72 * side : 72 * (side + 1), :] = (71 - query_bin == half_bin).astype(f32).astype(bf16)
 
-    def attend(page, pair):
+    def attend(page, group):
         slot = page % 2
-        at = pl.ds(pl.multiple_of(pair * pair_width, pair_width), pair_width)
+        at = pl.ds(pl.multiple_of(group * group_width, group_width), group_width)
         own_rows = pl.ds(pl.multiple_of(page * row_count, 16), row_count)
-        both_query = pair_masked(query_ref[own_rows, at])
-        both_back = pair_masked(mixture_back_ref[own_rows, at])
+        both_query = split_heads(query_ref[own_rows, at])
+        both_back = split_heads(mixture_back_ref[own_rows, at])
         back[...] = dot_nt(both_back, value_buf[slot, :, at])
-        for start in range(0, 2 * row_count, CHUNK):
+        for start in range(0, members * row_count, CHUNK):
             there = slice(start, start + CHUNK)
             here = slice(start % row_count, start % row_count + CHUNK)
             parts, total = [], None
             for block_at in range(0, key_pad, 128):
                 lane = slice(block_at, block_at + 128)
-                part = weights_buf[slot, pair, there, lane].astype(f32)
+                part = weights_buf[slot, group, there, lane].astype(f32)
                 product = part * back[there, lane]
                 total = product if total is None else total + product
                 parts.append(part)
@@ -1248,10 +1247,10 @@
                     step * mask_ref[here, key_pad + 128 * index : key_pad + 128 * (index + 1)]
                 )
         query_back[own_rows, at] = (
-            pair_merged(dot_nn(steps[:, 0:key_pad], key_buf[slot, :, at])) * 0.125
+            merge_heads(dot_nn(steps[:, 0:key_pad], key_buf[slot, :, at])) * 0.125
         ).astype(bf16)
         for kind, value in enumerate(
-            (dot_tn(steps[:, 0:key_pad], both_query), dot_tn(weights_buf[slot, pair], both_back))
+            (dot_tn(steps[:, 0:key_pad], both_query), dot_tn(weights_buf[slot, group], both_back))
         ):
             value = value.astype(bf16)
             for where in range(4):
@@ -1261,8 +1260,8 @@
                     text_slots + where * patch_span : text_slots + (where + 1) * patch_span
                 ]
         bins = dot_nt(steps[...], hot_ref[...]).astype(bf16)
-        for side in range(2):
-            head = 2 * pair + side
+        for side in range(members):
+            head = members * group + side
             base = side * row_count
             both = dot_nn(query_hot_ref[...], bins[base : base + row_count])
             table_acc[head, 0:72, :] += both[0:72, 0:128]
@@ -1300,68 +1299,74 @@
         1: [("core", 0), ("core", 1)], 2: [("core", 2), ("core", 3)], 4: [("core", 4), ("core", 5)],
         6: [("core", 6), ("core", 7)], 8: [(0, 0)], 12: [(0, 1)],
     }
+    last_turn = count * groups - 1
 
     def step_body(turn, carry):
-        page, pair = turn // pairs, turn % pairs
-
-        @pl.when(pair == 0)
+        page, group = turn // groups, turn % groups
+
+        @pl.when(group == 0)
         def _():
             start_page(page)
 
         for at_turn, names in events.items():
 
-            @pl.when(turn == at_turn)
+            @pl.when(turn == min(at_turn, last_turn))
             def _(names=names, at_turn=at_turn):
                 if at_turn == min(events):
                     keep_load.wait()
                 for name in names:
                     early.take(*name)
 
-        @pl.when((pair == 2) & (page > 0))
+        @pl.when(turn == min(3, last_turn))
+        def _():
+            for copy in later_loads:
+                copy.start()
+
+        @pl.when((group == 1) & (page > 0))
         def _():
             pass_on(page - 1)
 
-        attend(page, pair)
-
-        @pl.when(pair == pairs - 1)
+        attend(page, group)
+
+        @pl.when(group == groups - 1)
         def _():
             sib_copy(page).start()
 
         return carry
 
-    lax.fori_loop(0, count * pairs, step_body, 0)
+    lax.fori_loop(0, count * groups, step_body, 0)
 
     for copy in later_loads:
         copy.wait()
-    flipped[...] = hidden[...].T
+    flipped[...] = key_back[...].T
     lanes = 384
     rows = width // pages
     half = rows // 2
 
     def weight_columns(index, gradient):
-        def tile(column, carry):
-            at = pl.ds(pl.multiple_of(column * lanes, lanes), lanes)
-            result = dot_nn(flipped[...], gradient[:, at]).astype(bf16)
-            for page in range(pages):
-                far = [apart((page >> level) & 1, bit) for level, bit in enumerate(bits)]
-                slots = [slot_of_bits(order) for order in early_orders(far, apart(column, across))]
-                first = page * rows
-                if index < 2:
-                    late[core if index == 0 else 1 - core, slots[index], 0:rows, :] = result[first : first + rows]
-                else:
-                    late[core, slots[0], rows : rows + half, :] = result[first : first + half]
-                    late[1 - core, slots[1], rows : rows + half, :] = result[first + half : first + rows]
+        def tile(four, carry):
+            tile_rows = pl.ds(pl.multiple_of(four * 4 * rows, 128), 4 * rows)
+            result = dot_nn(flipped[tile_rows, :], gradient[...]).astype(bf16)
+            for inner in range(4):
+                page = four * 4 + inner
+                first = inner * rows
+                for column in range(2):
+                    far = [apart((page // 2**level) % 2, bit) for level, bit in enumerate(bits)]
+                    slots = [slot_of_bits(order) for order in early_orders(far, apart(column, across))]
+                    at = slice(column * lanes, (column + 1) * lanes)
+                    if index < 2:
+                        late[core if index == 0 else 1 - core, slots[index], 0:rows, :] = result[
+                            first : first + rows, at
+                        ]
+                    else:
+                        late[core, slots[0], rows : rows + half, :] = result[first : first + half, at]
+                        late[1 - core, slots[1], rows : rows + half, :] = result[first + half : first + rows, at]
             return carry
 
-        lax.fori_loop(0, 2, tile, 0)
+        lax.fori_loop(0, pages // 4, tile, 0)
 
     def project_back(gradient, matrix):
-        def tile(column, carry):
-            at = pl.ds(pl.multiple_of(column * 256, 256), 256)
-            total_back[:, at] = total_back[:, at] + dot_nt(gradient[...], matrices[matrix, at, :])
-            return carry
-
-        lax.fori_loop(0, width // 256, tile, 0)
+        total_back[...] = total_back[...] + dot_nt(gradient[...], matrices[matrix])
 
     pass_on(count - 1)
     weight_columns(0, query_back)
@@ -1403,6 +1408,8 @@
         at_row = 8 + head
         sums[1, at_row : at_row + 1, :] = table_out[head, 0:1, :]
 
+    for name in ((0, 2), (1, 0)):
+        early.take(*name)
     for page in range(count):
         far_copy(page).wait_recv()
         own_rows = slice(page * row_count, (page + 1) * row_count)
@@ -1414,8 +1421,6 @@
     weight_columns(1, key_back)
     weight_columns(2, value_back)
     late_sum.start()
-    for name in ((0, 2), (1, 0)):
-        early.take(*name)
     project_back(key_back, 1)
     project_back(value_back, 2)
     sums[0, 11:12, :] = column_sum(value_back[...].astype(f32))
@@ -1496,6 +1501,7 @@
                 sums[1, index - 1 : index, at] = value
         return carry
 
+    early.take(2, 0)
     lax.fori_loop(0, width // 256, position_tile, 0)
 
     sum_partners = [opposite] + on_page
@@ -1516,7 +1522,6 @@
     late_sum.take(0, 0)
     sum_step(0)
     late_sum.take(0, 1)
-    early.take(2, 0)
     sum_step(1)
     late_sum.take(1, 0)
     sum_step(2)
@@ -1564,7 +1569,8 @@
     row_count = span + patch_span
     total_rows = count * row_count
     bundle, weights, keys = far_values[0], far_values[1], far_values[2]
-    pairs, key_pad = weights.shape[1], keys.shape[1]
+    groups, grouped_rows, key_pad = weights.shape[1:]
+    heads = groups * grouped_rows // row_count
     blocks, early_rows, lanes = bundle.shape[1:]
     late_rows = 3 * width // (2 * pages)
     levels = pages.bit_length() - 1
@@ -1598,28 +1604,27 @@
             VMEM((2, blocks, late_rows, lanes), bf16),
             VMEM((blocks, late_rows, lanes), bf16),
             landings(late_rows),
-            VMEM((2, pairs, 2 * row_count, key_pad), bf16),
+            VMEM((2, groups, grouped_rows, key_pad), bf16),
             VMEM((2, key_pad, width), bf16),
             VMEM((2, key_pad, width), bf16),
             VMEM((count, 4, 2, row_count, width), bf16),
             VMEM((count, 2, 2, row_count, width), bf16),
             VMEM((count, 2, row_count, width), bf16),
             VMEM((3, width, width), bf16),
-            VMEM((total_rows, width), bf16),
             VMEM((width, total_rows), bf16),
             VMEM((total_rows, width), f32),
             VMEM((total_rows, width), bf16),
             VMEM((total_rows, width), bf16),
             VMEM((total_rows, width), bf16),
-            VMEM((2 * row_count, key_pad), f32),
-            VMEM((2 * row_count, 3 * key_pad), bf16),
+            VMEM((grouped_rows, key_pad), f32),
+            VMEM((grouped_rows, 3 * key_pad), bf16),
             VMEM((row_count, 2 * key_pad), bf16),
             VMEM((256, 3 * key_pad), bf16),
             VMEM((192, row_count), bf16),
             VMEM((row_count, 128), i32),
-            VMEM((2 * pairs, 192, 128), f32),
-            VMEM((2 * pairs, span + 64 + 2 * patch_span, 128), f32),
-            VMEM((2 * pairs, 8, width), f32),
+            VMEM((heads, 192, 128), f32),
+            VMEM((heads, span + 64 + 2 * patch_span, 128), f32),
+            VMEM((heads, 8, width), f32),
             VMEM((count, span + 32, width), bf16),
             VMEM((count, patch_span + 32, width), bf16),
             VMEM((2, 24, width), f32),
@@ -1671,7 +1676,7 @@
     up = jnp.where(first, block[0 : 2 * rows], up_in_ref[...].astype(f32))
     up_ref[:, 0 : 2 * columns] = up[0:rows]
     up_ref[:, 2 * columns : 4 * columns] = up[rows : 2 * rows]
-    down_ref[...] = jnp.where(first, down_in_ref[...].astype(f32), high[0:wide_rows])
+    down_ref[...] = jnp.where(first, down_in_ref[...].astype(f32), high[0:wide_rows]).T
     kept = jnp.where(first, low[wide_rows:], high[wide_rows:])
     got = mixed_in_ref[0:half, :].astype(f32)
     out_ref[0:half, :] = jnp.where(first, kept, got)
@@ -1707,7 +1712,7 @@
         out_shape=(
             square, square, square, square,
             jax.ShapeDtypeStruct((rows, 4 * columns), f32),
-            jax.ShapeDtypeStruct((4 * rows, columns), f32),
+            jax.ShapeDtypeStruct((columns, 4 * rows), f32),
             taps, taps,
             jax.ShapeDtypeStruct((heads, line_bins), f32), plane, plane,
             jax.ShapeDtypeStruct((16, width), f32),
@@ -1895,6 +1900,7 @@
         places, hidden, mixture_low, cotangent, patch_cotangent,
         (out_weight, up_weight, down_weight), vectors, pages,
     )
+    pair_rows = weights.reshape(page_count, head_count // 2, 2 * row_count, -1)
     if in_tiles(model_width, pages):
         tokens_gradient, patches_gradient, early_state, late_state, sums, up_in, down_in, mixed_in = backward(
             pages,
@@ -1903,7 +1909,7 @@
                 queries, delta_mixture, columns, key_rows, query_rows, tokens, patches, taps, middle_sums,
             ),
             (
-                feedforward_bundle, weights, keys, values, hidden_low, delta_first, query_weight, key_weight,
+                feedforward_bundle, pair_rows, keys, values, hidden_low, delta_first, query_weight, key_weight,
                 value_weight,
             ),
             tokens,
@@ -1926,7 +1932,7 @@
             value_part,
             out_part,
             up_part,
-            down_part,
+            down_part.T,
             text_part.T,
             patch_part.T,
             vector_rows[10],
@@ -1958,7 +1964,7 @@
             keys[page],
             values[page],
             delta_mixture[page],
-            weights[page],
+            pair_rows[page],
         )
         got = swap(delta_blocks[2:], "seq", 1)
         chip_sum = delta_blocks[:2].astype(jnp.float32) + got.astype(jnp.float32)

time: 218 us -> 202 us (0.927)
  Pallas kernels: 204 us -> 190 us
    pallas_call x1, Pallas kernels: 111 us -> 104 us  [backward(): pl.pallas_call(staged(functools.partial(backward_kernel, pages), 1, len(l...]
    pallas_call x1, Pallas kernels: 41 us -> 36.2 us  [middle(): pl.pallas_call(functools.partial(middle_kernel, pages, direct), out_shape...]
    unnamed x8 -> x7, local copies, waits for them, and re-layouts: 4.86 us -> 3 us
where the time goes in v3:
time: 202 us
  Pallas kernels  190 us (94%)
  local copies, waits for them, and re-layouts  6.84 us (3%)
  other arithmetic  4.35 us (2%)
    pallas_call x1, Pallas kernels, backward(): pl.pallas_call(staged(functools.partial(backward_kernel, pages), 1, len(l...  104 us
    pallas_call x1, Pallas kernels, forward(): pl.pallas_call(staged(functools.partial(forward_kernel, pages), 1, 4), ou...  47.4 us
    pallas_call x1, Pallas kernels, middle(): pl.pallas_call(functools.partial(middle_kernel, pages, direct), out_shape...  36.2 us

profile of v3, /device:TPU:0, one launch (start us, length us, event | category | flops | bytes accessed | tf_op | source)
XLA Modules:
  0.0 202.0 jit_solution(8862557972620903824)
XLA Ops:
  0.7 0.7 reshape.105
  1.4 1.5 select_convert_fusion.refs_3_.vector_any
  2.9 1.3 copy.50.refs_1_
  4.2 0.8 maximum_bitcast_fusion
  5.0 0.6 pad_convert_fusion.refs_2_.refs_8_
  5.6 0.1 pad.16.clone
  5.7 1.4 maximum_convert_fusion.refs_4_
  7.1 47.4 %forward.1 = (f32[432,768]{1,0:T(8,128)}, bf16[432,768]{1,0:T(8,128)(2,1)}, bf16[432,768]{1,0:T(8,128)(2,1)}, bf16[432,768]{1,0:T(8,128)(2,1)}, s32[3,144,256]{2...) custom-call(s32[3]{0:T(128)} %refs_0_.3, ...), custom_call_target="tpu_custom_call" | custom-call | flops 8000000000 | bytes 25000000 | tf_op jit(solution)/shard_map/forward/pallas_call | solution.py:494
  54.6 36.2 %middle.1 = (f32[3,128,768]{2,1,0:T(8,128)}, f32[3,16,768]{2,1,0:T(8,128)}, f32[432,768]{1,0:T(8,128)}, bf16[432,768]{1,0:T(8,128)(2,1)}, f32[16,768]{1,0:T(8,128)}, /*index=5*/bf16[2,16,432,384]{3,2,1,0:T(8,128)(2,1)}) custom-call(f32[12,768]{1,0:T(8,128)} %select_convert_fusion.refs_3_.vector_any, f32[432,768]{1,0:T(8,128)} %get-tuple-element.60.rest_0_, ...), custom_call_target="tpu_custom_call" | custom-call | flops 14000000000 | bytes 30000000 | tf_op jit(solution)/shard_map/middle/pallas_call | solution.py:958
  90.8 103.8 %backward.1 = (f32[3,128,768]{2,1,0:T(8,128)}, f32[3,16,768]{2,1,0:T(8,128)}, bf16[432,384]{1,0:T(8,128)(2,1)}, bf16[144,384]{1,0:T(8,128)(2,1)}, f32[2,24,768]{...) custom-call(s32[3]{0:T(128)} %refs_0_.3, ...), custom_call_target="tpu_custom_call" | custom-call | flops 12000000000 | bytes 40000000 | tf_op jit(solution)/shard_map/backward/pallas_call | solution.py:1585
  194.6 0.0 copy-start
  194.6 2.7 %finish.1 = (f32[96,192]{1,0:T(8,128)}, f32[96,192]{1,0:T(8,128)}, f32[96,192]{1,0:T(8,128)}, f32[96,192]{1,0:T(8,128)}, f32[96,768]{1,0:T(8,128)}, /*index=5*/f...) custom-call(bf16[432,384]{1,0:T(8,128)(2,1)} %get-tuple-element.78.r, ...), custom_call_target="tpu_custom_call" | custom-call | tf_op jit(solution)/shard_map/finish/pallas_call | solution.py:1710
  197.2 0.0 copy-start.1
  197.2 1.6 slice_reduce_fusion
  198.9 0.8 slice.30
  199.7 0.6 reshape.107
  200.3 0.0 copy-done
  200.3 1.0 copy.53
  201.3 0.0 copy-done.1
  201.3 0.7 copy.54
  (5 shorter events, 0.0 us)
Async XLA Ops:
  194.6 5.8 %copy-start = (f32[3,128,768]{2,1,0:T(8,128)S(1)}, f32[3,128,768]{2,1,0:T(8,128)}, u32[]{:S(2)}) copy-start(f32[3,128,768]{2,1,0:T(8,128)} %get-tuple-element.138) | copy-start | bytes 3538948
  197.2 4.1 %copy-start.1 = (f32[3,16,768]{2,1,0:T(8,128)S(1)}, f32[3,16,768]{2,1,0:T(8,128)}, u32[]{:S(2)}) copy-start(f32[3,16,768]{2,1,0:T(8,128)} %get-tuple-element.139) | copy-start | bytes 442372

commit v4 on v3

--- a/solution.py
+++ b/solution.py
@@ -184,12 +184,12 @@
 
 def forward_kernel(
     pages,
-    staging, length_ref, box_ref, taps_ref, vector_ref, table_ref, tokens_any, patches_any, query_weight_any, key_weight_any,
-    value_weight_any,
-    hidden_ref, hidden_low_ref, query_ref, mixture_ref, columns_ref, rows_ref, query_rows_ref, key_any, value_any,
-    weights_any,
+    staging, length_ref, box_ref, text_taps_ref, patch_taps_ref, across_table_ref, upward_table_ref, line_table_ref,
+    query_bias_ref, value_bias_ref, tokens_any, patches_any, query_weight_any, key_weight_any, value_weight_any,
+    hidden_ref, hidden_low_ref, query_ref, mixture_ref, columns_ref, rows_ref, query_rows_ref, taps_ref, key_any,
+    value_any, weights_any,
     own, matrices, key_ref, value_ref, weights_ref, arrived, text, grid, low, scores, across_ref, upward_ref,
-    live_ref, line_ref, packed_ref,
+    live_ref, line_ref, packed_ref, table_ref, vector_ref,
     load_sem, store_sem, send_sem, recv_sem,
 ):
     page_at, _, seq, _, _ = places_of(pages)
@@ -252,7 +252,18 @@
 
     for copy in staging:
         copy.wait()
-    steps = jnp.floor(table_ref[...].astype(jnp.float32) * FIXED + 0.5).astype(jnp.int32)
+    table_ref[...] = jnp.zeros_like(table_ref)
+    start = 0
+    for source in (across_table_ref, upward_table_ref, line_table_ref):
+        heads, bins = source.shape
+        table_ref[0:heads, start : start + bins] = source[...].astype(jnp.float32)
+        start += bins
+    steps = jnp.floor(table_ref[...] * FIXED + 0.5).astype(jnp.int32)
+    vector_ref[0:1, :] = query_bias_ref[...].astype(jnp.float32).reshape(1, width)
+    vector_ref[1:2, :] = value_bias_ref[...].astype(jnp.float32).reshape(1, width)
+    taps_ref[...] = jnp.zeros_like(taps_ref)
+    taps_ref[0:9, :] = text_taps_ref[...].astype(jnp.float32)
+    taps_ref[9:18, :] = patch_taps_ref[...].astype(jnp.float32)
     for pair in range(pairs):
         words = (steps[2 * pair : 2 * pair + 1] + 8192) + steps[2 * pair + 1 : 2 * pair + 2] * 65536
         packed_ref[0, pair : pair + 1, :] = words[:, 0:128]
@@ -289,9 +300,7 @@
         query_cell = seq * patch_span + cell
         row_cell = seq * patch_span + lax.broadcasted_iota(jnp.int32, (patch_span, 1), 0)
         for plane in range(2):
-            boxes = box_ref[plane]
-            of_page = lax.broadcasted_iota(jnp.int32, boxes.shape, 0) == page
-            box = jnp.sum(jnp.where(of_page, boxes, 0), axis=0, keepdims=True)
+            box = box_ref[page, plane : plane + 1, :]
             patch = 146 * ((cell % GRID_SIDE) if plane == 0 else (cell // GRID_SIDE)) + 73
             own_patch = 146 * ((query_cell % GRID_SIDE) if plane == 0 else (query_cell // GRID_SIDE)) + 73
             column_patch = 146 * ((row_cell % GRID_SIDE) if plane == 0 else (row_cell // GRID_SIDE)) + 73
@@ -479,30 +488,33 @@
     return [pl.BlockSpec(memory_space=pl.ANY)] * count
 
 
-def forward(pages, lengths, tokens, patches, box, taps, matrices, vectors, table):
+def forward(pages, lengths, tokens, patches, box, taps, tables, biases, matrices):
     count, span, width = tokens.shape
     patch_span = patches.shape[1]
     row_count = span + patch_span
     total_rows = count * row_count
     key_pad = -(-4 * row_count // 128) * 128
-    pairs = table.shape[0] // 2
-    members = 4 if table.shape[0] % 4 == 0 else 2
-    groups = table.shape[0] // members
+    heads = tables[0].shape[0]
+    pairs = heads // 2
+    members = 4 if heads % 4 == 0 else 2
+    groups = heads // members
+    small = (box, *taps, *tables, *biases)
     bf16, f32, i32 = jnp.bfloat16, jnp.float32, jnp.int32
     own = jax.ShapeDtypeStruct((total_rows, width), bf16)
     every = jax.ShapeDtypeStruct((count, key_pad, width), bf16)
     return pl.pallas_call(
-        staged(functools.partial(forward_kernel, pages), 1, 4),
+        staged(functools.partial(forward_kernel, pages), 1, len(small)),
         out_shape=(
             jax.ShapeDtypeStruct((total_rows, width), f32), own, own, own,
             jax.ShapeDtypeStruct((count, row_count, 256), i32),
             jax.ShapeDtypeStruct((count, 8, key_pad), i32),
             jax.ShapeDtypeStruct((count, 8, 256), i32),
+            jax.ShapeDtypeStruct((24, width), f32),
             every, every,
             jax.ShapeDtypeStruct((count, groups, members * row_count, key_pad), bf16),
         ),
-        in_specs=[pl.BlockSpec(memory_space=pltpu.SMEM)] + anywhere(9),
-        out_specs=tuple(in_vmem(7) + anywhere(3)),
+        in_specs=[pl.BlockSpec(memory_space=pltpu.SMEM)] + anywhere(len(small) + 5),
+        out_specs=tuple(in_vmem(8) + anywhere(3)),
         scratch_shapes=[
             VMEM((count, row_count, width), bf16),
             VMEM((3, width, width), bf16),
@@ -519,18 +531,20 @@
             VMEM((8, key_pad), f32),
             VMEM((pairs, row_count, key_pad), i32),
             VMEM((2, 8, 128), i32),
+            VMEM((-(-heads // 8) * 8, 256), f32),
+            VMEM((8, width), f32),
             pltpu.SemaphoreType.DMA((5,)),
             pltpu.SemaphoreType.DMA((3, count)),
             pltpu.SemaphoreType.DMA((5, count)),
             pltpu.SemaphoreType.DMA((5, count)),
         ]
-        + stage_for((box, taps, vectors, table)),
+        + stage_for(small),
         compiler_params=pltpu.CompilerParams(
             collective_id=0, has_side_effects=True, vmem_limit_bytes=KERNEL_VMEM
         ),
         cost_estimate=pl.CostEstimate(flops=8_000_000_000, bytes_accessed=25_000_000, transcendentals=3_000_000),
         name="forward",
-    )(lengths, box, taps, vectors, table, tokens, patches, *matrices)
+    )(lengths, *small, tokens, patches, *matrices)
 
 
 def backward_page_kernel(
@@ -739,21 +753,19 @@
 
 def middle_kernel(
     pages, direct,
-    vector_any, *rest,
+    *rest,
 ):
     scalar_ref = position()
-    arguments, rest = (*rest[:7], vector_any), rest[7:]
+    arguments, rest = rest[:14], rest[14:]
     output_ref, patch_output_ref, first_back_ref, mixture_back_ref, sums_ref, *rest = rest
-    *rest, load_sem, store_sem = rest
-    copied, rest = rest[-8:], rest[:-8]
-    hidden_ref, mixture_ref, cotangent_ref, patch_cotangent_ref, out_weight_ref, up_weight_ref, down_weight_ref, vector_ref = (
-        copied
-    )
+    *rest, vector_ref, load_sem, store_sem = rest
+    copied, rest = rest[-14:], rest[:-14]
+    hidden_ref, mixture_ref, cotangent_ref, patch_cotangent_ref, out_weight_ref, up_weight_ref, down_weight_ref = copied[:7]
     loads = [
         pltpu.make_async_copy(source, target, load_sem.at[index])
         for index, (source, target) in enumerate(zip(arguments, copied, strict=True))
     ]
-    for index in (7, 1, 4, 0, 5, 6, 2, 3):
+    for index in (*range(7, 14), 1, 4, 0, 5, 6, 2, 3):
         loads[index].start()
     if direct:
         bundle_any, *rest, bundle_ref = rest
@@ -776,8 +788,13 @@
         state[:, at] = hidden_ref[:, at] + (dot_nn(mixture_ref[...], out_weight_ref[:, at]) + vector_ref[2:3, at])
         return carry
 
-    for index in (0, 1, 4, 7):
+    for index in (*range(7, 14), 0, 1, 4):
         loads[index].wait()
+    for index, source in enumerate(copied[7:13]):
+        vector_ref[2 + index : 3 + index, :] = source[...].astype(jnp.float32).reshape(1, width)
+    for index in range(wide // width):
+        part = copied[13][pl.ds(index * width, width)]
+        vector_ref[8 + index : 9 + index, :] = part.astype(jnp.float32).reshape(1, width)
     lax.fori_loop(0, width // lanes, attention_tile, 0)
 
     def first_norm(chunk, carry):
@@ -965,7 +982,7 @@
             jax.ShapeDtypeStruct((16, width), f32),
         )
         + extra,
-        in_specs=anywhere(8),
+        in_specs=anywhere(7 + len(vectors)),
         out_specs=tuple(in_vmem(5) + (anywhere(1) if direct else in_vmem(len(extra)))),
         scratch_shapes=[
             pltpu.VMEM((total_rows, width), f32),
@@ -982,13 +999,13 @@
         + [pltpu.VMEM(value.shape, value.dtype) for value in (extra if direct else ())]
         + [
             pltpu.VMEM(value.shape, value.dtype)
-            for value in (hidden, mixture, cotangent, patch_cotangent, *matrices, vectors)
+            for value in (hidden, mixture, cotangent, patch_cotangent, *matrices, *vectors)
         ]
-        + [pltpu.SemaphoreType.DMA((8,)), pltpu.SemaphoreType.DMA((3,))],
+        + [pltpu.VMEM((16, width), f32), pltpu.SemaphoreType.DMA((14,)), pltpu.SemaphoreType.DMA((3,))],
         compiler_params=pltpu.CompilerParams(vmem_limit_bytes=KERNEL_VMEM),
         cost_estimate=pl.CostEstimate(flops=14_000_000_000, bytes_accessed=30_000_000, transcendentals=2_600_000),
         name="middle",
-    )(vectors, hidden, mixture, cotangent, patch_cotangent, *matrices)
+    )(hidden, mixture, cotangent, patch_cotangent, *matrices, *vectors)
     first, rest = result[:5], result[5:]
     if direct:
         return first + rest
@@ -1658,11 +1675,20 @@
     return moved[:, :bins]
 
 
-def finish_kernel(
-    staging, early_ref, late_ref, sums_ref, up_in_ref, down_in_ref, mixed_in_ref,
-    query_ref, key_ref, value_ref, out_ref, up_ref, down_ref, taps_ref, patch_taps_ref, line_ref, across_ref,
-    upward_ref, vector_ref,
-):
+def finish_kernel(staging, early_ref, late_ref, sums_ref, up_in_ref, down_in_ref, mixed_in_ref, *rest):
+    carried, rest = rest[:2], rest[2:]
+    *rest, carry_sem = rest
+    rest, targets = rest[:-2], rest[-2:]
+    (
+        query_ref, key_ref, value_ref, out_ref, up_ref, down_ref, taps_ref, patch_taps_ref, line_ref, across_ref,
+        upward_ref, *vector_refs,
+    ) = rest
+    carries = [
+        pltpu.make_async_copy(source, target, carry_sem.at[index])
+        for index, (source, target) in enumerate(zip(carried, targets, strict=True))
+    ]
+    for copy in carries:
+        copy.start()
     f32 = jnp.float32
     rows, columns = query_ref.shape
     half = rows // 2
@@ -1698,10 +1724,14 @@
     across_ref[...] = clip_lanes(back[8:24, 0:256], 72, across_ref.shape[1])[0:heads]
     upward_ref[...] = clip_lanes(back[8:24, 256:512], 72, upward_ref.shape[1])[0:heads]
     line_ref[...] = clip_lanes(back[8:24, 512:640], 32, line_ref.shape[1])[0:heads]
-    vector_ref[...] = front[0:16]
-
-
-def finish(values, width, heads, line_bins, plane_bins):
+    for source, target in zip((10, 11, 0, UP_BIAS, 1, 2, 3, 4, 5), vector_refs, strict=True):
+        for part in range(target.shape[0] // width):
+            target[pl.ds(part * width, width)] = front[source + part, :]
+    for copy in carries:
+        copy.wait()
+
+
+def finish(values, carried, width, wide, heads, line_bins, plane_bins):
     rows, columns = values[1].shape[0] * 2 // 3, values[1].shape[1] // 2
     f32 = jnp.float32
     square = jax.ShapeDtypeStruct((rows, columns), f32)
@@ -1715,14 +1745,15 @@
             jax.ShapeDtypeStruct((columns, 4 * rows), f32),
             taps, taps,
             jax.ShapeDtypeStruct((heads, line_bins), f32), plane, plane,
-            jax.ShapeDtypeStruct((16, width), f32),
+            *(jax.ShapeDtypeStruct((size,), f32) for size in (width,) * 3 + (wide,) + (width,) * 5),
+            *(jax.ShapeDtypeStruct(value.shape, f32) for value in carried),
         ),
-        in_specs=anywhere(len(values)),
-        out_specs=tuple(in_vmem(12)),
-        scratch_shapes=stage_for(values),
+        in_specs=anywhere(len(values) + len(carried)),
+        out_specs=tuple(in_vmem(22)),
+        scratch_shapes=[pltpu.SemaphoreType.DMA((2,))] + stage_for(values),
         compiler_params=pltpu.CompilerParams(vmem_limit_bytes=KERNEL_VMEM),
         name="finish",
-    )(*values)
+    )(*values, *carried)
 
 
 def exchange(value, pages, step):
@@ -1862,33 +1893,12 @@
     patch_masked = patches * patch_factor.astype(jnp.bfloat16)
     patch_rimmed = with_halo(patch_masked, (("seq", 1),), reach)
     pages = lax.axis_size("page")
-    table = jnp.concatenate(
-        [
-            horizontal_bias_table,
-            vertical_bias_table,
-            reading_bias_table,
-            jnp.zeros((head_count, 256 - 2 * plane_bins - line_bins), jnp.bfloat16),
-        ],
-        axis=1,
-    ).astype(jnp.float32)
-    taps = jnp.pad(
-        jnp.concatenate([conv_weight, patch_conv_weight], axis=1).astype(jnp.float32).T, ((0, 6), (0, 0))
-    )
-    vector_row = jnp.arange(8 + up_bias.shape[0] // model_width, dtype=jnp.int32)[:, None]
-    vectors = jnp.pad(up_bias.reshape(-1, model_width), ((8, 0), (0, 0)))
-    for index, vector in enumerate(
-        (
-            query_bias, value_bias, out_bias, down_bias, attention_gain, attention_shift, feedforward_gain,
-            feedforward_shift,
-        )
-    ):
-        vectors = jnp.where(vector_row == index, vector[None, :], vectors)
-    vectors = vectors.astype(jnp.float32)
     (
-        hidden, hidden_low, queries, mixture_low, columns, key_rows, query_rows, keys, values, weights,
+        hidden, hidden_low, queries, mixture_low, columns, key_rows, query_rows, taps, keys, values, weights,
     ) = forward(
-        pages, page_length, tokens, patches, box_position, taps, (query_weight, key_weight, value_weight),
-        vectors, table,
+        pages, page_length, tokens, patches, box_position.transpose(1, 0, 2), (conv_weight.T, patch_conv_weight.T),
+        (horizontal_bias_table, vertical_bias_table, reading_bias_table), (query_bias, value_bias),
+        (query_weight, key_weight, value_weight),
     )
     places = jnp.stack(
         [seq_index, seq_index % 2, lax.axis_index("page"), seq_index // 2]
@@ -1898,11 +1908,15 @@
 
     output, patch_output, delta_first, delta_mixture, middle_sums, feedforward_bundle = middle(
         places, hidden, mixture_low, cotangent, patch_cotangent,
-        (out_weight, up_weight, down_weight), vectors, pages,
+        (out_weight, up_weight, down_weight),
+        (
+            out_bias, down_bias, attention_gain, attention_shift, feedforward_gain, feedforward_shift, up_bias,
+        ),
+        pages,
     )
     pair_rows = weights.reshape(page_count, head_count // 2, 2 * row_count, -1)
     if in_tiles(model_width, pages):
-        tokens_gradient, patches_gradient, early_state, late_state, sums, up_in, down_in, mixed_in = backward(
+        tokens_back, patches_back, early_state, late_state, sums, up_in, down_in, mixed_in = backward(
             pages,
             page_length,
             (
@@ -1917,9 +1931,10 @@
         )
         (
             query_part, key_part, value_part, out_part, up_part, down_part, text_part, patch_part, line_part,
-            across_part, upward_part, vector_rows,
+            across_part, upward_part, *vector_parts, tokens_gradient, patches_gradient,
         ) = finish(
-            (early_state, late_state, sums, up_in, down_in, mixed_in), model_width, head_count, line_bins,
+            (early_state, late_state, sums, up_in, down_in, mixed_in),
+            (tokens_back, patches_back), model_width, up_weight.shape[1], head_count, line_bins,
             plane_bins,
         )
         return (
@@ -1935,15 +1950,7 @@
             down_part.T,
             text_part.T,
             patch_part.T,
-            vector_rows[10],
-            vector_rows[11],
-            vector_rows[OUT_BIAS],
-            vector_rows[UP_BIAS : UP_BIAS + 4].reshape(-1),
-            vector_rows[DOWN_BIAS],
-            vector_rows[FIRST_GAIN],
-            vector_rows[FIRST_SHIFT],
-            vector_rows[SECOND_GAIN],
-            vector_rows[SECOND_SHIFT],
+            *vector_parts,
             line_part,
             across_part,
             upward_part,

time: 202 us -> 192 us (0.950)
  local copies, waits for them, and re-layouts: 6.84 us -> 0 us
  other arithmetic: 4.35 us -> 0 us
    unnamed x7 -> x0, local copies, waits for them, and re-layouts: 3 us -> none
    convert_element_type x2 -> x0, other arithmetic: 2.92 us -> none  [the longest x1 1.51 us: shards(): vectors = vectors.astype(jnp.float32)]
    slice x2 -> x0, local copies, waits for them, and re-layouts: 2.45 us -> none  [the longest x1 1.65 us: shards(): vector_rows[SECOND_SHIFT]]
where the time goes in v4:
time: 192 us
  Pallas kernels  191 us (99%)
    pallas_call x1, Pallas kernels, backward(): pl.pallas_call(staged(functools.partial(backward_kernel, pages), 1, len(l...  104 us
    pallas_call x1, Pallas kernels, forward(): pl.pallas_call(staged(functools.partial(forward_kernel, pages), 1, len(sm...  47.4 us
    pallas_call x1, Pallas kernels, middle(): pl.pallas_call(functools.partial(middle_kernel, pages, direct), out_shape...  36.3 us

profile of v4, /device:TPU:0, one launch (start us, length us, event | category | flops | bytes accessed | tf_op | source)
XLA Modules:
  0.0 191.9 jit_solution(13711193578264418217)
XLA Ops:
  0.7 47.4 %forward.1 = (f32[432,768]{1,0:T(8,128)}, bf16[432,768]{1,0:T(8,128)(2,1)}, bf16[432,768]{1,0:T(8,128)(2,1)}, bf16[432,768]{1,0:T(8,128)(2,1)}, s32[3,144,256]{2...) custom-call(s32[3]{0:T(128)} %refs_0_.3, ...), custom_call_target="tpu_custom_call" | custom-call | flops 8000000000 | bytes 25000000 | tf_op jit(solution)/shard_map/forward/pallas_call | solution.py:505
  48.1 36.3 %middle.1 = (f32[3,128,768]{2,1,0:T(8,128)}, f32[3,16,768]{2,1,0:T(8,128)}, f32[432,768]{1,0:T(8,128)}, bf16[432,768]{1,0:T(8,128)(2,1)}, f32[16,768]{1,0:T(8,128)}, /*index=5*/bf16[2,16,432,384]{3,2,1,0:T(8,128)(2,1)}) custom-call(f32[432,768]{1,0:T(8,128)} %get-tuple-element.71.rest_0_, bf16[432,768]{1,0:T(8,128)(2,1)} %get-tuple-element.72.rest_1_, ...), custom_call_target="tpu_custom_call" | custom-call | flops 14000000000 | bytes 30000000 | tf_op jit(solution)/shard_map/middle/pallas_call | solution.py:975
  84.4 103.8 %backward.1 = (f32[3,128,768]{2,1,0:T(8,128)}, f32[3,16,768]{2,1,0:T(8,128)}, bf16[432,384]{1,0:T(8,128)(2,1)}, bf16[144,384]{1,0:T(8,128)(2,1)}, f32[2,24,768]{...) custom-call(s32[3]{0:T(128)} %refs_0_.3, ...), custom_call_target="tpu_custom_call" | custom-call | flops 12000000000 | bytes 40000000 | tf_op jit(solution)/shard_map/backward/pallas_call | solution.py:1602
  188.1 3.6 %finish.1 = (f32[96,192]{1,0:T(8,128)}, f32[96,192]{1,0:T(8,128)}, f32[96,192]{1,0:T(8,128)}, f32[96,192]{1,0:T(8,128)}, f32[96,768]{1,0:T(8,128)}, /*index=5*/f...) custom-call(bf16[432,384]{1,0:T(8,128)(2,1)} %get-tuple-element.88.r, ...), custom_call_target="tpu_custom_call" | custom-call | tf_op jit(solution)/shard_map/finish/pallas_call | solution.py:1740

commit v5 on v4

--- a/solution.py
+++ b/solution.py
@@ -147,6 +147,7 @@
 
 
 CHUNK = 16
+FORWARD_CHUNK = 48
 
 
 MESH = pl.DeviceIdType.MESH
@@ -400,10 +401,10 @@
         def attend(group, carry):
             at = pl.ds(pl.multiple_of(group * group_width, group_width), group_width)
             scores[...] = dot_nt(split_heads(query_ref[own_rows, at] * jnp.bfloat16(FIXED)), key_ref[page, :, at])
-            for start, sub in ((start, sub) for start in range(0, row_count, CHUNK) for sub in range(members // 2)):
+            for start, sub in ((start, sub) for start in range(0, row_count, FORWARD_CHUNK) for sub in range(members // 2)):
                 pair = group * (members // 2) + sub
                 plane_row = packed_ref[0, pl.ds(pair, 1), :]
-                here = slice(start, start + CHUNK)
+                here = slice(start, start + FORWARD_CHUNK)
                 packed = []
                 for block_at in range(0, key_pad, 128):
                     lane = slice(block_at, block_at + 128)
@@ -414,7 +415,7 @@
                     )
                 for side in range(2):
                     first = (2 * sub + side) * row_count + start
-                    there = slice(first, first + CHUNK)
+                    there = slice(first, first + FORWARD_CHUNK)
                     parts, top = [], None
                     for index, word in enumerate(packed):
                         lane = slice(128 * index, 128 * (index + 1))
@@ -1300,17 +1301,26 @@
             (span, patch_span, 4, span + 64 + patch_span),
         )
 
-    def sib_copy(page):
-        return remote(outgoing.at[page, 2:4], from_sib.at[page], sib_send.at[page], sib_recv.at[page], *sibling)
-
-    def far_copy(page):
-        return remote(outgoing.at[page, 1], from_far.at[page], far_send.at[page], far_recv.at[page], *opposite)
-
-    def pass_on(page):
-        sib_copy(page).wait_recv()
+    def sib_copy(page, part):
+        at = slice(part * width // 2, (part + 1) * width // 2)
+        return remote(
+            outgoing.at[page, 2:4, :, :, at], from_sib.at[page, :, :, :, at], sib_send.at[page, part],
+            sib_recv.at[page, part], *sibling,
+        )
+
+    def far_copy(page, part):
+        at = slice(part * width // 2, (part + 1) * width // 2)
+        return remote(
+            outgoing.at[page, 1, :, :, at], from_far.at[page, :, :, at], far_send.at[page, part],
+            far_recv.at[page, part], *opposite,
+        )
+
+    def pass_on(page, part):
+        sib_copy(page, part).wait_recv()
+        at = slice(part * width // 2, (part + 1) * width // 2)
         for kind in range(2):
-            outgoing[page, 1, kind] = outgoing[page, 1, kind] + from_sib[page, 1, kind]
-        far_copy(page).start()
+            outgoing[page, 1, kind, :, at] = outgoing[page, 1, kind, :, at] + from_sib[page, 1, kind, :, at]
+        far_copy(page, part).start()
 
     events = {
         1: [("core", 0), ("core", 1)], 2: [("core", 2), ("core", 3)], 4: [("core", 4), ("core", 5)],
@@ -1339,15 +1349,21 @@
             for copy in later_loads:
                 copy.start()
 
-        @pl.when((group == 1) & (page > 0))
+        @pl.when((group == 2) & (page > 0))
         def _():
-            pass_on(page - 1)
-
-        attend(page, group)
+            pass_on(page - 1, 1)
 
         @pl.when(group == groups - 1)
         def _():
-            sib_copy(page).start()
+            pass_on(page, 0)
+
+        attend(page, group)
+
+        for part in range(2):
+
+            @pl.when(group == (part + 1) * groups // 2 - 1)
+            def _(part=part):
+                sib_copy(page, part).start()
 
         return carry
 
@@ -1385,7 +1401,7 @@
     def project_back(gradient, matrix):
         total_back[...] = total_back[...] + dot_nt(gradient[...], matrices[matrix])
 
-    pass_on(count - 1)
+    pass_on(count - 1, 1)
     weight_columns(0, query_back)
     project_back(query_back, 0)
     sums[0, 0:16, :] = middle_sums_ref[...]
@@ -1428,7 +1444,8 @@
     for name in ((0, 2), (1, 0)):
         early.take(*name)
     for page in range(count):
-        far_copy(page).wait_recv()
+        for part in range(2):
+            far_copy(page, part).wait_recv()
         own_rows = slice(page * row_count, (page + 1) * row_count)
         for kind, target in enumerate((key_back, value_back)):
             target[own_rows, :] = (
@@ -1576,8 +1593,9 @@
     early.finish()
     late_sum.finish()
     for page in range(count):
-        sib_copy(page).wait_send()
-        far_copy(page).wait_send()
+        for part in range(2):
+            sib_copy(page, part).wait_send()
+            far_copy(page, part).wait_send()
 
 
 def backward(pages, lengths, local_values, far_values, tokens, patches):
@@ -1653,7 +1671,7 @@
             VMEM((early_rows // 9 + late_rows, lanes // 2), bf16),
             dma((6,)), dma((3, 2)),
             dma((early_count,)), dma((early_count,)), dma((late_count,)), dma((late_count,)),
-            dma((count,)), dma((count,)), dma((count,)), dma((count,)),
+            dma((count, 2)), dma((count, 2)), dma((count, 2)), dma((count, 2)),
             dma((4,)), dma((4,)), dma((3 + levels,)), dma((3 + levels,)), dma((3,)), dma((3,)),
         ]
         + stage_for(local_values),

time: 192 us -> 187 us (0.974)
  Pallas kernels: 191 us -> 186 us
    pallas_call x1, Pallas kernels: 104 us -> 100 us  [backward(): pl.pallas_call(staged(functools.partial(backward_kernel, pages), 1, len(l...]
where the time goes in v5:
time: 187 us
  Pallas kernels  186 us (99%)
    pallas_call x1, Pallas kernels, backward(): pl.pallas_call(staged(functools.partial(backward_kernel, pages), 1, len(l...  100 us
    pallas_call x1, Pallas kernels, forward(): pl.pallas_call(staged(functools.partial(forward_kernel, pages), 1, len(sm...  46.2 us
    pallas_call x1, Pallas kernels, middle(): pl.pallas_call(functools.partial(middle_kernel, pages, direct), out_shape...  36.3 us

profile of v5, /device:TPU:0, one launch (start us, length us, event | category | flops | bytes accessed | tf_op | source)
XLA Modules:
  0.0 187.0 jit_solution(15137614849017779347)
XLA Ops:
  0.7 46.2 %forward.1 = (f32[432,768]{1,0:T(8,128)}, bf16[432,768]{1,0:T(8,128)(2,1)}, bf16[432,768]{1,0:T(8,128)(2,1)}, bf16[432,768]{1,0:T(8,128)(2,1)}, s32[3,144,256]{2...) custom-call(s32[3]{0:T(128)} %refs_0_.3, ...), custom_call_target="tpu_custom_call" | custom-call | flops 8000000000 | bytes 25000000 | tf_op jit(solution)/shard_map/forward/pallas_call | solution.py:506
  46.9 36.3 %middle.1 = (f32[3,128,768]{2,1,0:T(8,128)}, f32[3,16,768]{2,1,0:T(8,128)}, f32[432,768]{1,0:T(8,128)}, bf16[432,768]{1,0:T(8,128)(2,1)}, f32[16,768]{1,0:T(8,128)}, /*index=5*/bf16[2,16,432,384]{3,2,1,0:T(8,128)(2,1)}) custom-call(f32[432,768]{1,0:T(8,128)} %get-tuple-element.71.rest_0_, bf16[432,768]{1,0:T(8,128)(2,1)} %get-tuple-element.72.rest_1_, ...), custom_call_target="tpu_custom_call" | custom-call | flops 14000000000 | bytes 30000000 | tf_op jit(solution)/shard_map/middle/pallas_call | solution.py:976
  83.2 100.1 %backward.1 = (f32[3,128,768]{2,1,0:T(8,128)}, f32[3,16,768]{2,1,0:T(8,128)}, bf16[432,384]{1,0:T(8,128)(2,1)}, bf16[144,384]{1,0:T(8,128)(2,1)}, f32[2,24,768]{...) custom-call(s32[3]{0:T(128)} %refs_0_.3, ...), custom_call_target="tpu_custom_call" | custom-call | flops 12000000000 | bytes 40000000 | tf_op jit(solution)/shard_map/backward/pallas_call | solution.py:1620
  183.3 3.6 %finish.1 = (f32[96,192]{1,0:T(8,128)}, f32[96,192]{1,0:T(8,128)}, f32[96,192]{1,0:T(8,128)}, f32[96,192]{1,0:T(8,128)}, f32[96,768]{1,0:T(8,128)}, /*index=5*/f...) custom-call(bf16[432,384]{1,0:T(8,128)(2,1)} %get-tuple-element.88.r, ...), custom_call_target="tpu_custom_call" | custom-call | tf_op jit(solution)/shard_map/finish/pallas_call | solution.py:1758

commit v6 on v5

--- a/solution.py
+++ b/solution.py
@@ -146,7 +146,7 @@
     return lax.dot_general(left, right, (((0,), (0,)), ((), ())), preferred_element_type=jnp.float32)
 
 
-CHUNK = 16
+CHUNK = 48
 FORWARD_CHUNK = 48
 
 
@@ -929,15 +929,18 @@
     ]
     stores[0].start()
 
-    def down_weight_tile(page, carry):
-        at = pl.ds(pl.multiple_of(page * tall, 128), tall)
+    def down_weight_tile(four, carry):
+        at = pl.ds(pl.multiple_of(four * 4 * tall, 128), 4 * tall)
         result = dot_tn(activated[:, at], down_back[...]).astype(jnp.bfloat16)
-        for column in range(2):
-            slot = early_slots(scalar_ref, page, column, levels)[1]
-            bundle_ref[1 - core, slot, 0:tall, :] = result[:, column * block : (column + 1) * block]
+        for inner in range(4):
+            for column in range(2):
+                slot = early_slots(scalar_ref, 4 * four + inner, column, levels)[1]
+                bundle_ref[1 - core, slot, 0:tall, :] = result[
+                    inner * tall : (inner + 1) * tall, column * block : (column + 1) * block
+                ]
         return carry
 
-    lax.fori_loop(0, pages, down_weight_tile, 0)
+    lax.fori_loop(0, pages // 4, down_weight_tile, 0)
     stores[1].start()
     flipped[...] = mixture_ref[...].T
     half = rows // 2

time: 187 us -> 186 us (level)
  no operation moved by 1% of the time
where the time goes in v6:
time: 186 us
  Pallas kernels  185 us (99%)
    pallas_call x1, Pallas kernels, backward(): pl.pallas_call(staged(functools.partial(backward_kernel, pages), 1, len(l...  100 us
    pallas_call x1, Pallas kernels, forward(): pl.pallas_call(staged(functools.partial(forward_kernel, pages), 1, len(sm...  46.2 us
    pallas_call x1, Pallas kernels, middle(): pl.pallas_call(functools.partial(middle_kernel, pages, direct), out_shape...  35.1 us

profile of v6, /device:TPU:0, one launch (start us, length us, event | category | flops | bytes accessed | tf_op | source)
XLA Modules:
  0.0 185.9 jit_solution(11896580586794450737)
XLA Ops:
  0.7 46.2 %forward.1 = (f32[432,768]{1,0:T(8,128)}, bf16[432,768]{1,0:T(8,128)(2,1)}, bf16[432,768]{1,0:T(8,128)(2,1)}, bf16[432,768]{1,0:T(8,128)(2,1)}, s32[3,144,256]{2...) custom-call(s32[3]{0:T(128)} %refs_0_.3, ...), custom_call_target="tpu_custom_call" | custom-call | flops 8000000000 | bytes 25000000 | tf_op jit(solution)/shard_map/forward/pallas_call | solution.py:506
  46.9 35.1 %middle.1 = (f32[3,128,768]{2,1,0:T(8,128)}, f32[3,16,768]{2,1,0:T(8,128)}, f32[432,768]{1,0:T(8,128)}, bf16[432,768]{1,0:T(8,128)(2,1)}, f32[16,768]{1,0:T(8,128)}, /*index=5*/bf16[2,16,432,384]{3,2,1,0:T(8,128)(2,1)}) custom-call(f32[432,768]{1,0:T(8,128)} %get-tuple-element.71.rest_0_, bf16[432,768]{1,0:T(8,128)(2,1)} %get-tuple-element.72.rest_1_, ...), custom_call_target="tpu_custom_call" | custom-call | flops 14000000000 | bytes 30000000 | tf_op jit(solution)/shard_map/middle/pallas_call | solution.py:979
  82.0 100.1 %backward.1 = (f32[3,128,768]{2,1,0:T(8,128)}, f32[3,16,768]{2,1,0:T(8,128)}, bf16[432,384]{1,0:T(8,128)(2,1)}, bf16[144,384]{1,0:T(8,128)(2,1)}, f32[2,24,768]{...) custom-call(s32[3]{0:T(128)} %refs_0_.3, ...), custom_call_target="tpu_custom_call" | custom-call | flops 12000000000 | bytes 40000000 | tf_op jit(solution)/shard_map/backward/pallas_call | solution.py:1623
  182.1 3.6 %finish.1 = (f32[96,192]{1,0:T(8,128)}, f32[96,192]{1,0:T(8,128)}, f32[96,192]{1,0:T(8,128)}, f32[96,192]{1,0:T(8,128)}, f32[96,768]{1,0:T(8,128)}, /*index=5*/f...) custom-call(bf16[432,384]{1,0:T(8,128)(2,1)} %get-tuple-element.88.r, ...), custom_call_target="tpu_custom_call" | custom-call | tf_op jit(solution)/shard_map/finish/pallas_call | solution.py:1761

commit v7 on v6

--- a/solution.py
+++ b/solution.py
@@ -854,13 +854,16 @@
     lax.fori_loop(0, count, second_page, 0)
 
     def up_back_tile(tile, carry):
-        at = tile_at(tile)
+        at = pl.ds(pl.multiple_of(tile * 2 * width, 2 * width), 2 * width)
         low = (dot_nt(down_back[...], down_weight_ref[at, :]) * slope[:, at]).astype(jnp.bfloat16)
         up_back[:, at] = low
-        sums_ref[pl.ds(UP_BIAS + tile, 1), :] = column_sum(low.astype(jnp.float32))
+        for part in range(2):
+            sums_ref[pl.ds(UP_BIAS + 2 * tile + part, 1), :] = column_sum(
+                low[:, part * width : (part + 1) * width].astype(jnp.float32)
+            )
         return carry
 
-    lax.fori_loop(0, wide // lanes, up_back_tile, 0)
+    lax.fori_loop(0, wide // (2 * width), up_back_tile, 0)
 
     def normed_back_tile(tile, carry):
         at = tile_at(tile)

time: 186 us -> 185 us (level)
  no operation moved by 1% of the time
where the time goes in v7:
time: 185 us
  Pallas kernels  184 us (99%)
    pallas_call x1, Pallas kernels, backward(): pl.pallas_call(staged(functools.partial(backward_kernel, pages), 1, len(l...  100 us
    pallas_call x1, Pallas kernels, forward(): pl.pallas_call(staged(functools.partial(forward_kernel, pages), 1, len(sm...  46.2 us
    pallas_call x1, Pallas kernels, middle(): pl.pallas_call(functools.partial(middle_kernel, pages, direct), out_shape...  34.5 us

profile of v7, /device:TPU:0, one launch (start us, length us, event | category | flops | bytes accessed | tf_op | source)
XLA Modules:
  0.0 185.2 jit_solution(8865946952095478431)
XLA Ops:
  0.7 46.2 %forward.1 = (f32[432,768]{1,0:T(8,128)}, bf16[432,768]{1,0:T(8,128)(2,1)}, bf16[432,768]{1,0:T(8,128)(2,1)}, bf16[432,768]{1,0:T(8,128)(2,1)}, s32[3,144,256]{2...) custom-call(s32[3]{0:T(128)} %refs_0_.3, ...), custom_call_target="tpu_custom_call" | custom-call | flops 8000000000 | bytes 25000000 | tf_op jit(solution)/shard_map/forward/pallas_call | solution.py:506
  46.9 34.5 %middle.1 = (f32[3,128,768]{2,1,0:T(8,128)}, f32[3,16,768]{2,1,0:T(8,128)}, f32[432,768]{1,0:T(8,128)}, bf16[432,768]{1,0:T(8,128)(2,1)}, f32[16,768]{1,0:T(8,128)}, /*index=5*/bf16[2,16,432,384]{3,2,1,0:T(8,128)(2,1)}) custom-call(f32[432,768]{1,0:T(8,128)} %get-tuple-element.71.rest_0_, bf16[432,768]{1,0:T(8,128)(2,1)} %get-tuple-element.72.rest_1_, ...), custom_call_target="tpu_custom_call" | custom-call | flops 14000000000 | bytes 30000000 | tf_op jit(solution)/shard_map/middle/pallas_call | solution.py:982
  81.4 100.1 %backward.1 = (f32[3,128,768]{2,1,0:T(8,128)}, f32[3,16,768]{2,1,0:T(8,128)}, bf16[432,384]{1,0:T(8,128)(2,1)}, bf16[144,384]{1,0:T(8,128)(2,1)}, f32[2,24,768]{...) custom-call(s32[3]{0:T(128)} %refs_0_.3, ...), custom_call_target="tpu_custom_call" | custom-call | flops 12000000000 | bytes 40000000 | tf_op jit(solution)/shard_map/backward/pallas_call | solution.py:1626
  181.5 3.6 %finish.1 = (f32[96,192]{1,0:T(8,128)}, f32[96,192]{1,0:T(8,128)}, f32[96,192]{1,0:T(8,128)}, f32[96,192]{1,0:T(8,128)}, f32[96,768]{1,0:T(8,128)}, /*index=5*/f...) custom-call(bf16[432,384]{1,0:T(8,128)(2,1)} %get-tuple-element.88.r, ...), custom_call_target="tpu_custom_call" | custom-call | tf_op jit(solution)/shard_map/finish/pallas_call | solution.py:1764
